TPU v7x, 128 devices: a whole 4x4x4 slice. The times are simulated.
128 devices in a mesh: band: 4 (over x), lon: 32 (over y, z, core).
Axes of the slice: x: 4, y: 4, z: 4, core: 2. Of those that a mesh axis runs over, the one named last changes fastest.
Arguments:
- members: bfloat16 [6144, 48, 256], P(('band', 'lon')), may hold values from -6 to 6
- obs_perts: bfloat16 [6144, 32, 256], P(('band', 'lon')), may hold values from -6 to 6
- innovations: bfloat16 [6144, 32], P(('band', 'lon')), may hold values from -12 to 12
- lists: int32 [1024, 64], P(('band', 'lon')), may hold values from 0 to 6143, as said below
- placement: int32 [6144], replicated, may hold values from 0 to 6143, as said below
- obs_taper: float32 [1024, 64, 32], P(('band', 'lon')), may hold values from 0.01 to 0.2
- state_taper: float32 [1024, 64], P(('band', 'lon')), may hold values from 0.2 to 1
Outputs:
- analysis: bfloat16 [6144, 48, 256], P(('band', 'lon'))
Inputs may be any that keep to these rules, and one draw needn't show every extreme that they name: `lists`: number the groups of 8 consecutive regions like the devices (band index times the lon count plus lon index) and call row // 48 a row's device. A group's entries name only blocks on the devices at band offset -1, 0 or 1 and lon offset -1, 0 or 1 (lon taken cyclically) from the group's own; from each such device that exists they name exactly 16 distinct blocks; every region names all 16 blocks of its own device; the 64 entries of one region are distinct. `placement`: A permutation of the block ids.
All inputs are finite; a program needn't handle non-finite values. Where the computation divides by a largest or mean magnitude, that divisor is 1e-20 or more.
Results may differ from a plain program's by a relative error of at most 0.0055.
Values may be sent and summed in bfloat16 or wider, within the bound.
No kernel may reach another device: no remote copies, remote signals or barrier semaphores. Data moves between devices by JAX's collectives and lax.ppermute only.
A program may use at most 128 MiB of HBM per device.

v0:
```python
import jax
import jax.numpy as jnp
from jax import lax
from jax.sharding import PartitionSpec as P

NS_ITERS = 5
CAP = 16


def from_behind(block, axis, distance):
    devices = range(lax.axis_size(axis))
    route = [(i - distance, i) for i in devices if i - distance in devices]
    return lax.ppermute(block, axis, route)


def shifted(block, axis, distance):
    devices = range(lax.axis_size(axis))
    route = [((i - distance) % len(devices), i) for i in devices]
    return lax.ppermute(block, axis, route)


def inverse_root(matrix, identity):
    current = matrix
    estimate = identity
    for iteration in range(NS_ITERS):
        factor = 1.5 * identity - 0.5 * jnp.dot(estimate, current, precision=lax.Precision.HIGHEST)
        current = jnp.dot(current, factor, precision=lax.Precision.HIGHEST)
        estimate = jnp.dot(factor, estimate, precision=lax.Precision.HIGHEST)
    return estimate


def region_mix(obs_float, innov_float, slot_weights, ensemble):
    identity = jnp.eye(ensemble, dtype=jnp.float32)
    gram_matrix = jnp.einsum(
        "jpk,jpl->kl",
        obs_float * slot_weights[:, :, None],
        obs_float,
        precision=lax.Precision.HIGHEST,
    )
    projection = jnp.einsum(
        "jp,jpk->k", slot_weights * innov_float, obs_float, precision=lax.Precision.HIGHEST
    )
    system = (ensemble - 1.0) * identity + gram_matrix
    scale_top = jnp.max(jnp.sum(jnp.abs(system), axis=1))
    inverse_sqrt = inverse_root(system / scale_top, identity) / jnp.sqrt(scale_top)
    halfway = jnp.dot(inverse_sqrt, projection, precision=lax.Precision.HIGHEST)
    mean_weights = jnp.dot(inverse_sqrt, halfway, precision=lax.Precision.HIGHEST)
    mixing = jnp.sqrt(ensemble - 1.0) * inverse_sqrt - identity + mean_weights[:, None]
    return mixing.astype(jnp.bfloat16)


def spread(layered, mover, direction, axis_pos):
    portions = []
    for ordinal in range(3):
        offset = direction * (ordinal - 1)
        if axis_pos == 0:
            portion = layered[ordinal]
        else:
            portion = layered[:, ordinal]
        portions.append(portion if offset == 0 else mover(portion, offset))
    return jnp.stack(portions, axis=axis_pos)


def route(layered, band_mover, lon_mover, direction):
    return spread(spread(layered, band_mover, direction, 0), lon_mover, direction, 1)


def asking_band(portion, offset):
    return from_behind(portion, "band", offset)


def asking_lon(portion, offset):
    return shifted(portion, "lon", offset)


def fetching_band(portion, offset):
    return from_behind(portion, "band", offset)


def fetching_lon(portion, offset):
    return shifted(portion, "lon", offset)


def returning_band(portion, offset):
    return from_behind(portion, "band", offset)


def returning_lon(portion, offset):
    return shifted(portion, "lon", offset)


def pick_rows(selector, source):
    flat = source.reshape(source.shape[0], -1)
    picked = jnp.dot(selector, flat, preferred_element_type=jnp.float32)
    return picked.astype(jnp.bfloat16).reshape((selector.shape[0],) + source.shape[1:])


def local(members, obs_perts, innovations, lists, placement, obs_taper, state_taper):
    lon_count = lax.axis_size("lon")
    band_here = lax.axis_index("band")
    lon_here = lax.axis_index("lon")
    block_count, state_rows, ensemble = members.shape
    obs_rows = obs_perts.shape[1]
    region_count, list_len = lists.shape
    entries = region_count * list_len
    pool_size = 9 * CAP
    row_ids = jnp.take(placement, lists.reshape(-1), axis=0)
    holder = row_ids // block_count
    band_step = holder // lon_count - band_here
    lon_step = (holder % lon_count - lon_here + 1) % lon_count - 1
    neighbour = (band_step + 1) * 3 + lon_step + 1
    inside_row = row_ids % block_count
    positions = jnp.arange(entries, dtype=jnp.int32)
    matching = row_ids[:, None] == row_ids[None, :]
    leading = jnp.logical_not(jnp.any(matching & (positions[None, :] < positions[:, None]), axis=1))
    class_hot = (
        (neighbour[:, None] == jnp.arange(9, dtype=jnp.int32)[None, :]) & leading[:, None]
    ).astype(jnp.int32)
    ordinal_in = jnp.sum((jnp.cumsum(class_hot, axis=0) - class_hot) * class_hot, axis=1)
    lead_slot = neighbour * CAP + ordinal_in
    slot_of = jnp.max(jnp.where(matching & leading[None, :], lead_slot[None, :], 0), axis=1)
    pool_ids = jnp.arange(pool_size, dtype=jnp.int32)
    entry_hot = slot_of[:, None] == pool_ids[None, :]
    wanted = jnp.sum(jnp.where(entry_hot, (inside_row + 1)[:, None], 0), axis=0)
    requested = jnp.max(
        jnp.where(entry_hot & leading[:, None], (inside_row + 1)[:, None], 0), axis=0
    )
    requested = jnp.minimum(requested, wanted)
    received = route(requested.reshape(3, 3, CAP), asking_band, asking_lon, 1)
    received_flat = received.reshape(-1)
    chosen = jnp.maximum(received_flat - 1, 0)
    block_ids = jnp.arange(block_count, dtype=jnp.int32)
    selector = (chosen[:, None] == block_ids[None, :]).astype(jnp.bfloat16)
    padded_innov = jnp.pad(innovations[:, None, :], ((0, 0), (0, 0), (0, ensemble - obs_rows)))
    payload = jnp.concatenate([members, obs_perts, padded_innov], axis=1)
    carried = state_rows + obs_rows + 1
    outgoing = pick_rows(selector, payload).reshape(3, 3, CAP, carried, ensemble)
    arrived = route(outgoing, fetching_band, fetching_lon, -1).reshape(pool_size, carried, ensemble)
    state_pool = arrived[:, :state_rows]
    obs_pool = arrived[:, state_rows : state_rows + obs_rows]
    innov_pool = arrived[:, state_rows + obs_rows, :obs_rows]
    obs_float = obs_pool.astype(jnp.float32)
    innov_float = innov_pool.astype(jnp.float32)
    slot_hot = entry_hot.astype(jnp.float32).reshape(region_count, list_len, pool_size)

    def one_region(region, increment):
        region_hot = lax.dynamic_index_in_dim(slot_hot, region, 0, keepdims=False)
        weights = lax.dynamic_index_in_dim(obs_taper, region, 0, keepdims=False)
        tapers = lax.dynamic_index_in_dim(state_taper, region, 0, keepdims=False)
        slot_weights = jnp.dot(region_hot.T, weights, precision=lax.Precision.HIGHEST)
        slot_tapers = jnp.dot(tapers, region_hot, precision=lax.Precision.HIGHEST)
        mixing = region_mix(obs_float, innov_float, slot_weights, ensemble)
        portion = jnp.einsum("qsk,kl->qsl", state_pool, mixing, preferred_element_type=jnp.float32)
        portion = lax.optimization_barrier(
            (portion * slot_tapers[:, None, None]).astype(jnp.bfloat16)
        )
        return increment + portion.astype(jnp.float32)

    increment = lax.fori_loop(
        0, region_count, one_region, jnp.zeros((pool_size, state_rows, ensemble), jnp.float32)
    )
    outgoing_sum = increment.astype(jnp.bfloat16).reshape(3, 3, CAP, state_rows, ensemble)
    returned = route(outgoing_sum, returning_band, returning_lon, 1).reshape(
        pool_size, state_rows * ensemble
    )
    target_hot = (
        jnp.arange(1, block_count + 1, dtype=jnp.int32)[:, None] == received_flat[None, :]
    ).astype(jnp.bfloat16)
    summed = jnp.dot(target_hot, returned, preferred_element_type=jnp.float32)
    summed = summed.reshape(block_count, state_rows, ensemble)
    return (members.astype(jnp.float32) + summed).astype(jnp.bfloat16)


def solution(mesh):
    in_specs = (
        P(("band", "lon"), None, None),
        P(("band", "lon"), None, None),
        P(("band", "lon"), None),
        P(("band", "lon"), None),
        P(),
        P(("band", "lon"), None, None),
        P(("band", "lon"), None),
    )
    out_specs = P(("band", "lon"), None, None)
    return jax.shard_map(local, mesh=mesh, in_specs=in_specs, out_specs=out_specs, check_vma=False)
```

profile of v0, /device:TPU:4, one launch (start us, length us, event | category | flops | bytes accessed | tf_op | source)
XLA Modules:
  0.0 519.0 jit_solution(14336054758719027997)
XLA Ops:
  2.4 3.1 gather_fusion
  10.8 3.4 collective-permute-start.1
  17.4 5.4 %collective-permute-start.2 = (s32[3,16]{1,0:T(4,128)S(1)}, s32[3,16]{1,0:T(4,128)S(1)}, u32[]{:S(2)}, u32[]{:S(2)}) collective-permute-start(s32[3,16]{1,0:T(4,128)S(1)} %bitcast.255), channel_id=1, source_target_pairs={{1,0},{2,1},{3,2},{4,3},{5,4},{6,5},{7,6},{8,7},{9,8},{10,9},{11,1... | collective-permute-start | bytes 584 | tf_op jit(solution)/shard_map/ppermute | solution.py:19
  24.2 5.0 collective-permute-done.3
  29.3 3.3 convolution_convert_fusion
  46.7 4.7 collective-permute-start.4
  54.2 27.8 %collective-permute-done.5 = bf16[3,16,81,256]{3,1,2,0:T(8,128)(2,1)} collective-permute-done((bf16[3,16,81,256]{3,1,2,0:T(8,128)(2,1)}, bf16[3,16,81,256]{3,1,2,0:T(8,128)(2,1)}, u32[]{:S(2)}, u32[]{:S(2)}) %collective-permute-start.5) | collective-permute-done | bytes 1990688 | tf_op jit(solution)/shard_map/ppermute | solution.py:13
  84.3 4.7 collective-permute-done.4
  94.3 4.0 collective-permute-start.7
  100.1 15.4 %collective-permute-start.6 = (bf16[3,16,81,256]{3,1,2,0:T(8,128)(2,1)}, bf16[3,16,81,256]{3,1,2,0:T(8,128)(2,1)}, u32[]{:S(2)}, u32[]{:S(2)}) collective-permute-start(bf16[3,16,81,256]{3,1,2,0:T(8,128)(2,1)} %copy.143), channel_id=1, source_target_pairs={{31,0},{0,1},{1,2},{2,3},{3,4},{4,5},{5,6},{6,7},{7,8},{8,9},{9,10... | collective-permute-start | bytes 5971976 | tf_op jit(solution)/shard_map/ppermute | solution.py:19
  115.7 5.4 %collective-permute-done.7 = bf16[3,16,81,256]{3,1,2,0:T(8,128)(2,1)} collective-permute-done((bf16[3,16,81,256]{3,1,2,0:T(8,128)(2,1)}, bf16[3,16,81,256]{3,1,2,0:T(8,128)(2,1)}, u32[]{:S(2)}, u32[]{:S(2)}) %collective-permute-start.7) | collective-permute-done | bytes 1990688 | tf_op jit(solution)/shard_map/ppermute | solution.py:19
  123.4 20.0 %collective-permute-done.6 = bf16[3,16,81,256]{3,1,2,0:T(8,128)(2,1)} collective-permute-done((bf16[3,16,81,256]{3,1,2,0:T(8,128)(2,1)}, bf16[3,16,81,256]{3,1,2,0:T(8,128)(2,1)}, u32[]{:S(2)}, u32[]{:S(2)}) %collective-permute-start.6) | collective-permute-done | bytes 1990688 | tf_op jit(solution)/shard_map/ppermute | solution.py:19
  152.7 309.5 %while.14 = (s32[]{:T(128)}, f32[144,48,256]{2,0,1:T(8,128)}, f32[8,64,144]{2,1,0:T(8,128)S(1)}, f32[8,64,32]{1,2,0:T(8,128)}, f32[144,32,256]{2,0,1:T(8,128)}, ...) while((s32[]{:T(128)}, f32[144,48,256]{2,0,1:T(8,128)}, ...), condition=%wide.region_10.11_spmd.clone, body=%wide.region_7.10_spmd.clone.sunk | while | flops 7380189696 | bytes 60170028 | solution.py:159
  153.6 12.0 %abs_reduce_fusion.2 = (f32[256]{0:T(256)S(1)}, f32[256,256]{0,1:T(8,128)S(1)}) fusion(f32[144,32,256]{2,0,1:T(8,128)} %get-tuple-element.301, f32[144,32]{0,1:T(8,128)S(1)} %fusion.215), kind=kOutput, calls=%fused_computation.23.clone.1 | convolution fusion | flops 3625385728 | bytes 5000192 | tf_op jit(solution)/shard_map/while/body/eval_jaxpr/jpk,jpl->kl/dot_general | solution.py:34
  175.4 4.1 convolution_bitcast_fusion.4
  183.7 5.9 %select_add_fusion.2 = f32[144,48,256]{2,0,1:T(8,128)} fusion(f32[144,48,256]{2,0,1:T(8,128)} %get-tuple-element.287, bf16[144,48,256]{2,0,1:T(8,128)(2,1)} %fusion.230, pred[]{:T(512)S(6)} %compare.41), kind=kLoop, calls=%fused_computation.1.clone.1 | loop fusion | flops 5308416 | bytes 17694720 | tf_op jit(solution)/shard_map/while/body/eval_jaxpr/add | solution.py:157
  190.6 12.0 %abs_reduce_fusion.2 = (f32[256]{0:T(256)S(1)}, f32[256,256]{0,1:T(8,128)S(1)}) fusion(f32[144,32,256]{2,0,1:T(8,128)} %get-tuple-element.301, f32[144,32]{0,1:T(8,128)S(1)} %fusion.215), kind=kOutput, calls=%fused_computation.23.clone.1 | convolution fusion | flops 3625385728 | bytes 5000192 | tf_op jit(solution)/shard_map/while/body/eval_jaxpr/jpk,jpl->kl/dot_general | solution.py:34
  212.3 4.1 convolution_bitcast_fusion.4
  217.7 2.9 fusion.230
  220.7 7.9 %select_add_fusion.2 = f32[144,48,256]{2,0,1:T(8,128)} fusion(f32[144,48,256]{2,0,1:T(8,128)} %get-tuple-element.287, bf16[144,48,256]{2,0,1:T(8,128)(2,1)} %fusion.230, pred[]{:T(512)S(6)} %compare.41), kind=kLoop, calls=%fused_computation.1.clone.1 | loop fusion | flops 5308416 | bytes 17694720 | tf_op jit(solution)/shard_map/while/body/eval_jaxpr/add | solution.py:157
  229.5 12.0 %abs_reduce_fusion.2 = (f32[256]{0:T(256)S(1)}, f32[256,256]{0,1:T(8,128)S(1)}) fusion(f32[144,32,256]{2,0,1:T(8,128)} %get-tuple-element.301, f32[144,32]{0,1:T(8,128)S(1)} %fusion.215), kind=kOutput, calls=%fused_computation.23.clone.1 | convolution fusion | flops 3625385728 | bytes 5000192 | tf_op jit(solution)/shard_map/while/body/eval_jaxpr/jpk,jpl->kl/dot_general | solution.py:34
  251.2 4.1 convolution_bitcast_fusion.4
  256.7 2.9 fusion.230
  259.6 7.9 %select_add_fusion.2 = f32[144,48,256]{2,0,1:T(8,128)} fusion(f32[144,48,256]{2,0,1:T(8,128)} %get-tuple-element.287, bf16[144,48,256]{2,0,1:T(8,128)(2,1)} %fusion.230, pred[]{:T(512)S(6)} %compare.41), kind=kLoop, calls=%fused_computation.1.clone.1 | loop fusion | flops 5308416 | bytes 17694720 | tf_op jit(solution)/shard_map/while/body/eval_jaxpr/add | solution.py:157
  268.4 12.0 %abs_reduce_fusion.2 = (f32[256]{0:T(256)S(1)}, f32[256,256]{0,1:T(8,128)S(1)}) fusion(f32[144,32,256]{2,0,1:T(8,128)} %get-tuple-element.301, f32[144,32]{0,1:T(8,128)S(1)} %fusion.215), kind=kOutput, calls=%fused_computation.23.clone.1 | convolution fusion | flops 3625385728 | bytes 5000192 | tf_op jit(solution)/shard_map/while/body/eval_jaxpr/jpk,jpl->kl/dot_general | solution.py:34
  290.2 4.1 convolution_bitcast_fusion.4
  295.6 2.9 fusion.230
  298.5 7.9 %select_add_fusion.2 = f32[144,48,256]{2,0,1:T(8,128)} fusion(f32[144,48,256]{2,0,1:T(8,128)} %get-tuple-element.287, bf16[144,48,256]{2,0,1:T(8,128)(2,1)} %fusion.230, pred[]{:T(512)S(6)} %compare.41), kind=kLoop, calls=%fused_computation.1.clone.1 | loop fusion | flops 5308416 | bytes 17694720 | tf_op jit(solution)/shard_map/while/body/eval_jaxpr/add | solution.py:157
  307.4 12.0 %abs_reduce_fusion.2 = (f32[256]{0:T(256)S(1)}, f32[256,256]{0,1:T(8,128)S(1)}) fusion(f32[144,32,256]{2,0,1:T(8,128)} %get-tuple-element.301, f32[144,32]{0,1:T(8,128)S(1)} %fusion.215), kind=kOutput, calls=%fused_computation.23.clone.1 | convolution fusion | flops 3625385728 | bytes 5000192 | tf_op jit(solution)/shard_map/while/body/eval_jaxpr/jpk,jpl->kl/dot_general | solution.py:34
  329.1 4.1 convolution_bitcast_fusion.4
  334.6 2.9 fusion.230
  337.5 7.9 %select_add_fusion.2 = f32[144,48,256]{2,0,1:T(8,128)} fusion(f32[144,48,256]{2,0,1:T(8,128)} %get-tuple-element.287, bf16[144,48,256]{2,0,1:T(8,128)(2,1)} %fusion.230, pred[]{:T(512)S(6)} %compare.41), kind=kLoop, calls=%fused_computation.1.clone.1 | loop fusion | flops 5308416 | bytes 17694720 | tf_op jit(solution)/shard_map/while/body/eval_jaxpr/add | solution.py:157
  346.3 12.0 %abs_reduce_fusion.2 = (f32[256]{0:T(256)S(1)}, f32[256,256]{0,1:T(8,128)S(1)}) fusion(f32[144,32,256]{2,0,1:T(8,128)} %get-tuple-element.301, f32[144,32]{0,1:T(8,128)S(1)} %fusion.215), kind=kOutput, calls=%fused_computation.23.clone.1 | convolution fusion | flops 3625385728 | bytes 5000192 | tf_op jit(solution)/shard_map/while/body/eval_jaxpr/jpk,jpl->kl/dot_general | solution.py:34
  368.1 4.1 convolution_bitcast_fusion.4
  373.5 2.9 fusion.230
  376.4 7.9 %select_add_fusion.2 = f32[144,48,256]{2,0,1:T(8,128)} fusion(f32[144,48,256]{2,0,1:T(8,128)} %get-tuple-element.287, bf16[144,48,256]{2,0,1:T(8,128)(2,1)} %fusion.230, pred[]{:T(512)S(6)} %compare.41), kind=kLoop, calls=%fused_computation.1.clone.1 | loop fusion | flops 5308416 | bytes 17694720 | tf_op jit(solution)/shard_map/while/body/eval_jaxpr/add | solution.py:157
  385.2 12.0 %abs_reduce_fusion.2 = (f32[256]{0:T(256)S(1)}, f32[256,256]{0,1:T(8,128)S(1)}) fusion(f32[144,32,256]{2,0,1:T(8,128)} %get-tuple-element.301, f32[144,32]{0,1:T(8,128)S(1)} %fusion.215), kind=kOutput, calls=%fused_computation.23.clone.1 | convolution fusion | flops 3625385728 | bytes 5000192 | tf_op jit(solution)/shard_map/while/body/eval_jaxpr/jpk,jpl->kl/dot_general | solution.py:34
  407.0 4.1 convolution_bitcast_fusion.4
  415.4 7.9 %select_add_fusion.2 = f32[144,48,256]{2,0,1:T(8,128)} fusion(f32[144,48,256]{2,0,1:T(8,128)} %get-tuple-element.287, bf16[144,48,256]{2,0,1:T(8,128)(2,1)} %fusion.230, pred[]{:T(512)S(6)} %compare.41), kind=kLoop, calls=%fused_computation.1.clone.1 | loop fusion | flops 5308416 | bytes 17694720 | tf_op jit(solution)/shard_map/while/body/eval_jaxpr/add | solution.py:157
  424.2 12.0 %abs_reduce_fusion.2 = (f32[256]{0:T(256)S(1)}, f32[256,256]{0,1:T(8,128)S(1)}) fusion(f32[144,32,256]{2,0,1:T(8,128)} %get-tuple-element.301, f32[144,32]{0,1:T(8,128)S(1)} %fusion.215), kind=kOutput, calls=%fused_computation.23.clone.1 | convolution fusion | flops 3625385728 | bytes 5000192 | tf_op jit(solution)/shard_map/while/body/eval_jaxpr/jpk,jpl->kl/dot_general | solution.py:34
  445.9 4.1 convolution_bitcast_fusion.4
  454.3 7.9 %select_add_fusion.2 = f32[144,48,256]{2,0,1:T(8,128)} fusion(f32[144,48,256]{2,0,1:T(8,128)} %get-tuple-element.287, bf16[144,48,256]{2,0,1:T(8,128)(2,1)} %fusion.230, pred[]{:T(512)S(6)} %compare.41), kind=kLoop, calls=%fused_computation.1.clone.1 | loop fusion | flops 5308416 | bytes 17694720 | tf_op jit(solution)/shard_map/while/body/eval_jaxpr/add | solution.py:157
  462.2 3.4 convert_element_type.75
  468.6 4.0 collective-permute-start.9
  473.1 13.8 %collective-permute-done.8 = bf16[3,16,48,256]{3,2,1,0:T(8,128)(2,1)S(1)} collective-permute-done((bf16[3,16,48,256]{3,2,1,0:T(8,128)(2,1)S(1)}, bf16[3,16,48,256]{3,2,1,0:T(8,128)(2,1)S(1)}, u32[]{:S(2)}, u32[]{:S(2)}) %collective-permute-start.8) | collective-permute-done | bytes 1179680 | tf_op jit(solution)/shard_map/ppermute | solution.py:13
  489.8 5.7 %collective-permute-start.10 = (bf16[3,16,48,256]{3,2,1,0:T(8,128)(2,1)S(1)}, bf16[3,16,48,256]{3,2,1,0:T(8,128)(2,1)S(1)}, u32[]{:S(2)}, u32[]{:S(2)}) collective-permute-start(bf16[3,16,48,256]{3,2,1,0:T(8,128)(2,1)S(1)} %get-tuple-element.208), channel_id=1, source_target_pairs={{1,0},{2,1},{3,2},{4,3},{5,4},{6,5},{7,6},{8,7},{9,8},{10,9},{11,1... | collective-permute-start | bytes 3538952 | tf_op jit(solution)/shard_map/ppermute | solution.py:19
  495.4 13.7 %collective-permute-done.10 = bf16[3,16,48,256]{3,2,1,0:T(8,128)(2,1)S(1)} collective-permute-done((bf16[3,16,48,256]{3,2,1,0:T(8,128)(2,1)S(1)}, bf16[3,16,48,256]{3,2,1,0:T(8,128)(2,1)S(1)}, u32[]{:S(2)}, u32[]{:S(2)}) %collective-permute-start.10) | collective-permute-done | bytes 1179680 | tf_op jit(solution)/shard_map/ppermute | solution.py:19
  509.2 5.2 %collective-permute-done.11 = bf16[3,16,48,256]{3,2,1,0:T(8,128)(2,1)S(1)} collective-permute-done((bf16[3,16,48,256]{3,2,1,0:T(8,128)(2,1)S(1)}, bf16[3,16,48,256]{3,2,1,0:T(8,128)(2,1)S(1)}, u32[]{:S(2)}, u32[]{:S(2)}) %collective-permute-start.11) | collective-permute-done | bytes 1179680 | tf_op jit(solution)/shard_map/ppermute | solution.py:19
  (271 shorter events, 159.1 us)
Async XLA Ops:
  0.0 2.4 copy-start
  0.0 14.2 %copy-start.5 = (bf16[48,32]{0,1:T(8,128)(2,1)S(1)}, bf16[48,32]{0,1:T(8,128)(2,1)}, u32[]{:S(2)}) copy-start(bf16[48,32]{0,1:T(8,128)(2,1)} %param.11) | copy-start | bytes 9220
  0.0 14.3 %copy-start.3 = (bf16[48,48,256]{2,1,0:T(8,128)(2,1)S(1)}, bf16[48,48,256]{2,1,0:T(8,128)(2,1)}, u32[]{:S(2)}) copy-start(bf16[48,48,256]{2,1,0:T(8,128)(2,1)} %param.9) | copy-start | bytes 3538948
  8.3 9.1 %collective-permute-start = (s32[3,16]{1,0:T(4,128)S(1)}, s32[3,16]{1,0:T(4,128)S(1)}, u32[]{:S(2)}, u32[]{:S(2)}) collective-permute-start(s32[3,16]{1,0:T(4,128)S(1)} %slice.97), channel_id=1, source_target_pairs={{32,0},{64,32},{96,64},{33,1},{65,33},{97,65},{34,2},{66,34},{98,6... | collective-permute-start | bytes 584 | tf_op jit(solution)/shard_map/ppermute | solution.py:13
  10.8 6.6 %collective-permute-start.1 = (s32[3,16]{1,0:T(4,128)S(1)}, s32[3,16]{1,0:T(4,128)S(1)}, u32[]{:S(2)}, u32[]{:S(2)}) collective-permute-start(s32[3,16]{1,0:T(4,128)S(1)} %slice.101), channel_id=1, source_target_pairs={{0,32},{32,64},{64,96},{1,33},{33,65},{65,97},{2,34},{34,66},{66,9... | collective-permute-start | bytes 584 | tf_op jit(solution)/shard_map/ppermute | solution.py:13
  17.4 6.7 %collective-permute-start.2 = (s32[3,16]{1,0:T(4,128)S(1)}, s32[3,16]{1,0:T(4,128)S(1)}, u32[]{:S(2)}, u32[]{:S(2)}) collective-permute-start(s32[3,16]{1,0:T(4,128)S(1)} %bitcast.255), channel_id=1, source_target_pairs={{1,0},{2,1},{3,2},{4,3},{5,4},{6,5},{7,6},{8,7},{9,8},{10,9},{11,1... | collective-permute-start | bytes 584 | tf_op jit(solution)/shard_map/ppermute | solution.py:19
  22.8 6.3 %collective-permute-start.3 = (s32[3,16]{1,0:T(4,128)S(1)}, s32[3,16]{1,0:T(4,128)S(1)}, u32[]{:S(2)}, u32[]{:S(2)}) collective-permute-start(s32[3,16]{1,0:T(4,128)S(1)} %bitcast.257), channel_id=1, source_target_pairs={{31,0},{0,1},{1,2},{2,3},{3,4},{4,5},{5,6},{6,7},{7,8},{8,9},{9,10... | collective-permute-start | bytes 584 | tf_op jit(solution)/shard_map/ppermute | solution.py:19
  39.8 42.3 %collective-permute-start.5 = (bf16[3,16,81,256]{3,1,2,0:T(8,128)(2,1)}, bf16[3,16,81,256]{3,1,2,0:T(8,128)(2,1)}, u32[]{:S(2)}, u32[]{:S(2)}) collective-permute-start(bf16[3,16,81,256]{3,1,2,0:T(8,128)(2,1)} %copy.141), channel_id=1, source_target_pairs={{32,0},{64,32},{96,64},{33,1},{65,33},{97,65},{34,2},{66,34},{98,6... | collective-permute-start | bytes 5971976 | tf_op jit(solution)/shard_map/ppermute | solution.py:13
  46.7 42.3 %collective-permute-start.4 = (bf16[3,16,81,256]{3,1,2,0:T(8,128)(2,1)}, bf16[3,16,81,256]{3,1,2,0:T(8,128)(2,1)}, u32[]{:S(2)}, u32[]{:S(2)}) collective-permute-start(bf16[3,16,81,256]{3,1,2,0:T(8,128)(2,1)} %copy.139), channel_id=1, source_target_pairs={{0,32},{32,64},{64,96},{1,33},{33,65},{65,97},{2,34},{34,66},{66,9... | collective-permute-start | bytes 5971976 | tf_op jit(solution)/shard_map/ppermute | solution.py:13
  94.3 26.8 %collective-permute-start.7 = (bf16[3,16,81,256]{3,1,2,0:T(8,128)(2,1)}, bf16[3,16,81,256]{3,1,2,0:T(8,128)(2,1)}, u32[]{:S(2)}, u32[]{:S(2)}) collective-permute-start(bf16[3,16,81,256]{3,1,2,0:T(8,128)(2,1)} %copy.145), channel_id=1, source_target_pairs={{1,0},{2,1},{3,2},{4,3},{5,4},{6,5},{7,6},{8,7},{9,8},{10,9},{11,1... | collective-permute-start | bytes 5971976 | tf_op jit(solution)/shard_map/ppermute | solution.py:19
  100.1 43.3 %collective-permute-start.6 = (bf16[3,16,81,256]{3,1,2,0:T(8,128)(2,1)}, bf16[3,16,81,256]{3,1,2,0:T(8,128)(2,1)}, u32[]{:S(2)}, u32[]{:S(2)}) collective-permute-start(bf16[3,16,81,256]{3,1,2,0:T(8,128)(2,1)} %copy.143), channel_id=1, source_target_pairs={{31,0},{0,1},{1,2},{2,3},{3,4},{4,5},{5,6},{6,7},{7,8},{8,9},{9,10... | collective-permute-start | bytes 5971976 | tf_op jit(solution)/shard_map/ppermute | solution.py:19
  175.4 5.5 %copy-start.2 = (bf16[144,48,256]{2,0,1:T(8,128)(2,1)S(1)}, bf16[144,48,256]{2,0,1:T(8,128)(2,1)}, u32[]{:S(2)}) copy-start(bf16[144,48,256]{2,0,1:T(8,128)(2,1)} %get-tuple-element.303) | copy-start | bytes 10616836 | tf_op jit(solution)/shard_map/while
  212.3 5.5 %copy-start.2 = (bf16[144,48,256]{2,0,1:T(8,128)(2,1)S(1)}, bf16[144,48,256]{2,0,1:T(8,128)(2,1)}, u32[]{:S(2)}) copy-start(bf16[144,48,256]{2,0,1:T(8,128)(2,1)} %get-tuple-element.303) | copy-start | bytes 10616836 | tf_op jit(solution)/shard_map/while
  251.2 5.5 %copy-start.2 = (bf16[144,48,256]{2,0,1:T(8,128)(2,1)S(1)}, bf16[144,48,256]{2,0,1:T(8,128)(2,1)}, u32[]{:S(2)}) copy-start(bf16[144,48,256]{2,0,1:T(8,128)(2,1)} %get-tuple-element.303) | copy-start | bytes 10616836 | tf_op jit(solution)/shard_map/while
  290.2 5.5 %copy-start.2 = (bf16[144,48,256]{2,0,1:T(8,128)(2,1)S(1)}, bf16[144,48,256]{2,0,1:T(8,128)(2,1)}, u32[]{:S(2)}) copy-start(bf16[144,48,256]{2,0,1:T(8,128)(2,1)} %get-tuple-element.303) | copy-start | bytes 10616836 | tf_op jit(solution)/shard_map/while
  329.1 5.5 %copy-start.2 = (bf16[144,48,256]{2,0,1:T(8,128)(2,1)S(1)}, bf16[144,48,256]{2,0,1:T(8,128)(2,1)}, u32[]{:S(2)}) copy-start(bf16[144,48,256]{2,0,1:T(8,128)(2,1)} %get-tuple-element.303) | copy-start | bytes 10616836 | tf_op jit(solution)/shard_map/while
  368.0 5.5 %copy-start.2 = (bf16[144,48,256]{2,0,1:T(8,128)(2,1)S(1)}, bf16[144,48,256]{2,0,1:T(8,128)(2,1)}, u32[]{:S(2)}) copy-start(bf16[144,48,256]{2,0,1:T(8,128)(2,1)} %get-tuple-element.303) | copy-start | bytes 10616836 | tf_op jit(solution)/shard_map/while
  407.0 5.5 %copy-start.2 = (bf16[144,48,256]{2,0,1:T(8,128)(2,1)S(1)}, bf16[144,48,256]{2,0,1:T(8,128)(2,1)}, u32[]{:S(2)}) copy-start(bf16[144,48,256]{2,0,1:T(8,128)(2,1)} %get-tuple-element.303) | copy-start | bytes 10616836 | tf_op jit(solution)/shard_map/while
  445.9 5.5 %copy-start.2 = (bf16[144,48,256]{2,0,1:T(8,128)(2,1)S(1)}, bf16[144,48,256]{2,0,1:T(8,128)(2,1)}, u32[]{:S(2)}) copy-start(bf16[144,48,256]{2,0,1:T(8,128)(2,1)} %get-tuple-element.303) | copy-start | bytes 10616836 | tf_op jit(solution)/shard_map/while
  466.3 20.6 %collective-permute-start.8 = (bf16[3,16,48,256]{3,2,1,0:T(8,128)(2,1)S(1)}, bf16[3,16,48,256]{3,2,1,0:T(8,128)(2,1)S(1)}, u32[]{:S(2)}, u32[]{:S(2)}) collective-permute-start(bf16[3,16,48,256]{3,2,1,0:T(8,128)(2,1)S(1)} %copy.149), channel_id=1, source_target_pairs={{32,0},{64,32},{96,64},{33,1},{65,33},{97,65},{34,2},{66,34},{98,6... | collective-permute-start | bytes 3538952 | tf_op jit(solution)/shard_map/ppermute | solution.py:13
  468.6 20.5 %collective-permute-start.9 = (bf16[3,16,48,256]{3,2,1,0:T(8,128)(2,1)S(1)}, bf16[3,16,48,256]{3,2,1,0:T(8,128)(2,1)S(1)}, u32[]{:S(2)}, u32[]{:S(2)}) collective-permute-start(bf16[3,16,48,256]{3,2,1,0:T(8,128)(2,1)S(1)} %copy.150), channel_id=1, source_target_pairs={{0,32},{32,64},{64,96},{1,33},{33,65},{65,97},{2,34},{34,66},{66,9... | collective-permute-start | bytes 3538952 | tf_op jit(solution)/shard_map/ppermute | solution.py:13
  489.8 19.4 %collective-permute-start.10 = (bf16[3,16,48,256]{3,2,1,0:T(8,128)(2,1)S(1)}, bf16[3,16,48,256]{3,2,1,0:T(8,128)(2,1)S(1)}, u32[]{:S(2)}, u32[]{:S(2)}) collective-permute-start(bf16[3,16,48,256]{3,2,1,0:T(8,128)(2,1)S(1)} %get-tuple-element.208), channel_id=1, source_target_pairs={{1,0},{2,1},{3,2},{4,3},{5,4},{6,5},{7,6},{8,7},{9,8},{10,9},{11,1... | collective-permute-start | bytes 3538952 | tf_op jit(solution)/shard_map/ppermute | solution.py:19
  495.4 18.9 %collective-permute-start.11 = (bf16[3,16,48,256]{3,2,1,0:T(8,128)(2,1)S(1)}, bf16[3,16,48,256]{3,2,1,0:T(8,128)(2,1)S(1)}, u32[]{:S(2)}, u32[]{:S(2)}) collective-permute-start(bf16[3,16,48,256]{3,2,1,0:T(8,128)(2,1)S(1)} %get-tuple-element.209), channel_id=1, source_target_pairs={{31,0},{0,1},{1,2},{2,3},{3,4},{4,5},{5,6},{6,7},{7,8},{8,9},{9,10... | collective-permute-start | bytes 3538952 | tf_op jit(solution)/shard_map/ppermute | solution.py:19
  514.4 1.3 copy-start.4
  515.7 3.0 copy-start.1
where the time goes:
time: 529 us; the launch traced here: 519 us
  matrix products  242 us (46%)
  waiting for transfers between devices  99.2 us (19%)
  other arithmetic  78.5 us (15%)
  starting transfers between devices  49.4 us (9%)
  local copies, waits for them, and re-layouts  43 us (8%)
  loops' own time  6.05 us (1%)
    dot_general x8, matrix products, region_mix(): jnp.einsum('jpk,jpl->kl', obs_float * slot_weights[:, :, None], obs_float...  96 us
    add x8, other arithmetic, one_region(): return increment + portion.astype(jnp.float32)  61.5 us
    ppermute x6, waiting for transfers between devices, shifted(): return lax.ppermute(block, axis, route)  50.7 us
    ppermute x6, waiting for transfers between devices, from_behind(): return lax.ppermute(block, axis, route)  48.5 us
    dot_general x8, matrix products, region_mix(): jnp.einsum('jp,jpk->k', slot_weights * innov_float, obs_float, precision=...  32.9 us
    ppermute x6, starting transfers between devices, shifted(): return lax.ppermute(block, axis, route)  30.5 us
    dot_general x40, matrix products, inverse_root(): jnp.dot(estimate, current, precision=lax.Precision.HIGHEST)  25.9 us
    dot_general x8, matrix products, one_region(): jnp.einsum('qsk,kl->qsl', state_pool, mixing, preferred_element_type=jnp....  23.3 us
  transfers between devices with their start and end apart: 12, of which 10 were waited for; matrix products, arithmetic and copies ran while one was open for 3% of the time, Pallas kernels for 0%

commit v1 on v0

v1 whole, which is shorter than its diff:
```python
import functools

import jax
import jax.numpy as jnp
from jax import lax
from jax.experimental import pallas as pl
from jax.experimental.pallas import tpu as pltpu
from jax.sharding import PartitionSpec as P

NS_ITERS = 5
CAP = 16
CLASSES = 9
BAND_SLOTS = 3 * CAP
CLASS_STRIDE = 64
KEYS = 640
META_LANES = 256

F32 = jnp.float32
BF16 = jnp.bfloat16
VMEM_SPEC = pl.BlockSpec(memory_space=pltpu.VMEM)
SMEM_SPEC = pl.BlockSpec(memory_space=pltpu.SMEM)


def dot(a, b):
    return jnp.dot(a, b, preferred_element_type=F32)


def call(kernel, outs, in_specs, name, flops, bytes_accessed, scratch=(), aliases=None):
    return pl.pallas_call(
        kernel,
        out_shape=outs,
        in_specs=in_specs,
        out_specs=jax.tree.map(lambda _: VMEM_SPEC, outs),
        scratch_shapes=list(scratch),
        input_output_aliases=aliases or {},
        compiler_params=pltpu.CompilerParams(vmem_limit_bytes=40 * 1024 * 1024),
        cost_estimate=pl.CostEstimate(
            flops=flops, bytes_accessed=bytes_accessed, transcendentals=0
        ),
        name=name,
    )


def table_kernel(regions, list_len, key_col, key_row, taper, state, weights, meta):
    entries = regions * list_len
    key_down = lax.broadcasted_iota(jnp.int32, (KEYS, entries), 0)
    hot_t = jnp.where(key_down == key_row[...], 1.0, 0.0).astype(BF16)
    counts = dot(hot_t, jnp.ones((entries, 128), BF16))
    present = jnp.minimum(counts, 1.0)
    row = lax.broadcasted_iota(jnp.int32, (KEYS, KEYS), 0)
    col = lax.broadcasted_iota(jnp.int32, (KEYS, KEYS), 1)
    before = (col < row) & (col // CLASS_STRIDE == row // CLASS_STRIDE)
    rank = dot(jnp.where(before, 1.0, 0.0).astype(BF16), present.astype(BF16))
    key_id = lax.broadcasted_iota(jnp.int32, (KEYS, 128), 0)
    slot = rank + (CAP * (key_id // CLASS_STRIDE)).astype(F32)
    inside = (key_id % CLASS_STRIDE).astype(F32)
    key_across = lax.broadcasted_iota(jnp.int32, (entries, KEYS), 1)
    hot = jnp.where(key_across == key_col[...], 1.0, 0.0).astype(BF16)
    entry_slot = dot(hot, slot.astype(BF16))
    lane = lax.broadcasted_iota(jnp.int32, (1, 128), 1).astype(F32)
    group = (lax.broadcasted_iota(jnp.int32, (1, 128), 1) // 32).astype(F32)
    meta[...] = jnp.zeros_like(meta)
    for c in range(2):
        match = (slot == lane + 128.0 * c) & (present > 0.0)
        rows = jnp.sum(jnp.where(match, inside, 0.0), axis=0, keepdims=True)
        meta[8:9, 128 * c : 128 * (c + 1)] = rows
    for r in range(regions):
        mine = entry_slot[r * list_len : (r + 1) * list_len]
        w = taper[r]
        for c in range(CLASSES * CAP // 4):
            hit = mine == group + 4.0 * c
            weights[r : r + 1, 128 * c : 128 * (c + 1)] = jnp.sum(
                jnp.where(hit, w, 0.0), axis=0, keepdims=True
            )
        t = state[r * list_len : (r + 1) * list_len]
        for c in range(2):
            hit = mine == lane + 128.0 * c
            meta[r : r + 1, 128 * c : 128 * (c + 1)] = jnp.sum(
                jnp.where(hit, t, 0.0), axis=0, keepdims=True
            )


def gather_blocks(sources, table, rows, first_slot, obs_rows, out):
    blocks = sources[0].shape[0] // (obs_rows + 1)
    down = lax.broadcasted_iota(jnp.int32, (blocks, META_LANES), 0).astype(F32)
    hot = jnp.where(down == rows, 1.0, 0.0).astype(BF16)
    for band in range(3):
        source = sources[band]

        def one(i, carry, source=source, band=band):
            slot = first_slot + CAP * band + i
            at = pl.multiple_of(table[8, slot].astype(jnp.int32) * obs_rows, obs_rows)
            to = pl.multiple_of((CAP * band + i) * obs_rows, obs_rows)
            out[pl.ds(to, obs_rows), :] = source[pl.ds(at, obs_rows), :]
            return carry

        lax.fori_loop(0, CAP, one, 0, unroll=True)
        innov = source[blocks * obs_rows :, :]
        picked = lax.dot_general(
            hot, innov, (((0,), (0,)), ((), ())), preferred_element_type=F32
        ).astype(BF16)
        base = 3 * CAP * obs_rows + CAP * band
        start = first_slot + CAP * band
        out[base : base + CAP, :] = picked[start : start + CAP]


def select_kernel(obs_rows, below, here, above, table_w, table_e, rows_w, rows_e, to_w, to_e):
    sources = (below, here, above)
    gather_blocks(sources, table_w, rows_w[8:9, :], 2 * BAND_SLOTS, obs_rows, to_w)
    gather_blocks(sources, table_e, rows_e[8:9, :], 0, obs_rows, to_e)


def add_gram(pool, first_slot, weights, obs_rows, regions, gram, proj, start):
    count = BAND_SLOTS * obs_rows
    lanes = slice(first_slot * obs_rows, first_slot * obs_rows + count)
    y = pool[:count, :]
    y_t = jnp.concatenate(
        [y[256 * c : 256 * (c + 1)].astype(F32).T.astype(BF16) for c in range(count // 256)],
        axis=1,
    )
    innov = pool[count : count + BAND_SLOTS, :].astype(F32)
    per = 256 // obs_rows
    sub = lax.broadcasted_iota(jnp.int32, (per, 256), 0)
    which = lax.broadcasted_iota(jnp.int32, (per, 256), 1) // obs_rows
    pieces = [
        jnp.sum(jnp.where(sub == which, innov[per * c : per * (c + 1)], 0.0), axis=0, keepdims=True)
        for c in range(count // 256)
    ]
    w = weights[:, lanes]
    wd = w * jnp.concatenate(pieces, axis=1)
    high = wd.astype(BF16)
    low = (wd - high.astype(F32)).astype(BF16)
    part = dot(jnp.concatenate([high, low], axis=0), y)
    part = part[:regions] + part[regions:]
    proj[...] = part if start else proj[...] + part
    w16 = w.astype(BF16)
    for r in range(regions):
        scaled = y_t * w16[r : r + 1, :]
        product = dot(scaled, y)
        rows = slice(256 * r, 256 * (r + 1))
        gram[rows, :] = product if start else gram[rows, :] + product


def own_gram_kernel(
    obs_rows, regions, below, here, above, table, rows, weights, gram, proj, pool
):
    gather_blocks((below, here, above), table, rows[8:9, :], BAND_SLOTS, obs_rows, pool)
    add_gram(pool, BAND_SLOTS, weights, obs_rows, regions, gram, proj, True)


def total(x):
    return jnp.sum(jnp.sum(x, axis=0, keepdims=True), axis=1, keepdims=True)


def roots(grams, proj_rows, eye, ensemble):
    count = len(grams)
    base = ensemble - 1.0
    each = range(count)
    absolute = [jnp.abs(grams[i] + base * eye) for i in each]
    scale = [
        jnp.max(jnp.sum(absolute[i], axis=0, keepdims=True), axis=1, keepdims=True) for i in each
    ]
    mean = [total(grams[i] * eye) / ensemble for i in each]
    f = [(mean[i] * eye - grams[i]) / scale[i] for i in each]
    c = [1.0 - (base + mean[i]) / scale[i] for i in each]
    a = [1.0 + 0.5 * c[i] for i in each]
    g = [0.5 * f[i] for i in each]
    for step in range(NS_ITERS - 1):
        fb = [f[i].astype(BF16) for i in each]
        f2 = [dot(fb[i], fb[i]) for i in each]
        f3 = [dot(f2[i].astype(BF16), fb[i]) for i in each]
        f = [
            (1.5 * c[i] + 0.75 * c[i] * c[i]) * f[i]
            + (0.75 + 0.75 * c[i]) * f2[i]
            + 0.25 * f3[i]
            for i in each
        ]
        c = [(0.75 + 0.25 * c[i]) * c[i] * c[i] for i in each]
        fg = [dot(f[i].astype(BF16), g[i].astype(BF16)) for i in each]
        g = [
            (1.0 + 0.5 * c[i]) * g[i] + (0.5 * a[i]) * f[i] + 0.5 * fg[i] for i in each
        ]
        a = [a[i] * (1.0 + 0.5 * c[i]) for i in each]
    gb = [g[i].astype(BF16) for i in each]
    first = lax.broadcasted_iota(jnp.int32, (16, ensemble), 0) < 8

    def times(i, v):
        high = v.astype(BF16).astype(F32)
        stacked = jnp.where(first, high, v - high).astype(BF16)
        q = dot(stacked, gb[i])
        return a[i] * v + q[0:1] + q[8:9]

    half = [times(i, proj_rows[i]) for i in each]
    wbar = [times(i, half[i]) / scale[i] for i in each]
    root = [a[i] * eye + g[i] for i in each]
    column = [jnp.sum(eye * wbar[i], axis=1, keepdims=True) for i in each]
    return [
        (lax.sqrt(base / scale[i]) * root[i] - eye + column[i]).astype(BF16) for i in each
    ]


def mix_kernel(obs_rows, regions, together, west, east, weights, gram_in, proj_in, mix, gram, proj):
    gram[...] = gram_in[...]
    proj[...] = proj_in[...]
    add_gram(west, 0, weights, obs_rows, regions, gram, proj, False)
    add_gram(east, 2 * BAND_SLOTS, weights, obs_rows, regions, gram, proj, False)
    n = gram.shape[1]
    down = lax.broadcasted_iota(jnp.int32, (n, n), 0)
    across = lax.broadcasted_iota(jnp.int32, (n, n), 1)
    eye = jnp.where(down == across, 1.0, 0.0)
    for first in range(0, regions, together):
        some = range(first, first + together)
        done = roots(
            [gram[n * r : n * (r + 1), :] for r in some],
            [proj[r : r + 1, :] for r in some],
            eye,
            n,
        )
        for r, m in zip(some, done):
            mix[n * r : n * (r + 1), :] = m


def add_increment(members, table, first_slot, mix, acc, left, right, state_rows, regions):
    n = members.shape[1]
    for i in range(CAP):
        at = pl.multiple_of(table[8, first_slot + i].astype(jnp.int32) * state_rows, state_rows)
        x = members[pl.ds(at, state_rows), :].astype(F32)
        for r in range(regions):
            left[state_rows * i : state_rows * (i + 1), n * r : n * (r + 1)] = (
                x * table[r, first_slot + i]
            ).astype(BF16)
    right[...] = dot(left[...], mix[...])
    for i in range(CAP):
        at = pl.multiple_of(table[8, first_slot + i].astype(jnp.int32) * state_rows, state_rows)
        acc[pl.ds(at, state_rows), :] += right[state_rows * i : state_rows * (i + 1), :]


def middle_kernel(slots, state_rows, regions, members, *refs):
    count = len(slots)
    tables, mixes = refs[:count], refs[count : 2 * count]
    acc, left, right = refs[2 * count :]
    acc[...] = members[...].astype(F32)
    for k in range(count):
        add_increment(
            members, tables[k], slots[k], mixes[k], acc, left, right, state_rows, regions
        )


def final_kernel(slots, state_rows, regions, members, acc_in, *refs):
    count = len(slots)
    tables, mixes = refs[:count], refs[count : 2 * count]
    out, acc, left, right = refs[2 * count :]
    acc[...] = acc_in[...]
    for k in range(count):
        add_increment(
            members, tables[k], slots[k], mixes[k], acc, left, right, state_rows, regions
        )
    out[...] = acc[...].astype(BF16)


def from_band(x, step):
    devices = range(lax.axis_size("band"))
    return lax.ppermute(x, "band", [(i + step, i) for i in devices if i + step in devices])


def from_lon(x, step):
    count = lax.axis_size("lon")
    return lax.ppermute(x, "lon", [((i + step) % count, i) for i in range(count)])


def local(members, obs_perts, innovations, lists, placement, obs_taper, state_taper):
    lon_count = lax.axis_size("lon")
    band_here = lax.axis_index("band")
    lon_here = lax.axis_index("lon")
    blocks, state_rows, n = members.shape
    obs_rows = obs_perts.shape[1]
    regions, list_len = lists.shape
    entries = regions * list_len
    repeat = n // obs_rows

    payload = jnp.concatenate(
        [obs_perts.reshape(blocks * obs_rows, n), jnp.tile(innovations, (1, repeat))], axis=0
    )
    below = from_band(payload, -1)
    above = from_band(payload, 1)

    row_ids = jnp.take(placement, lists.reshape(-1), axis=0)
    holder = row_ids // blocks
    band_step = holder // lon_count - band_here
    lon_step = (holder % lon_count - lon_here + 1) % lon_count - 1
    key = ((lon_step + 1) * 3 + band_step + 1) * CLASS_STRIDE + row_ids % blocks
    weights, meta = call(
        functools.partial(table_kernel, regions, list_len),
        (
            jax.ShapeDtypeStruct((regions, CLASSES * CAP * obs_rows), F32),
            jax.ShapeDtypeStruct((16, META_LANES), F32),
        ),
        [VMEM_SPEC] * 4,
        "tables",
        10**9,
        10**6,
    )(
        key[:, None],
        key[None, :],
        jnp.tile(obs_taper, (1, 1, 128 // obs_rows)),
        state_taper.reshape(entries, 1),
    )
    meta_w = from_lon(meta, -1)
    meta_e = from_lon(meta, 1)

    sent = (BAND_SLOTS * (obs_rows + 1), n)
    sent_shape = jax.ShapeDtypeStruct(sent, BF16)
    to_w, to_e = call(
        functools.partial(select_kernel, obs_rows),
        (sent_shape, sent_shape),
        [VMEM_SPEC] * 3 + [SMEM_SPEC] * 2 + [VMEM_SPEC] * 2,
        "select",
        10**8,
        4 * 10**6,
    )(below, payload, above, meta_w, meta_e, meta_w, meta_e)
    west = from_lon(to_e, -1)
    east = from_lon(to_w, 1)

    metas = jnp.concatenate([meta_w, meta, meta_e], axis=0)
    metas_below = from_band(metas, -1)
    metas_above = from_band(metas, 1)

    gram_shape = jax.ShapeDtypeStruct((regions * n, n), F32)
    proj_shape = jax.ShapeDtypeStruct((regions, n), F32)
    gram, proj = call(
        functools.partial(own_gram_kernel, obs_rows, regions),
        (gram_shape, proj_shape),
        [VMEM_SPEC] * 3 + [SMEM_SPEC] + [VMEM_SPEC] * 2,
        "own_gram",
        2 * regions * sent[0] * n * n,
        5 * 10**6,
        [pltpu.VMEM(sent, BF16)],
    )(below, payload, above, meta, meta, weights)
    mix = call(
        functools.partial(mix_kernel, obs_rows, regions, 4),
        jax.ShapeDtypeStruct((regions * n, n), BF16),
        [VMEM_SPEC] * 5,
        "mixing",
        2 * regions * (2 * sent[0] + 12 * n) * n * n,
        5 * 10**6,
        [pltpu.VMEM((regions * n, n), F32), pltpu.VMEM((regions, n), F32)],
    )(west, east, weights, gram, proj)

    mix_below = from_band(mix, -1)
    mix_above = from_band(mix, 1)
    mix_w = from_lon(mix, -1)
    mix_e = from_lon(mix, 1)
    mix_wb = from_lon(mix_below, -1)
    mix_eb = from_lon(mix_below, 1)
    mix_wa = from_lon(mix_above, -1)
    mix_ea = from_lon(mix_above, 1)

    stacked = {-1: metas_below, 0: metas, 1: metas_above}

    def table(lon, band):
        return stacked[band][16 * (lon + 1) : 16 * (lon + 2)]

    def slots(lon, band):
        return CAP * (CLASSES - 1 - ((lon + 1) * 3 + band + 1))

    flat = members.reshape(blocks * state_rows, n)
    scratch = [
        pltpu.VMEM((CAP * state_rows, regions * n), BF16),
        pltpu.VMEM((CAP * state_rows, n), F32),
    ]
    inner = [(0, 0), (0, -1), (0, 1), (-1, 0), (1, 0)]
    group_flops = 2 * CAP * state_rows * regions * n * n
    acc = call(
        functools.partial(middle_kernel, [slots(*o) for o in inner], state_rows, regions),
        jax.ShapeDtypeStruct((blocks * state_rows, n), F32),
        [VMEM_SPEC] + [SMEM_SPEC] * 5 + [VMEM_SPEC] * 5,
        "increments",
        5 * group_flops,
        9 * 10**6,
        scratch,
    )(flat, *[table(*o) for o in inner], mix, mix_below, mix_above, mix_w, mix_e)
    outer = [(-1, -1), (1, -1), (-1, 1), (1, 1)]
    out = call(
        functools.partial(final_kernel, [slots(*o) for o in outer], state_rows, regions),
        jax.ShapeDtypeStruct((blocks * state_rows, n), BF16),
        [VMEM_SPEC] * 2 + [SMEM_SPEC] * 4 + [VMEM_SPEC] * 4,
        "finish",
        4 * group_flops,
        9 * 10**6,
        [pltpu.VMEM((blocks * state_rows, n), F32)] + scratch,
    )(flat, acc, *[table(*o) for o in outer], mix_wb, mix_eb, mix_wa, mix_ea)
    return out.reshape(members.shape)


def solution(mesh):
    in_specs = (
        P(("band", "lon"), None, None),
        P(("band", "lon"), None, None),
        P(("band", "lon"), None),
        P(("band", "lon"), None),
        P(),
        P(("band", "lon"), None, None),
        P(("band", "lon"), None),
    )
    out_specs = P(("band", "lon"), None, None)
    return jax.shard_map(local, mesh=mesh, in_specs=in_specs, out_specs=out_specs, check_vma=False)
```

time: 529 us -> 124 us (0.23); the launches traced: 519 us -> 122 us
  matrix products: 242 us -> 0 us
  other arithmetic: 78.5 us -> 2.11 us
  waiting for transfers between devices: 99.2 us -> 41.9 us
  local copies, waits for them, and re-layouts: 43 us -> 6.81 us
  Pallas kernels: 0 us -> 29.2 us
  starting transfers between devices: 49.4 us -> 41.8 us
  loops' own time: 6.05 us -> 0 us
    dot_general x170 -> x0, matrix products: 242 us -> none  [the longest x8 96 us: region_mix(): jnp.einsum('jpk,jpl->kl', obs_float * slot_weights[:, :, None], obs_float...]
    add x13 -> x2, other arithmetic: 61.7 us -> 0.77 us  [local(): key = ((lon_step + 1) * 3 + band_step + 1) * CLASS_STRIDE + row_ids % blocks]
    ppermute x12 -> x16, waiting for transfers between devices: 99.2 us -> 41.9 us  [the longest x6 21.4 us: from_band(): lax.ppermute(x, 'band', [(i + step, i) for i in devices if i + step in de...]
    pallas_call x0 -> x6, Pallas kernels: none -> 29.2 us  [the longest x1 9.53 us: local(): call(functools.partial(mix_kernel, obs_rows, regions, 4), jax.ShapeDtypeS...]
    squeeze x10 -> x0, local copies, waits for them, and re-layouts: 14 us -> none  [the longest x6 9.81 us: spread(): portion = layered[ordinal]]
    ppermute x4 -> x0, local copies, waits for them, and re-layouts: 9.15 us -> none  [the longest x2 4.57 us: shifted(): return lax.ppermute(block, axis, route)]
    slice x11 -> x2, local copies, waits for them, and re-layouts: 8.85 us -> 0.01 us  [table(): return stacked[band][16 * (lon + 1):16 * (lon + 2)]]
    ppermute x12 -> x16, starting transfers between devices: 49.4 us -> 41.8 us  [the longest x10 25.3 us: from_lon(): lax.ppermute(x, 'lon', [((i + step) % count, i) for i in range(count)])]
  transfers between devices with their start and end apart: 12 -> 16, of which waited for: 10 -> 9; matrix products, arithmetic and copies ran while one was open for 3% -> 6% of each run, Pallas kernels for 0% -> 10%
where the time goes in v1:
time: 124 us; the launch traced here: 122 us
  waiting for transfers between devices  41.9 us (34%)
  starting transfers between devices  41.8 us (34%)
  Pallas kernels  29.2 us (24%)
  local copies, waits for them, and re-layouts  6.81 us (5%)
  other arithmetic  2.11 us (2%)
    ppermute x10, starting transfers between devices, from_lon(): lax.ppermute(x, 'lon', [((i + step) % count, i) for i in range(count)])  25.3 us
    ppermute x6, waiting for transfers between devices, from_band(): lax.ppermute(x, 'band', [(i + step, i) for i in devices if i + step in de...  21.4 us
    ppermute x10, waiting for transfers between devices, from_lon(): lax.ppermute(x, 'lon', [((i + step) % count, i) for i in range(count)])  20.6 us
    ppermute x6, starting transfers between devices, from_band(): lax.ppermute(x, 'band', [(i + step, i) for i in devices if i + step in de...  16.5 us
    pallas_call x1, Pallas kernels, local(): call(functools.partial(mix_kernel, obs_rows, regions, 4), jax.ShapeDtypeS...  9.53 us
    pallas_call x1, Pallas kernels, local(): call(functools.partial(final_kernel, [slots(*o) for o in outer], state_ro...  6.38 us
    pallas_call x1, Pallas kernels, local(): call(functools.partial(middle_kernel, [slots(*o) for o in inner], state_r...  6.34 us
    gather x2, local copies, waits for them, and re-layouts, local(): row_ids = jnp.take(placement, lists.reshape(-1), axis=0)  3.29 us
  transfers between devices with their start and end apart: 16, of which 9 were waited for; matrix products, arithmetic and copies ran while one was open for 6% of the time, Pallas kernels for 10%

profile of v1, /device:TPU:4, one launch (start us, length us, event | category | flops | bytes accessed | tf_op | source)
XLA Modules:
  0.0 122.1 jit_solution(10752967117985067361)
XLA Ops:
  0.0 0.8 copy.24
  0.8 0.1 tile.21
  0.9 1.2 pad_maximum_fusion.here
  2.1 0.0 copy-start.2
  2.2 3.2 %collective-permute-start.4 = (bf16[1584,256]{1,0:T(8,128)(2,1)S(1)}, bf16[1584,256]{1,0:T(8,128)(2,1)S(1)}, u32[]{:S(2)}, u32[]{:S(2)}) collective-permute-start(bf16[1584,256]{1,0:T(8,128)(2,1)S(1)} %pad_maximum_fusion.here), channel_id=1, source_target_pairs={{0,32},{32,64},{64,96},{1,33},{33,65},{65,97},{2,34},{34,66},{66,9... | collective-permute-start | bytes 2433032 | tf_op jit(solution)/shard_map/ppermute | solution.py:263
  5.4 2.7 %collective-permute-start.5 = (bf16[1584,256]{1,0:T(8,128)(2,1)S(1)}, bf16[1584,256]{1,0:T(8,128)(2,1)S(1)}, u32[]{:S(2)}, u32[]{:S(2)}) collective-permute-start(bf16[1584,256]{1,0:T(8,128)(2,1)S(1)} %pad_maximum_fusion.here), channel_id=1, source_target_pairs={{32,0},{64,32},{96,64},{33,1},{65,33},{97,65},{34,2},{66,34},{98,6... | collective-permute-start | bytes 2433032 | tf_op jit(solution)/shard_map/ppermute | solution.py:263
  8.2 0.2 reshape.459
  8.4 0.1 reshape.447
  8.4 0.1 fusion.12
  8.6 0.0 copy-start.4
  8.6 3.1 %gather_fusion = s32[512]{0:T(512)S(1)} fusion(s32[6144]{0:T(1024)S(1)} %copy-done, s32[1024]{0:T(1024)S(1)} %pad_clamp_fusion), kind=kCustom, calls=%fused_computation | custom fusion | bytes 6144 | tf_op jit(solution)/shard_map/jit(_take)/gather | solution.py:287
  11.8 0.1 copy.20
  11.9 0.9 tile.8
  12.8 1.2 copy.22.taper
  14.0 0.2 reshape.460.state
  14.2 0.1 fusion.13.key_row
  14.3 0.7 fusion.7.key_col
  15.0 2.6 %tables.1 = (f32[8,4608]{1,0:T(8,128)S(1)}, f32[16,256]{1,0:T(8,128)S(1)}) custom-call(s32[512,1]{1,0:T(8,128)S(1)} %fusion.7.key_col, s32[1,512]{1,0:T(1,128)S(1)} %fusion.13.key_row, f32[8,64,128]{2,1,0:T(8,128)S(1)} %copy.22.taper, f32[512,1]{1,0:T(8,128)S(1)} %reshape.460.state), custom_call_target="tpu_custom_call" | custom-call | flops 1000000000 | bytes 1000000 | tf_op jit(solution)/shard_map/tables/pallas_call | solution.py:292
  17.6 0.1 collective-permute-start
  17.7 5.4 %collective-permute-start.1 = (f32[16,256]{1,0:T(8,128)S(1)}, f32[16,256]{1,0:T(8,128)S(1)}, u32[]{:S(2)}, u32[]{:S(2)}) collective-permute-start(f32[16,256]{1,0:T(8,128)S(1)} %get-tuple-element.11.table.rows.refs_0_), channel_id=1, source_target_pairs={{1,0},{2,1},{3,2},{4,3},{5,4},{6,5},{7,6},{8,7},{9,8},{10,9},{11,1... | collective-permute-start | bytes 49160 | tf_op jit(solution)/shard_map/ppermute | solution.py:268
  23.1 1.3 %collective-permute-done.table_w.rows_w.refs_3_ = f32[16,256]{1,0:T(8,128)S(1)} collective-permute-done((f32[16,256]{1,0:T(8,128)S(1)}, f32[16,256]{1,0:T(8,128)S(1)}, u32[]{:S(2)}, u32[]{:S(2)}) %collective-permute-start) | collective-permute-done | bytes 16416 | tf_op jit(solution)/shard_map/ppermute | solution.py:268
  24.5 0.1 collective-permute-done.1.table_e.rows_e.refs_4_
  24.6 0.0 collective-permute-done.4.below
  24.6 2.3 %collective-permute-done.5.above = bf16[1584,256]{1,0:T(8,128)(2,1)S(1)} collective-permute-done((bf16[1584,256]{1,0:T(8,128)(2,1)S(1)}, bf16[1584,256]{1,0:T(8,128)(2,1)S(1)}, u32[]{:S(2)}, u32[]{:S(2)}) %collective-permute-start.5) | collective-permute-done | bytes 811040 | tf_op jit(solution)/shard_map/ppermute | solution.py:263
  26.8 1.5 %select.89 = (bf16[1584,256]{1,0:T(8,128)(2,1)S(1)}, bf16[1584,256]{1,0:T(8,128)(2,1)S(1)}) custom-call(bf16[1584,256]{1,0:T(8,128)(2,1)S(1)} %collective-permute-done.4.below, bf16[1584,256]{1,0:T(8,128)(2,1)S(1)} %pad_maximum_fusion.here, bf16[1584,256]{1,0:T(8,128)(2,1)S(1)} %collective-permute-done.5.above, ...), custom_call_target="tpu_custom_call" | custom-call | flops 100000000 | bytes 4000000 | tf_op jit(solution)/shard_map/select/pallas_call | solution.py:313
  28.3 0.1 collective-permute-start.6
  28.4 5.1 %collective-permute-start.7 = (bf16[1584,256]{1,0:T(8,128)(2,1)S(1)}, bf16[1584,256]{1,0:T(8,128)(2,1)S(1)}, u32[]{:S(2)}, u32[]{:S(2)}) collective-permute-start(bf16[1584,256]{1,0:T(8,128)(2,1)S(1)} %get-tuple-element.13), channel_id=1, source_target_pairs={{1,0},{2,1},{3,2},{4,3},{5,4},{6,5},{7,6},{8,7},{9,8},{10,9},{11,1... | collective-permute-start | bytes 2433032 | tf_op jit(solution)/shard_map/ppermute | solution.py:268
  33.4 2.9 %own_gram.1 = (f32[2048,256]{1,0:T(8,128)S(1)}, f32[8,256]{1,0:T(8,128)S(1)}) custom-call(bf16[1584,256]{1,0:T(8,128)(2,1)S(1)} %collective-permute-done.4.below, bf16[1584,256]{1,0:T(8,128)(2,1)S(1)} %pad_maximum_fusion.here, bf16[1584,256]{1,0:T(8,128)(2,1)S(1)} %collective-permute-done.5.above, f32[16,256]{1,0:T(8,128)S(1)} %get-tuple-element.11.table.rows.refs_0_, ...), custom_call_target="tpu_custom_call" | custom-call | flops 1660944384 | bytes 5000000 | tf_op jit(solution)/shard_map/own_gram/pallas_call | solution.py:330
  36.4 7.0 %collective-permute-done.6.west = bf16[1584,256]{1,0:T(8,128)(2,1)S(1)} collective-permute-done((bf16[1584,256]{1,0:T(8,128)(2,1)S(1)}, bf16[1584,256]{1,0:T(8,128)(2,1)S(1)}, u32[]{:S(2)}, u32[]{:S(2)}) %collective-permute-start.6) | collective-permute-done | bytes 811040 | tf_op jit(solution)/shard_map/ppermute | solution.py:268
  43.4 9.5 %mixing.1.refs_5_ = bf16[2048,256]{1,0:T(8,128)(2,1)S(1)} custom-call(bf16[1584,256]{1,0:T(8,128)(2,1)S(1)} %collective-permute-done.6.west, bf16[1584,256]{1,0:T(8,128)(2,1)S(1)} %collective-permute-done.7.east, f32[8,4608]{1,0:T(8,128)S(1)} %get-tuple-element.14.weights, f32[2048,256]{1,0:T(8,128)S(1)} %get-tuple-element.15.gram_in, ...), custom_call_target="tpu_custom_call" | custom-call | flops 6543114240 | bytes 5000000 | tf_op jit(solution)/shard_map/mixing/pallas_call | solution.py:339
  52.9 1.9 %collective-permute-start.8 = (bf16[2048,256]{1,0:T(8,128)(2,1)S(1)}, bf16[2048,256]{1,0:T(8,128)(2,1)S(1)}, u32[]{:S(2)}, u32[]{:S(2)}) collective-permute-start(bf16[2048,256]{1,0:T(8,128)(2,1)S(1)} %mixing.1.refs_5_), channel_id=1, source_target_pairs={{0,32},{32,64},{64,96},{1,33},{33,65},{65,97},{2,34},{34,66},{66,9... | collective-permute-start | bytes 3145736 | tf_op jit(solution)/shard_map/ppermute | solution.py:263
  54.8 3.9 %collective-permute-start.9 = (bf16[2048,256]{1,0:T(8,128)(2,1)S(1)}, bf16[2048,256]{1,0:T(8,128)(2,1)S(1)}, u32[]{:S(2)}, u32[]{:S(2)}) collective-permute-start(bf16[2048,256]{1,0:T(8,128)(2,1)S(1)} %mixing.1.refs_5_), channel_id=1, source_target_pairs={{32,0},{64,32},{96,64},{33,1},{65,33},{97,65},{34,2},{66,34},{98,6... | collective-permute-start | bytes 3145736 | tf_op jit(solution)/shard_map/ppermute | solution.py:263
  58.8 0.1 collective-permute-start.10
  58.8 5.1 %collective-permute-start.11 = (bf16[2048,256]{1,0:T(8,128)(2,1)S(1)}, bf16[2048,256]{1,0:T(8,128)(2,1)S(1)}, u32[]{:S(2)}, u32[]{:S(2)}) collective-permute-start(bf16[2048,256]{1,0:T(8,128)(2,1)S(1)} %mixing.1.refs_5_), channel_id=1, source_target_pairs={{1,0},{2,1},{3,2},{4,3},{5,4},{6,5},{7,6},{8,7},{9,8},{10,9},{11,1... | collective-permute-start | bytes 3145736 | tf_op jit(solution)/shard_map/ppermute | solution.py:268
  63.9 2.8 %collective-permute-start.3 = (f32[48,256]{1,0:T(8,128)S(1)}, f32[48,256]{1,0:T(8,128)S(1)}, u32[]{:S(2)}, u32[]{:S(2)}) collective-permute-start(f32[48,256]{1,0:T(8,128)S(1)} %constant_dynamic-update-slice_fusion), channel_id=1, source_target_pairs={{32,0},{64,32},{96,64},{33,1},{65,33},{97,65},{34,2},{66,34},{98,6... | collective-permute-start | bytes 147464 | tf_op jit(solution)/shard_map/ppermute | solution.py:263
  66.7 15.1 %collective-permute-done.3 = f32[48,256]{1,0:T(8,128)S(1)} collective-permute-done((f32[48,256]{1,0:T(8,128)S(1)}, f32[48,256]{1,0:T(8,128)S(1)}, u32[]{:S(2)}, u32[]{:S(2)}) %collective-permute-start.3) | collective-permute-done | bytes 49184 | tf_op jit(solution)/shard_map/ppermute | solution.py:263
  81.8 1.9 %collective-permute-start.2 = (f32[48,256]{1,0:T(8,128)S(1)}, f32[48,256]{1,0:T(8,128)S(1)}, u32[]{:S(2)}, u32[]{:S(2)}) collective-permute-start(f32[48,256]{1,0:T(8,128)S(1)} %constant_dynamic-update-slice_fusion), channel_id=1, source_target_pairs={{0,32},{32,64},{64,96},{1,33},{33,65},{65,97},{2,34},{34,66},{66,9... | collective-permute-start | bytes 147464 | tf_op jit(solution)/shard_map/ppermute | solution.py:263
  83.7 0.0 collective-permute-done.8.refs_6_
  83.8 0.1 collective-permute-start.12
  83.8 4.0 %collective-permute-done.2 = f32[48,256]{1,0:T(8,128)S(1)} collective-permute-done((f32[48,256]{1,0:T(8,128)S(1)}, f32[48,256]{1,0:T(8,128)S(1)}, u32[]{:S(2)}, u32[]{:S(2)}) %collective-permute-start.2) | collective-permute-done | bytes 49184 | tf_op jit(solution)/shard_map/ppermute | solution.py:263
  87.8 4.4 %collective-permute-start.13 = (bf16[2048,256]{1,0:T(8,128)(2,1)S(1)}, bf16[2048,256]{1,0:T(8,128)(2,1)S(1)}, u32[]{:S(2)}, u32[]{:S(2)}) collective-permute-start(bf16[2048,256]{1,0:T(8,128)(2,1)S(1)} %collective-permute-done.8.refs_6_), channel_id=1, source_target_pairs={{1,0},{2,1},{3,2},{4,3},{5,4},{6,5},{7,6},{8,7},{9,8},{10,9},{11,1... | collective-permute-start | bytes 3145736 | tf_op jit(solution)/shard_map/ppermute | solution.py:268
  92.2 5.1 %collective-permute-start.15 = (bf16[2048,256]{1,0:T(8,128)(2,1)S(1)}, bf16[2048,256]{1,0:T(8,128)(2,1)S(1)}, u32[]{:S(2)}, u32[]{:S(2)}) collective-permute-start(bf16[2048,256]{1,0:T(8,128)(2,1)S(1)} %collective-permute-done.9.refs_7_), channel_id=1, source_target_pairs={{1,0},{2,1},{3,2},{4,3},{5,4},{6,5},{7,6},{8,7},{9,8},{10,9},{11,1... | collective-permute-start | bytes 3145736 | tf_op jit(solution)/shard_map/ppermute | solution.py:268
  97.3 6.3 %increments.1.acc_in = f32[2304,256]{1,0:T(8,128)S(1)} custom-call(bf16[2304,256]{1,0:T(8,128)(2,1)S(1)} %bitcast.6, f32[16,256]{1,0:T(8,128)S(1)} %get-tuple-element.11.table.rows.refs_0_, f32[16,256]{1,0:T(8,128)S(1)} %get-tuple-element.22.refs_1_, f32[16,256]{1,0:T(8,128)S(1)} %get-tuple-element.19.refs_2_, ...), custom_call_target="tpu_custom_call" | custom-call | flops 4026531840 | bytes 9000000 | tf_op jit(solution)/shard_map/increments/pallas_call | solution.py:373
  103.6 0.0 collective-permute-done.12.refs_4_
  103.6 0.9 collective-permute-done.13.refs_5_
  104.5 8.1 %collective-permute-done.14.refs_6_ = bf16[2048,256]{1,0:T(8,128)(2,1)S(1)} collective-permute-done((bf16[2048,256]{1,0:T(8,128)(2,1)S(1)}, bf16[2048,256]{1,0:T(8,128)(2,1)S(1)}, u32[]{:S(2)}, u32[]{:S(2)}) %collective-permute-start.14) | collective-permute-done | bytes 1048608 | tf_op jit(solution)/shard_map/ppermute | solution.py:268
  112.6 3.1 %collective-permute-done.15.refs_7_ = bf16[2048,256]{1,0:T(8,128)(2,1)S(1)} collective-permute-done((bf16[2048,256]{1,0:T(8,128)(2,1)S(1)}, bf16[2048,256]{1,0:T(8,128)(2,1)S(1)}, u32[]{:S(2)}, u32[]{:S(2)}) %collective-permute-start.15) | collective-permute-done | bytes 1048608 | tf_op jit(solution)/shard_map/ppermute | solution.py:268
  115.7 6.4 %finish.1 = bf16[2304,256]{1,0:T(8,128)(2,1)} custom-call(bf16[2304,256]{1,0:T(8,128)(2,1)S(1)} %bitcast.7, f32[2304,256]{1,0:T(8,128)S(1)} %increments.1.acc_in, f32[16,256]{1,0:T(8,128)S(1)} %get-tuple-element.21.refs_0_, f32[16,256]{1,0:T(8,128)S(1)} %get-tuple-element.20.refs_1_, f32[16,256]{1,0:T(8,128)S(1)} %get-tuple-element.18.refs_2_, ...), custom_call_target="tpu_custom_call" | custom-call | flops 3221225472 | bytes 9000000 | tf_op jit(solution)/shard_map/finish/pallas_call | solution.py:383
  (20 shorter events, 0.1 us)
Async XLA Ops:
  0.0 8.6 %copy-start = (s32[6144]{0:T(1024)S(1)}, s32[6144]{0:T(1024)}, u32[]{:S(2)}) copy-start(s32[6144]{0:T(1024)} %param.11) | copy-start | bytes 73732
  0.0 8.1 %copy-start.3 = (s32[8,64]{1,0:T(8,128)S(1)}, s32[8,64]{1,0:T(8,128)}, u32[]{:S(2)}) copy-start(s32[8,64]{1,0:T(8,128)} %param.10) | copy-start | bytes 6148
  2.1 9.8 %copy-start.2 = (f32[8,64,32]{1,2,0:T(8,128)S(1)}, f32[8,64,32]{1,2,0:T(8,128)}, u32[]{:S(2)}) copy-start(f32[8,64,32]{1,2,0:T(8,128)} %param.12) | copy-start | bytes 196612
  2.2 22.4 %collective-permute-start.4 = (bf16[1584,256]{1,0:T(8,128)(2,1)S(1)}, bf16[1584,256]{1,0:T(8,128)(2,1)S(1)}, u32[]{:S(2)}, u32[]{:S(2)}) collective-permute-start(bf16[1584,256]{1,0:T(8,128)(2,1)S(1)} %pad_maximum_fusion.here), channel_id=1, source_target_pairs={{0,32},{32,64},{64,96},{1,33},{33,65},{65,97},{2,34},{34,66},{66,9... | collective-permute-start | bytes 2433032 | tf_op jit(solution)/shard_map/ppermute | solution.py:263
  5.4 21.4 %collective-permute-start.5 = (bf16[1584,256]{1,0:T(8,128)(2,1)S(1)}, bf16[1584,256]{1,0:T(8,128)(2,1)S(1)}, u32[]{:S(2)}, u32[]{:S(2)}) collective-permute-start(bf16[1584,256]{1,0:T(8,128)(2,1)S(1)} %pad_maximum_fusion.here), channel_id=1, source_target_pairs={{32,0},{64,32},{96,64},{33,1},{65,33},{97,65},{34,2},{66,34},{98,6... | collective-permute-start | bytes 2433032 | tf_op jit(solution)/shard_map/ppermute | solution.py:263
  8.6 5.4 %copy-start.4 = (f32[8,64]{1,0:T(8,128)S(1)}, f32[8,64]{1,0:T(8,128)}, u32[]{:S(2)}) copy-start(f32[8,64]{1,0:T(8,128)} %param.13) | copy-start | bytes 6148
  17.6 6.9 %collective-permute-start = (f32[16,256]{1,0:T(8,128)S(1)}, f32[16,256]{1,0:T(8,128)S(1)}, u32[]{:S(2)}, u32[]{:S(2)}) collective-permute-start(f32[16,256]{1,0:T(8,128)S(1)} %get-tuple-element.11.table.rows.refs_0_), channel_id=1, source_target_pairs={{31,0},{0,1},{1,2},{2,3},{3,4},{4,5},{5,6},{6,7},{7,8},{8,9},{9,10... | collective-permute-start | bytes 49160 | tf_op jit(solution)/shard_map/ppermute | solution.py:268
  17.7 6.9 %collective-permute-start.1 = (f32[16,256]{1,0:T(8,128)S(1)}, f32[16,256]{1,0:T(8,128)S(1)}, u32[]{:S(2)}, u32[]{:S(2)}) collective-permute-start(f32[16,256]{1,0:T(8,128)S(1)} %get-tuple-element.11.table.rows.refs_0_), channel_id=1, source_target_pairs={{1,0},{2,1},{3,2},{4,3},{5,4},{6,5},{7,6},{8,7},{9,8},{10,9},{11,1... | collective-permute-start | bytes 49160 | tf_op jit(solution)/shard_map/ppermute | solution.py:268
  28.3 15.1 %collective-permute-start.6 = (bf16[1584,256]{1,0:T(8,128)(2,1)S(1)}, bf16[1584,256]{1,0:T(8,128)(2,1)S(1)}, u32[]{:S(2)}, u32[]{:S(2)}) collective-permute-start(bf16[1584,256]{1,0:T(8,128)(2,1)S(1)} %get-tuple-element.12), channel_id=1, source_target_pairs={{31,0},{0,1},{1,2},{2,3},{3,4},{4,5},{5,6},{6,7},{7,8},{8,9},{9,10... | collective-permute-start | bytes 2433032 | tf_op jit(solution)/shard_map/ppermute | solution.py:268
  28.4 15.0 %collective-permute-start.7 = (bf16[1584,256]{1,0:T(8,128)(2,1)S(1)}, bf16[1584,256]{1,0:T(8,128)(2,1)S(1)}, u32[]{:S(2)}, u32[]{:S(2)}) collective-permute-start(bf16[1584,256]{1,0:T(8,128)(2,1)S(1)} %get-tuple-element.13), channel_id=1, source_target_pairs={{1,0},{2,1},{3,2},{4,3},{5,4},{6,5},{7,6},{8,7},{9,8},{10,9},{11,1... | collective-permute-start | bytes 2433032 | tf_op jit(solution)/shard_map/ppermute | solution.py:268
  43.4 53.9 %copy-start.1 = (bf16[48,48,256]{2,1,0:T(8,128)(2,1)S(1)}, bf16[48,48,256]{2,1,0:T(8,128)(2,1)}, u32[]{:S(2)}) copy-start(bf16[48,48,256]{2,1,0:T(8,128)(2,1)} %param.7) | copy-start | bytes 3538948
  52.9 30.8 %collective-permute-start.8 = (bf16[2048,256]{1,0:T(8,128)(2,1)S(1)}, bf16[2048,256]{1,0:T(8,128)(2,1)S(1)}, u32[]{:S(2)}, u32[]{:S(2)}) collective-permute-start(bf16[2048,256]{1,0:T(8,128)(2,1)S(1)} %mixing.1.refs_5_), channel_id=1, source_target_pairs={{0,32},{32,64},{64,96},{1,33},{33,65},{65,97},{2,34},{34,66},{66,9... | collective-permute-start | bytes 3145736 | tf_op jit(solution)/shard_map/ppermute | solution.py:263
  54.8 37.3 %collective-permute-start.9 = (bf16[2048,256]{1,0:T(8,128)(2,1)S(1)}, bf16[2048,256]{1,0:T(8,128)(2,1)S(1)}, u32[]{:S(2)}, u32[]{:S(2)}) collective-permute-start(bf16[2048,256]{1,0:T(8,128)(2,1)S(1)} %mixing.1.refs_5_), channel_id=1, source_target_pairs={{32,0},{64,32},{96,64},{33,1},{65,33},{97,65},{34,2},{66,34},{98,6... | collective-permute-start | bytes 3145736 | tf_op jit(solution)/shard_map/ppermute | solution.py:263
  58.8 33.4 %collective-permute-start.10 = (bf16[2048,256]{1,0:T(8,128)(2,1)S(1)}, bf16[2048,256]{1,0:T(8,128)(2,1)S(1)}, u32[]{:S(2)}, u32[]{:S(2)}) collective-permute-start(bf16[2048,256]{1,0:T(8,128)(2,1)S(1)} %mixing.1.refs_5_), channel_id=1, source_target_pairs={{31,0},{0,1},{1,2},{2,3},{3,4},{4,5},{5,6},{6,7},{7,8},{8,9},{9,10... | collective-permute-start | bytes 3145736 | tf_op jit(solution)/shard_map/ppermute | solution.py:268
  58.8 38.4 %collective-permute-start.11 = (bf16[2048,256]{1,0:T(8,128)(2,1)S(1)}, bf16[2048,256]{1,0:T(8,128)(2,1)S(1)}, u32[]{:S(2)}, u32[]{:S(2)}) collective-permute-start(bf16[2048,256]{1,0:T(8,128)(2,1)S(1)} %mixing.1.refs_5_), channel_id=1, source_target_pairs={{1,0},{2,1},{3,2},{4,3},{5,4},{6,5},{7,6},{8,7},{9,8},{10,9},{11,1... | collective-permute-start | bytes 3145736 | tf_op jit(solution)/shard_map/ppermute | solution.py:268
  63.9 17.9 %collective-permute-start.3 = (f32[48,256]{1,0:T(8,128)S(1)}, f32[48,256]{1,0:T(8,128)S(1)}, u32[]{:S(2)}, u32[]{:S(2)}) collective-permute-start(f32[48,256]{1,0:T(8,128)S(1)} %constant_dynamic-update-slice_fusion), channel_id=1, source_target_pairs={{32,0},{64,32},{96,64},{33,1},{65,33},{97,65},{34,2},{66,34},{98,6... | collective-permute-start | bytes 147464 | tf_op jit(solution)/shard_map/ppermute | solution.py:263
  81.8 6.0 %collective-permute-start.2 = (f32[48,256]{1,0:T(8,128)S(1)}, f32[48,256]{1,0:T(8,128)S(1)}, u32[]{:S(2)}, u32[]{:S(2)}) collective-permute-start(f32[48,256]{1,0:T(8,128)S(1)} %constant_dynamic-update-slice_fusion), channel_id=1, source_target_pairs={{0,32},{32,64},{64,96},{1,33},{33,65},{65,97},{2,34},{34,66},{66,9... | collective-permute-start | bytes 147464 | tf_op jit(solution)/shard_map/ppermute | solution.py:263
  83.8 19.9 %collective-permute-start.12 = (bf16[2048,256]{1,0:T(8,128)(2,1)S(1)}, bf16[2048,256]{1,0:T(8,128)(2,1)S(1)}, u32[]{:S(2)}, u32[]{:S(2)}) collective-permute-start(bf16[2048,256]{1,0:T(8,128)(2,1)S(1)} %collective-permute-done.8.refs_6_), channel_id=1, source_target_pairs={{31,0},{0,1},{1,2},{2,3},{3,4},{4,5},{5,6},{6,7},{7,8},{8,9},{9,10... | collective-permute-start | bytes 3145736 | tf_op jit(solution)/shard_map/ppermute | solution.py:268
  87.8 16.7 %collective-permute-start.13 = (bf16[2048,256]{1,0:T(8,128)(2,1)S(1)}, bf16[2048,256]{1,0:T(8,128)(2,1)S(1)}, u32[]{:S(2)}, u32[]{:S(2)}) collective-permute-start(bf16[2048,256]{1,0:T(8,128)(2,1)S(1)} %collective-permute-done.8.refs_6_), channel_id=1, source_target_pairs={{1,0},{2,1},{3,2},{4,3},{5,4},{6,5},{7,6},{8,7},{9,8},{10,9},{11,1... | collective-permute-start | bytes 3145736 | tf_op jit(solution)/shard_map/ppermute | solution.py:268
  92.2 20.4 %collective-permute-start.14 = (bf16[2048,256]{1,0:T(8,128)(2,1)S(1)}, bf16[2048,256]{1,0:T(8,128)(2,1)S(1)}, u32[]{:S(2)}, u32[]{:S(2)}) collective-permute-start(bf16[2048,256]{1,0:T(8,128)(2,1)S(1)} %collective-permute-done.9.refs_7_), channel_id=1, source_target_pairs={{31,0},{0,1},{1,2},{2,3},{3,4},{4,5},{5,6},{6,7},{7,8},{8,9},{9,10... | collective-permute-start | bytes 3145736 | tf_op jit(solution)/shard_map/ppermute | solution.py:268
  92.2 23.5 %collective-permute-start.15 = (bf16[2048,256]{1,0:T(8,128)(2,1)S(1)}, bf16[2048,256]{1,0:T(8,128)(2,1)S(1)}, u32[]{:S(2)}, u32[]{:S(2)}) collective-permute-start(bf16[2048,256]{1,0:T(8,128)(2,1)S(1)} %collective-permute-done.9.refs_7_), channel_id=1, source_target_pairs={{1,0},{2,1},{3,2},{4,3},{5,4},{6,5},{7,6},{8,7},{9,8},{10,9},{11,1... | collective-permute-start | bytes 3145736 | tf_op jit(solution)/shard_map/ppermute | solution.py:268

commit v2 on v1

v2 whole, which is shorter than its diff:
```python
import functools

import jax
import jax.numpy as jnp
from jax import lax
from jax.experimental import pallas as pl
from jax.experimental.pallas import tpu as pltpu
from jax.sharding import PartitionSpec as P

NS_ITERS = 5
CAP = 16
CLASSES = 9
BAND_SLOTS = 3 * CAP
CLASS_STRIDE = 64
KEYS = 640
META_LANES = 256

F32 = jnp.float32
BF16 = jnp.bfloat16
VMEM_SPEC = pl.BlockSpec(memory_space=pltpu.VMEM)
SMEM_SPEC = pl.BlockSpec(memory_space=pltpu.SMEM)


def dot(a, b):
    return jnp.dot(a, b, preferred_element_type=F32)


def call(kernel, outs, in_specs, name, flops, bytes_accessed, scratch=(), aliases=None):
    return pl.pallas_call(
        kernel,
        out_shape=outs,
        in_specs=in_specs,
        out_specs=jax.tree.map(lambda _: VMEM_SPEC, outs),
        scratch_shapes=list(scratch),
        input_output_aliases=aliases or {},
        compiler_params=pltpu.CompilerParams(vmem_limit_bytes=40 * 1024 * 1024),
        cost_estimate=pl.CostEstimate(
            flops=flops, bytes_accessed=bytes_accessed, transcendentals=0
        ),
        name=name,
    )


def table_kernel(shape, lists, placement, state, innov, obs, meta, entry_slot, obs_copy):
    lon_count, blocks = shape
    regions, list_len = lists.shape
    entries = regions * list_len
    obs_rows = innov.shape[1]
    obs_copy[...] = obs[...]
    p = lax.broadcasted_iota(jnp.int32, (obs_rows, META_LANES), 0)
    q = lax.broadcasted_iota(jnp.int32, (obs_rows, META_LANES), 1) % obs_rows
    meta[16:, :] = dot(innov[...], jnp.where(p == q, 1.0, 0.0).astype(BF16))

    def columns(x):
        t = x.T
        return jnp.concatenate(
            [jnp.broadcast_to(t[:, r : r + 1], (list_len, 128)) for r in range(regions)], axis=0
        )

    lane = lax.broadcasted_iota(jnp.int32, (1, 128), 1).astype(F32)
    ones = jnp.ones((128, 128), BF16)
    ids = columns(lists[...].astype(F32))
    line = jnp.floor(ids * (1.0 / 128.0))
    table_rows = placement.shape[0]
    line_hot = jnp.where(line == lane, 1.0, 0.0).astype(BF16)[:, :table_rows]
    at = lane == ids - 128.0 * line
    places = placement[...].astype(F32)
    high = jnp.floor(places * (1.0 / 64.0))

    def look(part):
        found = dot(line_hot, part.astype(BF16))
        return dot(jnp.where(at, found, 0.0).astype(BF16), ones)

    row = 64.0 * look(high) + look(places - 64.0 * high)
    holder = jnp.floor((row + 0.5) * (1.0 / blocks))
    inside = row - blocks * holder
    holder_band = jnp.floor((holder + 0.5) * (1.0 / lon_count))
    band_step = holder_band - lax.axis_index("band").astype(F32)
    lon_step = holder - lon_count * holder_band - lax.axis_index("lon").astype(F32) + 1.0
    lon_step = jnp.where(lon_step < 0.0, lon_step + lon_count, lon_step)
    lon_step = jnp.where(lon_step >= lon_count, lon_step - lon_count, lon_step)
    key = (lon_step * 3.0 + band_step + 1.0) * CLASS_STRIDE + inside

    hot = jnp.concatenate(
        [jnp.where(key == lane + 128.0 * c, 1.0, 0.0) for c in range(KEYS // 128)], axis=1
    ).astype(BF16)
    counts = lax.dot_general(
        hot,
        jnp.ones((entries, 128), BF16),
        (((0,), (0,)), ((), ())),
        preferred_element_type=F32,
    )
    present = jnp.minimum(counts, 1.0)
    down = lax.broadcasted_iota(jnp.int32, (KEYS, KEYS), 0)
    across = lax.broadcasted_iota(jnp.int32, (KEYS, KEYS), 1)
    before = (across < down) & (across // CLASS_STRIDE == down // CLASS_STRIDE)
    rank = dot(jnp.where(before, 1.0, 0.0).astype(BF16), present.astype(BF16))
    key_id = lax.broadcasted_iota(jnp.int32, (KEYS, 128), 0)
    slot = rank + (CAP * (key_id // CLASS_STRIDE)).astype(F32)
    block = (key_id % CLASS_STRIDE).astype(F32)
    slots = dot(hot, slot.astype(BF16))
    entry_slot[...] = slots
    meta[0:16, :] = jnp.zeros((16, META_LANES), F32)
    tapers = columns(state[...])
    for c in range(2):
        match = (slot == lane + 128.0 * c) & (present > 0.0)
        rows = jnp.sum(jnp.where(match, block, 0.0), axis=0, keepdims=True)
        meta[8:9, 128 * c : 128 * (c + 1)] = rows
        hit = jnp.where(slots == lane + 128.0 * c, tapers, 0.0)
        for r in range(regions):
            meta[r : r + 1, 128 * c : 128 * (c + 1)] = jnp.sum(
                hit[r * list_len : (r + 1) * list_len], axis=0, keepdims=True
            )


def weight_kernel(regions, list_len, entry_slot, taper, weights):
    obs_rows = taper.shape[1]
    group = (lax.broadcasted_iota(jnp.int32, (1, 128), 1) // obs_rows).astype(F32)
    p = lax.broadcasted_iota(jnp.int32, (obs_rows, 128), 0)
    q = lax.broadcasted_iota(jnp.int32, (obs_rows, 128), 1) % obs_rows
    spread = jnp.where(p == q, 1.0, 0.0).astype(BF16)

    def across(x):
        return lax.dot_general(
            x, spread, (((0,), (0,)), ((), ())), preferred_element_type=F32
        )

    for r in range(regions):
        mine = entry_slot[r * list_len : (r + 1) * list_len, :]
        high = taper[r].astype(BF16)
        low = (taper[r] - high.astype(F32)).astype(BF16)
        w = across(high) + across(low)
        for c in range(CLASSES * CAP // 4):
            hit = mine == group + 4.0 * c
            weights[r : r + 1, 128 * c : 128 * (c + 1)] = jnp.sum(
                jnp.where(hit, w, 0.0), axis=0, keepdims=True
            )


def gather_blocks(sources, table, first_slot, obs_rows, out):
    for band in range(3):
        for i in range(CAP):
            slot = first_slot + CAP * band + i
            at = pl.multiple_of(table[8, slot].astype(jnp.int32) * obs_rows, obs_rows)
            to = (CAP * band + i) * obs_rows
            out[to : to + obs_rows, :] = sources[band][pl.ds(at, obs_rows), :]


def select_kernel(obs_rows, below, here, above, table_w, table_e, to_w, to_e):
    sources = (below, here, above)
    gather_blocks(sources, table_w, 2 * BAND_SLOTS, obs_rows, to_w)
    gather_blocks(sources, table_e, 0, obs_rows, to_e)


def transposed(y):
    return jnp.concatenate(
        [y[256 * c : 256 * (c + 1)].astype(F32).T.astype(BF16) for c in range(y.shape[0] // 256)],
        axis=1,
    )


def own_gram_kernel(obs_rows, regions, below, here, above, table, weights, gram, pool):
    gather_blocks((below, here, above), table, BAND_SLOTS, obs_rows, pool)
    y = pool[...]
    y_t = transposed(y)
    first = BAND_SLOTS * obs_rows
    w16 = weights[:, first : 2 * first].astype(BF16)
    for r in range(regions):
        gram[256 * r : 256 * (r + 1), :] = dot(y_t * w16[r : r + 1, :], y)


def innov_kernel(obs_rows, regions, meta, below, here, above, weights, pool, scaled, proj):
    blocks = here.shape[0] // 3 - 16
    down = lax.broadcasted_iota(jnp.int32, (blocks, META_LANES), 0).astype(F32)
    hot = jnp.where(down == meta[8:9, :], 1.0, 0.0).T.astype(BF16)
    per = META_LANES // obs_rows
    sub = lax.broadcasted_iota(jnp.int32, (per, META_LANES), 0)
    which = lax.broadcasted_iota(jnp.int32, (per, META_LANES), 1) // obs_rows
    pieces = []
    for n in range(CLASSES):
        source = (below, here, above)[n % 3]
        base = (16 + blocks) * (n // 3) + 16
        innov = source[base : base + blocks, :].astype(BF16)
        picked = dot(hot[CAP * n : CAP * (n + 1)], innov)
        for c in range(CAP // per):
            part = jnp.where(sub == which, picked[per * c : per * (c + 1)], 0.0)
            pieces.append(jnp.sum(part, axis=0, keepdims=True))
    wd = weights[...] * jnp.concatenate(pieces, axis=1)
    high = wd.astype(BF16)
    both = jnp.concatenate([high.astype(F32), wd - high.astype(F32)], axis=0).astype(BF16)
    scaled[...] = both
    first = BAND_SLOTS * obs_rows
    part = dot(both[:, first : 2 * first], pool[...])
    proj[...] = part[:regions] + part[regions:]


def total(x):
    return jnp.sum(jnp.sum(x, axis=0, keepdims=True), axis=1, keepdims=True)


def roots(grams, proj_rows, eye, ensemble):
    count = len(grams)
    base = ensemble - 1.0
    each = range(count)
    absolute = [jnp.abs(grams[i] + base * eye) for i in each]
    scale = [
        jnp.max(jnp.sum(absolute[i], axis=0, keepdims=True), axis=1, keepdims=True) for i in each
    ]
    mean = [total(grams[i] * eye) / ensemble for i in each]
    f = [(mean[i] * eye - grams[i]) / scale[i] for i in each]
    c = [1.0 - (base + mean[i]) / scale[i] for i in each]
    a = [1.0 + 0.5 * c[i] for i in each]
    g = [0.5 * f[i] for i in each]
    for step in range(NS_ITERS - 1):
        fb = [f[i].astype(BF16) for i in each]
        f2 = [dot(fb[i], fb[i]) for i in each]
        f3 = [dot(f2[i].astype(BF16), fb[i]) for i in each]
        f = [
            (1.5 * c[i] + 0.75 * c[i] * c[i]) * f[i]
            + (0.75 + 0.75 * c[i]) * f2[i]
            + 0.25 * f3[i]
            for i in each
        ]
        c = [(0.75 + 0.25 * c[i]) * c[i] * c[i] for i in each]
        fg = [dot(f[i].astype(BF16), g[i].astype(BF16)) for i in each]
        g = [
            (1.0 + 0.5 * c[i]) * g[i] + (0.5 * a[i]) * f[i] + 0.5 * fg[i] for i in each
        ]
        a = [a[i] * (1.0 + 0.5 * c[i]) for i in each]
    gb = [g[i].astype(BF16) for i in each]
    first = lax.broadcasted_iota(jnp.int32, (16, ensemble), 0) < 8

    def times(i, v):
        high = v.astype(BF16).astype(F32)
        stacked = jnp.where(first, high, v - high).astype(BF16)
        q = dot(stacked, gb[i])
        return a[i] * v + q[0:1] + q[8:9]

    half = [times(i, proj_rows[i]) for i in each]
    wbar = [times(i, half[i]) / scale[i] for i in each]
    return [
        lax.sqrt(base / scale[i]) * (a[i] * eye + g[i]) - eye for i in each
    ], wbar


def pack(symmetric, wbar, corner_eye, upper):
    quarter = symmetric[128:, 128:]
    merged = jnp.where(upper, symmetric[:128, :128], quarter)
    diagonal = jnp.sum(quarter * corner_eye, axis=0, keepdims=True)
    high = wbar.astype(BF16).astype(F32)
    low = wbar - high
    rows = [diagonal, high[:, :128], high[:, 128:], low[:, :128], low[:, 128:]]
    down = lax.broadcasted_iota(jnp.int32, (16, 128), 0)
    extra = jnp.zeros((16, 128), F32)
    for k, r in enumerate(rows):
        extra = jnp.where(down == k, r, extra)
    return symmetric[:128, 128:].astype(BF16), merged.astype(BF16), extra.astype(BF16)


def mix_regions(first, count, gram, proj, packed):
    n = 256
    extras = n * proj.shape[0]
    down = lax.broadcasted_iota(jnp.int32, (n, n), 0)
    across = lax.broadcasted_iota(jnp.int32, (n, n), 1)
    eye = jnp.where(down == across, 1.0, 0.0)
    upper = (down <= across)[:128, :128]
    some = range(first, first + count)
    matrices, weights = roots(
        [gram[r - first] for r in some], [proj[r : r + 1, :] for r in some], eye, n
    )
    for k, r in enumerate(some):
        right, merged, extra = pack(matrices[k], weights[k], eye[:128, :128], upper)
        packed[n * r : n * r + 128, :] = right
        packed[n * r + 128 : n * (r + 1), :] = merged
        packed[extras + 16 * r : extras + 16 * (r + 1), :] = extra


def grams_of(first, count, gram_own, weights, parts):
    out = []
    for r in range(first, first + count):
        total_r = gram_own[256 * r : 256 * (r + 1), :]
        for y, y_t, lane in parts:
            w16 = weights[r : r + 1, lane : lane + y.shape[0]].astype(BF16)
            total_r = total_r + dot(y_t * w16, y)
        out.append(total_r)
    return out


def mix_kernel(together, west, east, weights, gram_own, scaled, proj_own, packed, proj):
    regions = proj.shape[0]
    size = west.shape[0]
    part = dot(scaled[:, :size], west[...]) + dot(scaled[:, 2 * size :], east[...])
    proj[...] = proj_own[...] + part[:regions] + part[regions:]
    parts = [
        (west[...], transposed(west[...]), 0),
        (east[...], transposed(east[...]), 2 * size),
    ]
    for first in range(0, regions, together):
        grams = grams_of(first, together, gram_own, weights, parts)
        mix_regions(first, together, grams, proj, packed)


def unpack(count, packed, full):
    n = 256
    down = lax.broadcasted_iota(jnp.int32, (128, 128), 0)
    across = lax.broadcasted_iota(jnp.int32, (128, 128), 1)
    upper = down <= across
    lower = down > across
    extra = packed[n * count : (n + 16) * count, :].astype(F32)
    missing = 128 - 16 * count
    if missing:
        padded = jnp.concatenate([extra, jnp.zeros((missing, 128), F32)], axis=0)
    else:
        padded = extra
    columns = padded.T
    for k in range(count):
        right = packed[n * k : n * k + 128, :].astype(F32)
        merged = packed[n * k + 128 : n * (k + 1), :].astype(F32)
        turned = merged.T
        top = columns[:, 16 * k + 1 : 16 * k + 2] + columns[:, 16 * k + 3 : 16 * k + 4]
        low = columns[:, 16 * k + 2 : 16 * k + 3] + columns[:, 16 * k + 4 : 16 * k + 5]
        diagonal = extra[16 * k : 16 * k + 1]
        corner = jnp.where(lower, merged, jnp.where(down == across, diagonal, turned))
        full[n * k : n * k + 128, :128] = (jnp.where(upper, merged, turned) + top).astype(BF16)
        full[n * k : n * k + 128, 128:] = (right + top).astype(BF16)
        full[n * k + 128 : n * (k + 1), :128] = (right.T + low).astype(BF16)
        full[n * k + 128 : n * (k + 1), 128:] = (corner + low).astype(BF16)


def add_increment(members, table, first_slot, packed, count, acc, left, full, state_rows):
    n = members.shape[1]
    unpack(count, packed, full)
    places = [
        pl.multiple_of(table[8, first_slot + i].astype(jnp.int32) * state_rows, state_rows)
        for i in range(CAP)
    ]
    for i in range(CAP):
        x = members[pl.ds(places[i], state_rows), :]
        for k in range(count):
            t = jnp.full((16, 128), table[k, first_slot + i], F32).astype(BF16)
            for u in range(state_rows // 16):
                for v in range(n // 128):
                    left[
                        state_rows * i + 16 * u : state_rows * i + 16 * (u + 1),
                        n * k + 128 * v : n * k + 128 * (v + 1),
                    ] = x[16 * u : 16 * (u + 1), 128 * v : 128 * (v + 1)] * t
    product = dot(left[...], full[...])
    for i in range(CAP):
        acc[pl.ds(places[i], state_rows), :] += product[state_rows * i : state_rows * (i + 1), :]


def increment_kernel(slots, start, finish, state_rows, count, *refs):
    refs = list(refs)
    members = refs.pop(0)
    before = None if start else refs.pop(0)
    items = len(slots)
    tables, packed, refs = refs[:items], refs[items : 2 * items], refs[2 * items :]
    if finish:
        out, acc = refs[:2]
        scratch = refs[2:]
    else:
        acc = refs[0]
        scratch = refs[1:]
    acc[...] = members[...].astype(F32) if start else before[...]
    for k, slot in enumerate(slots):
        left, full = scratch[2 * (k % 2) : 2 * (k % 2) + 2]
        add_increment(members, tables[k], slot, packed[k], count, acc, left, full, state_rows)
    if finish:
        out[...] = acc[...].astype(BF16)


def from_band(x, step):
    devices = range(lax.axis_size("band"))
    return lax.ppermute(x, "band", [(i + step, i) for i in devices if i + step in devices])


def from_lon(x, step):
    count = lax.axis_size("lon")
    return lax.ppermute(x, "lon", [((i + step) % count, i) for i in range(count)])


def local(members, obs_perts, innovations, lists, placement, obs_taper, state_taper):
    lon_count = lax.axis_size("lon")
    blocks, state_rows, n = members.shape
    obs_rows = obs_perts.shape[1]
    regions, list_len = lists.shape
    entries = regions * list_len

    obs = obs_perts.reshape(blocks * obs_rows, n)
    below = from_band(obs, -1)
    above = from_band(obs, 1)

    size = BAND_SLOTS * obs_rows
    pool_shape = jax.ShapeDtypeStruct((size, n), BF16)
    meta, entry_slot, obs = call(
        functools.partial(table_kernel, (lon_count, blocks)),
        (
            jax.ShapeDtypeStruct((16 + blocks, META_LANES), F32),
            jax.ShapeDtypeStruct((entries, 128), F32),
            pool_shape,
        ),
        [VMEM_SPEC] * 5,
        "tables",
        10**9,
        10**6,
    )(lists, placement.reshape(-1, 128), state_taper, innovations, obs)
    meta_w = from_lon(meta, -1)
    meta_e = from_lon(meta, 1)
    weights = call(
        functools.partial(weight_kernel, regions, list_len),
        jax.ShapeDtypeStruct((regions, CLASSES * CAP * obs_rows), F32),
        [VMEM_SPEC] * 2,
        "weights",
        10**9,
        10**6,
    )(entry_slot, jnp.swapaxes(obs_taper, 1, 2))
    below, above, weights = lax.optimization_barrier((below, above, weights))

    to_w, to_e = call(
        functools.partial(select_kernel, obs_rows),
        (pool_shape, pool_shape),
        [VMEM_SPEC] * 3 + [SMEM_SPEC] * 2,
        "select",
        10**8,
        4 * 10**6,
    )(below, obs, above, meta_w, meta_e)
    west = from_lon(to_e, -1)
    east = from_lon(to_w, 1)
    metas = jnp.concatenate([meta_w, meta, meta_e], axis=0)
    metas_below = from_band(metas, -1)
    metas_above = from_band(metas, 1)

    region_flops = 2 * n**3
    gram_own, pool = call(
        functools.partial(own_gram_kernel, obs_rows, regions),
        (jax.ShapeDtypeStruct((regions * n, n), F32), pool_shape),
        [VMEM_SPEC] * 3 + [SMEM_SPEC] + [VMEM_SPEC],
        "own_gram",
        regions * 6 * region_flops,
        5 * 10**6,
    )(below, obs, above, meta, weights)
    proj_shape = jax.ShapeDtypeStruct((regions, n), F32)
    scaled, proj_own = call(
        functools.partial(innov_kernel, obs_rows, regions),
        (jax.ShapeDtypeStruct((2 * regions, 3 * size), BF16), proj_shape),
        [VMEM_SPEC] * 6,
        "innov",
        10**8,
        2 * 10**6,
    )(meta, metas_below, metas, metas_above, weights, pool)
    mix = call(
        functools.partial(mix_kernel, 4),
        jax.ShapeDtypeStruct((regions * (n + 16), 128), BF16),
        [VMEM_SPEC] * 6,
        "mixing",
        regions * 24 * region_flops,
        4 * 10**6,
        [pltpu.VMEM(proj_shape.shape, F32)],
    )(west, east, weights, gram_own, scaled, proj_own)

    arrived = {}
    for band, packed in ((0, mix), (-1, from_band(mix, -1)), (1, from_band(mix, 1))):
        arrived[0, band] = packed
        for lon in (-1, 1):
            arrived[lon, band] = from_lon(packed, lon)

    stacked = {-1: metas_below, 0: metas, 1: metas_above}
    rows = 16 + blocks

    def table(lon, band):
        return stacked[band][rows * (lon + 1) : rows * (lon + 1) + 16]

    def slots(lon, band):
        return CAP * (CLASSES - 1 - ((lon + 1) * 3 + band + 1))

    flat = members.reshape(blocks * state_rows, n)
    acc_shape = jax.ShapeDtypeStruct((blocks * state_rows, n), F32)
    scratch = [
        pltpu.VMEM((CAP * state_rows, regions * n), BF16),
        pltpu.VMEM((regions * n, n), BF16),
    ] * 2

    def increments(acc, groups, finish, name):
        start = acc is None
        kernel = functools.partial(
            increment_kernel, [slots(*g) for g in groups], start, finish, state_rows, regions
        )
        return call(
            kernel,
            jax.ShapeDtypeStruct(acc_shape.shape, BF16) if finish else acc_shape,
            [VMEM_SPEC] * (1 if start else 2)
            + [SMEM_SPEC] * len(groups)
            + [VMEM_SPEC] * len(groups),
            name,
            len(groups) * 3 * regions * region_flops,
            6 * 10**6,
            ([pltpu.VMEM(acc_shape.shape, F32)] if finish else []) + scratch,
        )(
            *([flat] if start else [flat, acc]),
            *[table(*g) for g in groups],
            *[arrived[g] for g in groups],
        )

    acc = increments(None, [(0, 0), (0, -1), (0, 1), (-1, 0), (1, 0)], False, "inner")
    acc = increments(acc, [(-1, -1), (1, -1)], False, "outer")
    acc = increments(acc, [(-1, 1), (1, 1)], True, "finish")
    return acc.reshape(members.shape)


def solution(mesh):
    in_specs = (
        P(("band", "lon"), None, None),
        P(("band", "lon"), None, None),
        P(("band", "lon"), None),
        P(("band", "lon"), None),
        P(),
        P(("band", "lon"), None, None),
        P(("band", "lon"), None),
    )
    out_specs = P(("band", "lon"), None, None)
    return jax.shard_map(local, mesh=mesh, in_specs=in_specs, out_specs=out_specs, check_vma=False)
```

time: 124 us -> 96 us (0.77)
  waiting for transfers between devices: 41.9 us -> 8.85 us
  Pallas kernels: 29.2 us -> 37.6 us
  local copies, waits for them, and re-layouts: 6.81 us -> 4.07 us
  other arithmetic: 2.11 us -> 0 us
  starting transfers between devices: 41.8 us -> 43.7 us
    ppermute x10, waiting for transfers between devices: 20.6 us -> 0.03 us  [from_lon(): lax.ppermute(x, 'lon', [((i + step) % count, i) for i in range(count)])]
    ppermute x6, waiting for transfers between devices: 21.4 us -> 8.82 us  [from_band(): lax.ppermute(x, 'band', [(i + step, i) for i in devices if i + step in de...]
    pallas_call x6 -> x9, Pallas kernels: 29.2 us -> 37.6 us  [the longest x3 17.1 us: increments(): call(kernel, jax.ShapeDtypeStruct(acc_shape.shape, BF16) if finish else a...]
    gather x2 -> x0, local copies, waits for them, and re-layouts: 3.29 us -> none  [local(): row_ids = jnp.take(placement, lists.reshape(-1), axis=0)]
    unnamed x13 -> x15, local copies, waits for them, and re-layouts: 0.83 us -> 4.05 us
    another operation x4 -> x0, local copies, waits for them, and re-layouts: 2.21 us -> none  [the longest x2 2.07 us: local(): jnp.tile(obs_taper, (1, 1, 128 // obs_rows))]
  transfers between devices with their start and end apart: 16 -> 16, of which waited for: 9 -> 3; matrix products, arithmetic and copies ran while one was open for 6% -> 1% of each run, Pallas kernels for 10% -> 21%
where the time goes in v2:
time: 96 us; the launch traced here: 94.5 us
  starting transfers between devices  43.7 us (46%)
  Pallas kernels  37.6 us (39%)
  waiting for transfers between devices  8.85 us (9%)
  local copies, waits for them, and re-layouts  4.07 us (4%)
    ppermute x10, starting transfers between devices, from_lon(): lax.ppermute(x, 'lon', [((i + step) % count, i) for i in range(count)])  26 us
    ppermute x6, starting transfers between devices, from_band(): lax.ppermute(x, 'band', [(i + step, i) for i in devices if i + step in de...  17.7 us
    pallas_call x3, Pallas kernels, increments(): call(kernel, jax.ShapeDtypeStruct(acc_shape.shape, BF16) if finish else a...  17.1 us
    pallas_call x1, Pallas kernels, local(): call(functools.partial(mix_kernel, 4), jax.ShapeDtypeStruct((regions * (n...  9.65 us
    ppermute x6, waiting for transfers between devices, from_band(): lax.ppermute(x, 'band', [(i + step, i) for i in devices if i + step in de...  8.82 us
    unnamed x15, local copies, waits for them, and re-layouts  4.05 us
    pallas_call x1, Pallas kernels, local(): call(functools.partial(own_gram_kernel, obs_rows, regions), (jax.ShapeDty...  3.46 us
    pallas_call x1, Pallas kernels, local(): call(functools.partial(select_kernel, obs_rows), (pool_shape, pool_shape)...  2.89 us
  transfers between devices with their start and end apart: 16, of which 3 were waited for; matrix products, arithmetic and copies ran while one was open for 1% of the time, Pallas kernels for 21%

profile of v2, /device:TPU:4, one launch (start us, length us, event | category | flops | bytes accessed | tf_op | source)
XLA Modules:
  0.0 94.5 jit_solution(9797577186186712581)
XLA Ops:
  0.0 3.1 %collective-permute-start.4 = (bf16[1536,256]{1,0:T(8,128)(2,1)}, bf16[1536,256]{1,0:T(8,128)(2,1)S(1)}, u32[]{:S(2)}, u32[]{:S(2)}) collective-permute-start(bf16[1536,256]{1,0:T(8,128)(2,1)} %bitcast.8), channel_id=1, source_target_pairs={{0,32},{32,64},{64,96},{1,33},{33,65},{65,97},{2,34},{34,66},{66,9... | collective-permute-start | bytes 2359304 | tf_op jit(solution)/shard_map/ppermute | solution.py:374
  3.1 2.7 %collective-permute-start.5 = (bf16[1536,256]{1,0:T(8,128)(2,1)}, bf16[1536,256]{1,0:T(8,128)(2,1)S(1)}, u32[]{:S(2)}, u32[]{:S(2)}) collective-permute-start(bf16[1536,256]{1,0:T(8,128)(2,1)} %bitcast.9), channel_id=1, source_target_pairs={{32,0},{64,32},{96,64},{33,1},{65,33},{97,65},{34,2},{66,34},{98,6... | collective-permute-start | bytes 2359304 | tf_op jit(solution)/shard_map/ppermute | solution.py:374
  5.9 0.8 copy.8.innov
  6.6 1.1 %copy-done.1 = bf16[48,32,256]{2,1,0:T(8,128)(2,1)S(1)} copy-done((bf16[48,32,256]{2,1,0:T(8,128)(2,1)S(1)}, bf16[48,32,256]{2,1,0:T(8,128)(2,1)}, u32[]{:S(2)}) %copy-start.1) | copy-done | bytes 786456
  7.8 0.7 copy-done.3
  8.5 0.7 copy-done.4
  9.2 0.7 copy-done.5
  9.9 2.1 %tables.1 = (f32[64,256]{1,0:T(8,128)S(1)}, f32[512,128]{1,0:T(8,128)S(1)}, bf16[1536,256]{1,0:T(8,128)(2,1)S(1)}) custom-call(s32[8,64]{1,0:T(8,128)S(1)} %copy-done.4, s32[48,128]{1,0:T(8,128)S(1)} %bitcast.12, f32[8,64]{1,0:T(8,128)S(1)} %copy-done.5, bf16[48,32]{1,0:T(8,128)(2,1)S(1)} %copy.8.innov, bf16[1536,256]{1,0:T(8,128)(2,1)S(1)} %bitcast.10), custom_call_target="tpu_custom_call" | custom-call | flops 1000000000 | bytes 1000000 | tf_op jit(solution)/shard_map/tables/pallas_call | solution.py:395
  12.0 0.1 collective-permute-start
  12.1 5.4 %collective-permute-start.1 = (f32[64,256]{1,0:T(8,128)S(1)}, f32[64,256]{1,0:T(8,128)S(1)}, u32[]{:S(2)}, u32[]{:S(2)}) collective-permute-start(f32[64,256]{1,0:T(8,128)S(1)} %get-tuple-element.17.table.meta), channel_id=1, source_target_pairs={{1,0},{2,1},{3,2},{4,3},{5,4},{6,5},{7,6},{8,7},{9,8},{10,9},{11,1... | collective-permute-start | bytes 196616 | tf_op jit(solution)/shard_map/ppermute | solution.py:379
  17.5 0.0 copy-done.2
  17.5 2.0 %weights.1 = f32[8,4608]{1,0:T(8,128)S(1)} custom-call(f32[512,128]{1,0:T(8,128)S(1)} %get-tuple-element.18.entry_slot, f32[8,32,64]{2,1,0:T(8,128)S(1)} %bitcast.11), custom_call_target="tpu_custom_call" | custom-call | flops 1000000000 | bytes 1000000 | tf_op jit(solution)/shard_map/weights/pallas_call | solution.py:409
  19.5 1.9 %collective-permute-done.4.below = bf16[1536,256]{1,0:T(8,128)(2,1)S(1)} collective-permute-done((bf16[1536,256]{1,0:T(8,128)(2,1)}, bf16[1536,256]{1,0:T(8,128)(2,1)S(1)}, u32[]{:S(2)}, u32[]{:S(2)}) %collective-permute-start.4) | collective-permute-done | bytes 786464 | tf_op jit(solution)/shard_map/ppermute | solution.py:374
  21.4 2.8 %collective-permute-done.5.above = bf16[1536,256]{1,0:T(8,128)(2,1)S(1)} collective-permute-done((bf16[1536,256]{1,0:T(8,128)(2,1)}, bf16[1536,256]{1,0:T(8,128)(2,1)S(1)}, u32[]{:S(2)}, u32[]{:S(2)}) %collective-permute-start.5) | collective-permute-done | bytes 786464 | tf_op jit(solution)/shard_map/ppermute | solution.py:374
  24.2 0.0 collective-permute-done.table_w
  24.2 0.0 collective-permute-done.1.table_e
  24.2 2.9 %select.1 = (bf16[1536,256]{1,0:T(8,128)(2,1)S(1)}, bf16[1536,256]{1,0:T(8,128)(2,1)S(1)}) custom-call(bf16[1536,256]{1,0:T(8,128)(2,1)S(1)} %collective-permute-done.4.below, bf16[1536,256]{1,0:T(8,128)(2,1)S(1)} %get-tuple-element.20.here, bf16[1536,256]{1,0:T(8,128)(2,1)S(1)} %collective-permute-done.5.above, f32[64,256]{1,0:T(8,128)S(1)} %collective-permute-done.table_w, ...), custom_call_target="tpu_custom_call" | custom-call | flops 100000000 | bytes 4000000 | tf_op jit(solution)/shard_map/select/pallas_call | solution.py:419
  27.1 0.1 collective-permute-start.6
  27.2 5.1 %collective-permute-start.7 = (bf16[1536,256]{1,0:T(8,128)(2,1)S(1)}, bf16[1536,256]{1,0:T(8,128)(2,1)S(1)}, u32[]{:S(2)}, u32[]{:S(2)}) collective-permute-start(bf16[1536,256]{1,0:T(8,128)(2,1)S(1)} %get-tuple-element.23), channel_id=1, source_target_pairs={{1,0},{2,1},{3,2},{4,3},{5,4},{6,5},{7,6},{8,7},{9,8},{10,9},{11,1... | collective-permute-start | bytes 2359304 | tf_op jit(solution)/shard_map/ppermute | solution.py:379
  32.3 1.9 %collective-permute-start.2 = (f32[192,256]{1,0:T(8,128)S(1)}, f32[192,256]{1,0:T(8,128)S(1)}, u32[]{:S(2)}, u32[]{:S(2)}) collective-permute-start(f32[192,256]{1,0:T(8,128)S(1)} %constant_dynamic-update-slice_fusion.here), channel_id=1, source_target_pairs={{0,32},{32,64},{64,96},{1,33},{33,65},{65,97},{2,34},{34,66},{66,9... | collective-permute-start | bytes 589832 | tf_op jit(solution)/shard_map/ppermute | solution.py:374
  34.2 4.1 %collective-permute-start.3 = (f32[192,256]{1,0:T(8,128)S(1)}, f32[192,256]{1,0:T(8,128)S(1)}, u32[]{:S(2)}, u32[]{:S(2)}) collective-permute-start(f32[192,256]{1,0:T(8,128)S(1)} %constant_dynamic-update-slice_fusion.here), channel_id=1, source_target_pairs={{32,0},{64,32},{96,64},{33,1},{65,33},{97,65},{34,2},{66,34},{98,6... | collective-permute-start | bytes 589832 | tf_op jit(solution)/shard_map/ppermute | solution.py:374
  38.3 3.5 %own_gram.1 = (f32[2048,256]{1,0:T(8,128)S(1)}, bf16[1536,256]{1,0:T(8,128)(2,1)S(1)}) custom-call(bf16[1536,256]{1,0:T(8,128)(2,1)S(1)} %collective-permute-done.4.below, bf16[1536,256]{1,0:T(8,128)(2,1)S(1)} %get-tuple-element.20.here, bf16[1536,256]{1,0:T(8,128)(2,1)S(1)} %collective-permute-done.5.above, f32[64,256]{1,0:T(8,128)S(1)} %get-tuple-element.17.table.meta, ...), custom_call_target="tpu_custom_call" | custom-call | flops 1610612736 | bytes 5000000 | tf_op jit(solution)/shard_map/own_gram/pallas_call | solution.py:434
  41.8 0.0 collective-permute-done.2.below
  41.8 0.0 collective-permute-done.3.above
  41.8 0.4 innov.2
  42.2 0.0 collective-permute-done.6.west
  42.2 0.0 collective-permute-done.7.east
  42.2 0.0 copy-start
  42.3 9.6 %mixing.1.refs_6_ = bf16[2176,128]{1,0:T(8,128)(2,1)S(1)} custom-call(bf16[1536,256]{1,0:T(8,128)(2,1)S(1)} %collective-permute-done.6.west, bf16[1536,256]{1,0:T(8,128)(2,1)S(1)} %collective-permute-done.7.east, f32[8,4608]{1,0:T(8,128)S(1)} %weights.1, f32[2048,256]{1,0:T(8,128)S(1)} %get-tuple-element.25.gram_own, ...), custom_call_target="tpu_custom_call" | custom-call | flops 6442450944 | bytes 4000000 | tf_op jit(solution)/shard_map/mixing/pallas_call | solution.py:451
  51.9 1.9 %collective-permute-start.8 = (bf16[2176,128]{1,0:T(8,128)(2,1)S(1)}, bf16[2176,128]{1,0:T(8,128)(2,1)S(1)}, u32[]{:S(2)}, u32[]{:S(2)}) collective-permute-start(bf16[2176,128]{1,0:T(8,128)(2,1)S(1)} %mixing.1.refs_6_), channel_id=1, source_target_pairs={{0,32},{32,64},{64,96},{1,33},{33,65},{65,97},{2,34},{34,66},{66,9... | collective-permute-start | bytes 1671176 | tf_op jit(solution)/shard_map/ppermute | solution.py:374
  53.8 3.9 %collective-permute-start.9 = (bf16[2176,128]{1,0:T(8,128)(2,1)S(1)}, bf16[2176,128]{1,0:T(8,128)(2,1)S(1)}, u32[]{:S(2)}, u32[]{:S(2)}) collective-permute-start(bf16[2176,128]{1,0:T(8,128)(2,1)S(1)} %mixing.1.refs_6_), channel_id=1, source_target_pairs={{32,0},{64,32},{96,64},{33,1},{65,33},{97,65},{34,2},{66,34},{98,6... | collective-permute-start | bytes 1671176 | tf_op jit(solution)/shard_map/ppermute | solution.py:374
  57.8 0.1 collective-permute-start.10
  57.8 5.1 %collective-permute-start.11 = (bf16[2176,128]{1,0:T(8,128)(2,1)S(1)}, bf16[2176,128]{1,0:T(8,128)(2,1)S(1)}, u32[]{:S(2)}, u32[]{:S(2)}) collective-permute-start(bf16[2176,128]{1,0:T(8,128)(2,1)S(1)} %mixing.1.refs_6_), channel_id=1, source_target_pairs={{1,0},{2,1},{3,2},{4,3},{5,4},{6,5},{7,6},{8,7},{9,8},{10,9},{11,1... | collective-permute-start | bytes 1671176 | tf_op jit(solution)/shard_map/ppermute | solution.py:379
  62.9 4.1 %collective-permute-done.8.refs_7_ = bf16[2176,128]{1,0:T(8,128)(2,1)S(1)} collective-permute-done((bf16[2176,128]{1,0:T(8,128)(2,1)S(1)}, bf16[2176,128]{1,0:T(8,128)(2,1)S(1)}, u32[]{:S(2)}, u32[]{:S(2)}) %collective-permute-start.8) | collective-permute-done | bytes 557088 | tf_op jit(solution)/shard_map/ppermute | solution.py:374
  67.0 0.0 collective-permute-start.12
  67.0 5.2 %collective-permute-start.13 = (bf16[2176,128]{1,0:T(8,128)(2,1)S(1)}, bf16[2176,128]{1,0:T(8,128)(2,1)S(1)}, u32[]{:S(2)}, u32[]{:S(2)}) collective-permute-start(bf16[2176,128]{1,0:T(8,128)(2,1)S(1)} %collective-permute-done.8.refs_7_), channel_id=1, source_target_pairs={{1,0},{2,1},{3,2},{4,3},{5,4},{6,5},{7,6},{8,7},{9,8},{10,9},{11,1... | collective-permute-start | bytes 1671176 | tf_op jit(solution)/shard_map/ppermute | solution.py:379
  72.2 0.0 collective-permute-done.9.refs_8_
  72.2 0.0 collective-permute-start.14
  72.2 0.0 collective-permute-done.10.refs_9_
  72.2 5.1 %collective-permute-start.15 = (bf16[2176,128]{1,0:T(8,128)(2,1)S(1)}, bf16[2176,128]{1,0:T(8,128)(2,1)S(1)}, u32[]{:S(2)}, u32[]{:S(2)}) collective-permute-start(bf16[2176,128]{1,0:T(8,128)(2,1)S(1)} %collective-permute-done.9.refs_8_), channel_id=1, source_target_pairs={{1,0},{2,1},{3,2},{4,3},{5,4},{6,5},{7,6},{8,7},{9,8},{10,9},{11,1... | collective-permute-start | bytes 1671176 | tf_op jit(solution)/shard_map/ppermute | solution.py:379
  77.3 0.0 collective-permute-done.11.refs_10_
  77.3 8.5 %inner.1.refs_1_ = f32[2304,256]{1,0:T(8,128)S(1)} custom-call(bf16[2304,256]{1,0:T(8,128)(2,1)S(1)} %bitcast.5, f32[16,256]{1,0:T(8,128)S(1)} %slice.27.refs_1_, f32[16,256]{1,0:T(8,128)S(1)} %get-tuple-element.34.refs_2_, f32[16,256]{1,0:T(8,128)S(1)} %get-tuple-element.31.refs_3_, f32[16,256]{1,0:T(8,128)S(1)} %slice.38.refs_4_, ...), custom_call_target="tpu_custom_call" | custom-call | flops 4026531840 | bytes 6000000 | tf_op jit(solution)/shard_map/inner/pallas_call | solution.py:488
  85.8 0.0 collective-permute-done.12.refs_4_
  85.8 0.0 collective-permute-done.13.refs_5_
  85.8 3.8 %outer.1.refs_1_ = f32[2304,256]{1,0:T(8,128)S(1)} custom-call(bf16[2304,256]{1,0:T(8,128)(2,1)S(1)} %bitcast.6, f32[2304,256]{1,0:T(8,128)S(1)} %inner.1.refs_1_, f32[16,256]{1,0:T(8,128)S(1)} %get-tuple-element.33.refs_2_, f32[16,256]{1,0:T(8,128)S(1)} %get-tuple-element.32.refs_3_, bf16[2176,128]{1,0:T(8,128)(2,1)S(1)} %collective-permute-done.12.refs_4_, ...), custom_call_target="tpu_custom_call" | custom-call | flops 1610612736 | bytes 6000000 | tf_op jit(solution)/shard_map/outer/pallas_call | solution.py:488
  89.7 0.0 collective-permute-done.14.refs_4_
  89.7 0.0 collective-permute-done.15.refs_5_
  89.7 4.8 %finish.1 = bf16[2304,256]{1,0:T(8,128)(2,1)} custom-call(bf16[2304,256]{1,0:T(8,128)(2,1)S(1)} %bitcast.7, f32[2304,256]{1,0:T(8,128)S(1)} %outer.1.refs_1_, f32[16,256]{1,0:T(8,128)S(1)} %get-tuple-element.30.refs_2_, f32[16,256]{1,0:T(8,128)S(1)} %get-tuple-element.29.refs_3_, bf16[2176,128]{1,0:T(8,128)(2,1)S(1)} %collective-permute-done.14.refs_4_, ...), custom_call_target="tpu_custom_call" | custom-call | flops 1610612736 | bytes 6000000 | tf_op jit(solution)/shard_map/finish/pallas_call | solution.py:488
  (14 shorter events, 0.0 us)
Async XLA Ops:
  0.0 21.4 %collective-permute-start.4 = (bf16[1536,256]{1,0:T(8,128)(2,1)}, bf16[1536,256]{1,0:T(8,128)(2,1)S(1)}, u32[]{:S(2)}, u32[]{:S(2)}) collective-permute-start(bf16[1536,256]{1,0:T(8,128)(2,1)} %bitcast.8), channel_id=1, source_target_pairs={{0,32},{32,64},{64,96},{1,33},{33,65},{65,97},{2,34},{34,66},{66,9... | collective-permute-start | bytes 2359304 | tf_op jit(solution)/shard_map/ppermute | solution.py:374
  3.1 21.1 %collective-permute-start.5 = (bf16[1536,256]{1,0:T(8,128)(2,1)}, bf16[1536,256]{1,0:T(8,128)(2,1)S(1)}, u32[]{:S(2)}, u32[]{:S(2)}) collective-permute-start(bf16[1536,256]{1,0:T(8,128)(2,1)} %bitcast.9), channel_id=1, source_target_pairs={{32,0},{64,32},{96,64},{33,1},{65,33},{97,65},{34,2},{66,34},{98,6... | collective-permute-start | bytes 2359304 | tf_op jit(solution)/shard_map/ppermute | solution.py:374
  6.6 1.1 %copy-start.1 = (bf16[48,32,256]{2,1,0:T(8,128)(2,1)S(1)}, bf16[48,32,256]{2,1,0:T(8,128)(2,1)}, u32[]{:S(2)}) copy-start(bf16[48,32,256]{2,1,0:T(8,128)(2,1)} %param.8) | copy-start | bytes 2359300
  7.8 0.7 copy-start.3
  8.5 0.7 copy-start.4
  9.2 0.7 copy-start.5
  9.9 7.6 %copy-start.2 = (f32[8,64,32]{1,2,0:T(8,128)S(1)}, f32[8,64,32]{1,2,0:T(8,128)}, u32[]{:S(2)}) copy-start(f32[8,64,32]{1,2,0:T(8,128)} %param.12) | copy-start | bytes 196612
  12.0 12.2 %collective-permute-start = (f32[64,256]{1,0:T(8,128)S(1)}, f32[64,256]{1,0:T(8,128)S(1)}, u32[]{:S(2)}, u32[]{:S(2)}) collective-permute-start(f32[64,256]{1,0:T(8,128)S(1)} %get-tuple-element.17.table.meta), channel_id=1, source_target_pairs={{31,0},{0,1},{1,2},{2,3},{3,4},{4,5},{5,6},{6,7},{7,8},{8,9},{9,10... | collective-permute-start | bytes 196616 | tf_op jit(solution)/shard_map/ppermute | solution.py:379
  12.1 12.1 %collective-permute-start.1 = (f32[64,256]{1,0:T(8,128)S(1)}, f32[64,256]{1,0:T(8,128)S(1)}, u32[]{:S(2)}, u32[]{:S(2)}) collective-permute-start(f32[64,256]{1,0:T(8,128)S(1)} %get-tuple-element.17.table.meta), channel_id=1, source_target_pairs={{1,0},{2,1},{3,2},{4,3},{5,4},{6,5},{7,6},{8,7},{9,8},{10,9},{11,1... | collective-permute-start | bytes 196616 | tf_op jit(solution)/shard_map/ppermute | solution.py:379
  27.1 15.1 %collective-permute-start.6 = (bf16[1536,256]{1,0:T(8,128)(2,1)S(1)}, bf16[1536,256]{1,0:T(8,128)(2,1)S(1)}, u32[]{:S(2)}, u32[]{:S(2)}) collective-permute-start(bf16[1536,256]{1,0:T(8,128)(2,1)S(1)} %get-tuple-element.22), channel_id=1, source_target_pairs={{31,0},{0,1},{1,2},{2,3},{3,4},{4,5},{5,6},{6,7},{7,8},{8,9},{9,10... | collective-permute-start | bytes 2359304 | tf_op jit(solution)/shard_map/ppermute | solution.py:379
  27.2 15.0 %collective-permute-start.7 = (bf16[1536,256]{1,0:T(8,128)(2,1)S(1)}, bf16[1536,256]{1,0:T(8,128)(2,1)S(1)}, u32[]{:S(2)}, u32[]{:S(2)}) collective-permute-start(bf16[1536,256]{1,0:T(8,128)(2,1)S(1)} %get-tuple-element.23), channel_id=1, source_target_pairs={{1,0},{2,1},{3,2},{4,3},{5,4},{6,5},{7,6},{8,7},{9,8},{10,9},{11,1... | collective-permute-start | bytes 2359304 | tf_op jit(solution)/shard_map/ppermute | solution.py:379
  32.3 9.5 %collective-permute-start.2 = (f32[192,256]{1,0:T(8,128)S(1)}, f32[192,256]{1,0:T(8,128)S(1)}, u32[]{:S(2)}, u32[]{:S(2)}) collective-permute-start(f32[192,256]{1,0:T(8,128)S(1)} %constant_dynamic-update-slice_fusion.here), channel_id=1, source_target_pairs={{0,32},{32,64},{64,96},{1,33},{33,65},{65,97},{2,34},{34,66},{66,9... | collective-permute-start | bytes 589832 | tf_op jit(solution)/shard_map/ppermute | solution.py:374
  34.2 7.6 %collective-permute-start.3 = (f32[192,256]{1,0:T(8,128)S(1)}, f32[192,256]{1,0:T(8,128)S(1)}, u32[]{:S(2)}, u32[]{:S(2)}) collective-permute-start(f32[192,256]{1,0:T(8,128)S(1)} %constant_dynamic-update-slice_fusion.here), channel_id=1, source_target_pairs={{32,0},{64,32},{96,64},{33,1},{65,33},{97,65},{34,2},{66,34},{98,6... | collective-permute-start | bytes 589832 | tf_op jit(solution)/shard_map/ppermute | solution.py:374
  42.2 35.0 %copy-start = (bf16[48,48,256]{2,1,0:T(8,128)(2,1)S(1)}, bf16[48,48,256]{2,1,0:T(8,128)(2,1)}, u32[]{:S(2)}) copy-start(bf16[48,48,256]{2,1,0:T(8,128)(2,1)} %param.7) | copy-start | bytes 3538948
  51.9 15.1 %collective-permute-start.8 = (bf16[2176,128]{1,0:T(8,128)(2,1)S(1)}, bf16[2176,128]{1,0:T(8,128)(2,1)S(1)}, u32[]{:S(2)}, u32[]{:S(2)}) collective-permute-start(bf16[2176,128]{1,0:T(8,128)(2,1)S(1)} %mixing.1.refs_6_), channel_id=1, source_target_pairs={{0,32},{32,64},{64,96},{1,33},{33,65},{65,97},{2,34},{34,66},{66,9... | collective-permute-start | bytes 1671176 | tf_op jit(solution)/shard_map/ppermute | solution.py:374
  53.8 18.4 %collective-permute-start.9 = (bf16[2176,128]{1,0:T(8,128)(2,1)S(1)}, bf16[2176,128]{1,0:T(8,128)(2,1)S(1)}, u32[]{:S(2)}, u32[]{:S(2)}) collective-permute-start(bf16[2176,128]{1,0:T(8,128)(2,1)S(1)} %mixing.1.refs_6_), channel_id=1, source_target_pairs={{32,0},{64,32},{96,64},{33,1},{65,33},{97,65},{34,2},{66,34},{98,6... | collective-permute-start | bytes 1671176 | tf_op jit(solution)/shard_map/ppermute | solution.py:374
  57.8 14.4 %collective-permute-start.10 = (bf16[2176,128]{1,0:T(8,128)(2,1)S(1)}, bf16[2176,128]{1,0:T(8,128)(2,1)S(1)}, u32[]{:S(2)}, u32[]{:S(2)}) collective-permute-start(bf16[2176,128]{1,0:T(8,128)(2,1)S(1)} %mixing.1.refs_6_), channel_id=1, source_target_pairs={{31,0},{0,1},{1,2},{2,3},{3,4},{4,5},{5,6},{6,7},{7,8},{8,9},{9,10... | collective-permute-start | bytes 1671176 | tf_op jit(solution)/shard_map/ppermute | solution.py:379
  57.8 19.4 %collective-permute-start.11 = (bf16[2176,128]{1,0:T(8,128)(2,1)S(1)}, bf16[2176,128]{1,0:T(8,128)(2,1)S(1)}, u32[]{:S(2)}, u32[]{:S(2)}) collective-permute-start(bf16[2176,128]{1,0:T(8,128)(2,1)S(1)} %mixing.1.refs_6_), channel_id=1, source_target_pairs={{1,0},{2,1},{3,2},{4,3},{5,4},{6,5},{7,6},{8,7},{9,8},{10,9},{11,1... | collective-permute-start | bytes 1671176 | tf_op jit(solution)/shard_map/ppermute | solution.py:379
  67.0 18.8 %collective-permute-start.12 = (bf16[2176,128]{1,0:T(8,128)(2,1)S(1)}, bf16[2176,128]{1,0:T(8,128)(2,1)S(1)}, u32[]{:S(2)}, u32[]{:S(2)}) collective-permute-start(bf16[2176,128]{1,0:T(8,128)(2,1)S(1)} %collective-permute-done.8.refs_7_), channel_id=1, source_target_pairs={{31,0},{0,1},{1,2},{2,3},{3,4},{4,5},{5,6},{6,7},{7,8},{8,9},{9,10... | collective-permute-start | bytes 1671176 | tf_op jit(solution)/shard_map/ppermute | solution.py:379
  67.0 18.8 %collective-permute-start.13 = (bf16[2176,128]{1,0:T(8,128)(2,1)S(1)}, bf16[2176,128]{1,0:T(8,128)(2,1)S(1)}, u32[]{:S(2)}, u32[]{:S(2)}) collective-permute-start(bf16[2176,128]{1,0:T(8,128)(2,1)S(1)} %collective-permute-done.8.refs_7_), channel_id=1, source_target_pairs={{1,0},{2,1},{3,2},{4,3},{5,4},{6,5},{7,6},{8,7},{9,8},{10,9},{11,1... | collective-permute-start | bytes 1671176 | tf_op jit(solution)/shard_map/ppermute | solution.py:379
  72.2 17.5 %collective-permute-start.14 = (bf16[2176,128]{1,0:T(8,128)(2,1)S(1)}, bf16[2176,128]{1,0:T(8,128)(2,1)S(1)}, u32[]{:S(2)}, u32[]{:S(2)}) collective-permute-start(bf16[2176,128]{1,0:T(8,128)(2,1)S(1)} %collective-permute-done.9.refs_8_), channel_id=1, source_target_pairs={{31,0},{0,1},{1,2},{2,3},{3,4},{4,5},{5,6},{6,7},{7,8},{8,9},{9,10... | collective-permute-start | bytes 1671176 | tf_op jit(solution)/shard_map/ppermute | solution.py:379
  72.2 17.5 %collective-permute-start.15 = (bf16[2176,128]{1,0:T(8,128)(2,1)S(1)}, bf16[2176,128]{1,0:T(8,128)(2,1)S(1)}, u32[]{:S(2)}, u32[]{:S(2)}) collective-permute-start(bf16[2176,128]{1,0:T(8,128)(2,1)S(1)} %collective-permute-done.9.refs_8_), channel_id=1, source_target_pairs={{1,0},{2,1},{3,2},{4,3},{5,4},{6,5},{7,6},{8,7},{9,8},{10,9},{11,1... | collective-permute-start | bytes 1671176 | tf_op jit(solution)/shard_map/ppermute | solution.py:379

commit v3 on v2

v3 whole, which is shorter than its diff:
```python
import functools

import jax
import jax.numpy as jnp
from jax import lax
from jax.experimental import pallas as pl
from jax.experimental.pallas import tpu as pltpu
from jax.sharding import PartitionSpec as P

NS_ITERS = 5
CAP = 16
SELF, FIRST, SECOND = 0, 1, 2
CLASSES = 9
BAND_SLOTS = 3 * CAP
CLASS_STRIDE = 64
KEYS = 640
META_LANES = 256
META_ROWS = 16
BLOCK_ROW = 8
INNOV_ROW = 9

F32 = jnp.float32
BF16 = jnp.bfloat16
VMEM_SPEC = pl.BlockSpec(memory_space=pltpu.VMEM)
SMEM_SPEC = pl.BlockSpec(memory_space=pltpu.SMEM)


def dot(a, b):
    return jnp.dot(a, b, preferred_element_type=F32)


def call(kernel, outs, in_specs, name, flops, bytes_accessed, scratch=(), aliases=None):
    return pl.pallas_call(
        kernel,
        out_shape=outs,
        in_specs=in_specs,
        out_specs=jax.tree.map(lambda _: VMEM_SPEC, outs),
        scratch_shapes=list(scratch),
        input_output_aliases=aliases or {},
        compiler_params=pltpu.CompilerParams(vmem_limit_bytes=40 * 1024 * 1024),
        cost_estimate=pl.CostEstimate(
            flops=flops, bytes_accessed=bytes_accessed, transcendentals=0
        ),
        name=name,
    )


def fold(x, width):
    per = META_LANES // width
    sub = lax.broadcasted_iota(jnp.int32, (per, META_LANES), 0)
    which = lax.broadcasted_iota(jnp.int32, (per, META_LANES), 1) // width
    return jnp.concatenate(
        [
            jnp.sum(jnp.where(sub == which, x[i : i + per], 0.0), axis=0, keepdims=True)
            for i in range(0, x.shape[0], per)
        ],
        axis=0,
    )


def table_kernel(shape, lists, placement, state, innov, obs, meta, entry_slot, obs_copy):
    lon_count, blocks = shape
    regions, list_len = lists.shape
    entries = regions * list_len
    obs_rows = innov.shape[1]
    obs_copy[...] = obs[...]
    p = lax.broadcasted_iota(jnp.int32, (obs_rows, META_LANES), 0)
    q = lax.broadcasted_iota(jnp.int32, (obs_rows, META_LANES), 1) % obs_rows
    repeated = dot(innov[...], jnp.where(p == q, 1.0, 0.0).astype(BF16))
    meta[...] = jnp.zeros_like(meta)
    folded = fold(repeated, obs_rows)
    meta[INNOV_ROW : INNOV_ROW + folded.shape[0], :] = folded

    def columns(x):
        t = x.T
        return jnp.concatenate(
            [jnp.broadcast_to(t[:, r : r + 1], (list_len, 128)) for r in range(regions)], axis=0
        )

    lane = lax.broadcasted_iota(jnp.int32, (1, 128), 1).astype(F32)
    ones = jnp.ones((128, 128), BF16)
    ids = columns(lists[...].astype(F32))
    line = jnp.floor(ids * (1.0 / 128.0))
    table_rows = placement.shape[0]
    line_hot = jnp.where(line == lane, 1.0, 0.0).astype(BF16)[:, :table_rows]
    at = lane == ids - 128.0 * line
    places = placement[...].astype(F32)
    high = jnp.floor(places * (1.0 / 64.0))

    def look(part):
        found = dot(line_hot, part.astype(BF16))
        return dot(jnp.where(at, found, 0.0).astype(BF16), ones)

    row = 64.0 * look(high) + look(places - 64.0 * high)
    holder = jnp.floor((row + 0.5) * (1.0 / blocks))
    inside = row - blocks * holder
    holder_band = jnp.floor((holder + 0.5) * (1.0 / lon_count))
    band_here = lax.axis_index("band")
    lon_here = lax.axis_index("lon")
    band_step = holder_band - band_here.astype(F32)
    lon_step = holder - lon_count * holder_band - lon_here.astype(F32)
    half = lon_count // 2
    lon_step = jnp.where(lon_step < -half, lon_step + lon_count, lon_step)
    lon_step = jnp.where(lon_step > half, lon_step - lon_count, lon_step)
    band_turn = band_step * (1 - 2 * (band_here % 2)).astype(F32)
    lon_turn = lon_step * (2 * (lon_here % 2) - 1).astype(F32)
    band_place = jnp.where(band_turn == 0.0, 0.0, jnp.where(band_turn > 0.0, 1.0, 2.0))
    lon_place = jnp.where(lon_turn == 0.0, 0.0, jnp.where(lon_turn > 0.0, 1.0, 2.0))
    key = (lon_place * 3.0 + band_place) * CLASS_STRIDE + inside

    hot = jnp.concatenate(
        [jnp.where(key == lane + 128.0 * c, 1.0, 0.0) for c in range(KEYS // 128)], axis=1
    ).astype(BF16)
    counts = lax.dot_general(
        hot,
        jnp.ones((entries, 128), BF16),
        (((0,), (0,)), ((), ())),
        preferred_element_type=F32,
    )
    present = jnp.minimum(counts, 1.0)
    down = lax.broadcasted_iota(jnp.int32, (KEYS, KEYS), 0)
    across = lax.broadcasted_iota(jnp.int32, (KEYS, KEYS), 1)
    before = (across < down) & (across // CLASS_STRIDE == down // CLASS_STRIDE)
    rank = dot(jnp.where(before, 1.0, 0.0).astype(BF16), present.astype(BF16))
    key_id = lax.broadcasted_iota(jnp.int32, (KEYS, 128), 0)
    slot = rank + (CAP * (key_id // CLASS_STRIDE)).astype(F32)
    block = (key_id % CLASS_STRIDE).astype(F32)
    slots = dot(hot, slot.astype(BF16))
    entry_slot[...] = slots
    tapers = columns(state[...])
    for c in range(2):
        match = (slot == lane + 128.0 * c) & (present > 0.0)
        rows = jnp.sum(jnp.where(match, block, 0.0), axis=0, keepdims=True)
        meta[BLOCK_ROW : BLOCK_ROW + 1, 128 * c : 128 * (c + 1)] = rows
        hit = jnp.where(slots == lane + 128.0 * c, tapers, 0.0)
        for r in range(regions):
            meta[r : r + 1, 128 * c : 128 * (c + 1)] = jnp.sum(
                hit[r * list_len : (r + 1) * list_len], axis=0, keepdims=True
            )


def weight_kernel(regions, list_len, entry_slot, taper, weights):
    obs_rows = taper.shape[1]
    group = (lax.broadcasted_iota(jnp.int32, (1, 128), 1) // obs_rows).astype(F32)
    p = lax.broadcasted_iota(jnp.int32, (obs_rows, 128), 0)
    q = lax.broadcasted_iota(jnp.int32, (obs_rows, 128), 1) % obs_rows
    spread = jnp.where(p == q, 1.0, 0.0).astype(BF16)

    def across(x):
        return lax.dot_general(
            x, spread, (((0,), (0,)), ((), ())), preferred_element_type=F32
        )

    for r in range(regions):
        mine = entry_slot[r * list_len : (r + 1) * list_len, :]
        high = taper[r].astype(BF16)
        low = (taper[r] - high.astype(F32)).astype(BF16)
        w = across(high) + across(low)
        for c in range(CLASSES * CAP // 4):
            hit = mine == group + 4.0 * c
            weights[r : r + 1, 128 * c : 128 * (c + 1)] = jnp.sum(
                jnp.where(hit, w, 0.0), axis=0, keepdims=True
            )


def gather_blocks(sources, table, first_slot, obs_rows, out):
    for k, source in enumerate(sources):
        for i in range(CAP):
            block = table[BLOCK_ROW, first_slot + CAP * k + i].astype(jnp.int32)
            at = pl.multiple_of(block * obs_rows, obs_rows)
            to = (CAP * k + i) * obs_rows
            out[to : to + obs_rows, :] = source[pl.ds(at, obs_rows), :]


def select_kernel(obs_rows, obs, obs_1, obs_2, table_1, table_2, to_1, to_2):
    sources = (obs, obs_1, obs_2)
    gather_blocks(sources, table_1, FIRST * BAND_SLOTS, obs_rows, to_1)
    gather_blocks(sources, table_2, SECOND * BAND_SLOTS, obs_rows, to_2)


def transposed(y):
    return jnp.concatenate(
        [y[256 * c : 256 * (c + 1)].astype(F32).T.astype(BF16) for c in range(y.shape[0] // 256)],
        axis=1,
    )


def own_gram_kernel(obs_rows, regions, obs, obs_1, obs_2, table, weights, gram, pool):
    gather_blocks((obs, obs_1, obs_2), table, SELF * BAND_SLOTS, obs_rows, pool)
    y = pool[...]
    y_t = transposed(y)
    first = SELF * BAND_SLOTS * obs_rows
    w16 = weights[:, first : first + y.shape[0]].astype(BF16)
    for r in range(regions):
        gram[256 * r : 256 * (r + 1), :] = dot(y_t * w16[r : r + 1, :], y)


def innov_kernel(obs_rows, regions, blocks, metas, metas_1, metas_2, weights, pool, scaled, proj):
    down = lax.broadcasted_iota(jnp.int32, (blocks, META_LANES), 0).astype(F32)
    mine = metas[META_ROWS * SELF + BLOCK_ROW : META_ROWS * SELF + BLOCK_ROW + 1, :]
    hot = jnp.where(down == mine, 1.0, 0.0).T.astype(BF16)
    per = META_LANES // obs_rows
    sub = lax.broadcasted_iota(jnp.int32, (per, META_LANES), 0)
    which = lax.broadcasted_iota(jnp.int32, (per, META_LANES), 1) // obs_rows
    picked = []
    for n in range(CLASSES):
        source = (metas, metas_1, metas_2)[n % 3]
        base = META_ROWS * (n // 3) + INNOV_ROW
        rows = [
            jnp.where(sub == which, source[base + i : base + i + 1, :], 0.0)
            for i in range(blocks // per)
        ]
        picked.append(dot(hot[CAP * n : CAP * (n + 1)], jnp.concatenate(rows, axis=0).astype(BF16)))
    p = lax.broadcasted_iota(jnp.int32, (META_LANES, META_LANES), 0) % obs_rows
    q = lax.broadcasted_iota(jnp.int32, (META_LANES, META_LANES), 1) % obs_rows
    spread = jnp.where(p == q, 1.0, 0.0).astype(BF16)
    repeated = dot(jnp.concatenate(picked, axis=0).astype(BF16), spread)
    folded = fold(repeated, obs_rows)
    lanes = jnp.concatenate([folded[i : i + 1] for i in range(folded.shape[0])], axis=1)
    wd = weights[...] * lanes
    high = wd.astype(BF16)
    both = jnp.concatenate([high.astype(F32), wd - high.astype(F32)], axis=0).astype(BF16)
    scaled[...] = both
    first = SELF * BAND_SLOTS * obs_rows
    part = dot(both[:, first : first + pool.shape[0]], pool[...])
    proj[...] = part[:regions] + part[regions:]


def quarters(x):
    return x[:128, :128], x[:128, 128:], x[128:, :128], x[128:, 128:]


def add_diagonal(x, d, eye):
    q = quarters(x)
    top = jnp.concatenate([q[0] + d * eye, q[1]], axis=1)
    low = jnp.concatenate([q[2], q[3] + d * eye], axis=1)
    return jnp.concatenate([top, low], axis=0)


def trace(x, eye):
    q = quarters(x)
    both = (q[0] + q[3]) * eye
    return jnp.sum(jnp.sum(both, axis=0, keepdims=True), axis=1, keepdims=True)


def roots(grams, proj_rows, eye, ensemble):
    each = range(len(grams))
    base = ensemble - 1.0
    scale = [
        base
        + jnp.max(jnp.sum(jnp.abs(grams[i]), axis=0, keepdims=True), axis=1, keepdims=True)
        for i in each
    ]
    inverse = [1.0 / scale[i] for i in each]
    mean = [trace(grams[i], eye) * (1.0 / ensemble) for i in each]
    u = [
        add_diagonal(grams[i] * (-0.5 * inverse[i]), 0.5 * inverse[i] * mean[i], eye)
        for i in each
    ]
    c = [1.0 - (base + mean[i]) * inverse[i] for i in each]
    a = [1.0 + 0.5 * c[i] for i in each]
    g = u
    ub = [u[i].astype(BF16) for i in each]
    gb = ub
    for step in range(NS_ITERS - 1):
        u2 = [dot(ub[i], ub[i]) for i in each]
        w = [((1.5 + 1.5 * c[i]) * u[i] + u2[i]).astype(BF16) for i in each]
        u3 = [dot(ub[i], w[i]) for i in each]
        u = [(1.5 * c[i] + 0.75 * c[i] * c[i]) * u[i] + u3[i] for i in each]
        c = [(0.75 + 0.25 * c[i]) * c[i] * c[i] for i in each]
        ub = [u[i].astype(BF16) for i in each]
        ug = [dot(ub[i], gb[i]) for i in each]
        g = [(1.0 + 0.5 * c[i]) * g[i] + a[i] * u[i] + ug[i] for i in each]
        gb = [g[i].astype(BF16) for i in each]
        a = [a[i] * (1.0 + 0.5 * c[i]) for i in each]
    first = lax.broadcasted_iota(jnp.int32, (16, ensemble), 0) < 8

    def times(i, v):
        high = v.astype(BF16).astype(F32)
        stacked = jnp.where(first, high, v - high).astype(BF16)
        q = dot(stacked, gb[i])
        return a[i] * v + q[0:1] + q[8:9]

    half = [times(i, proj_rows[i]) for i in each]
    wbar = [times(i, half[i]) * inverse[i] for i in each]
    factor = [lax.sqrt(base * inverse[i]) for i in each]
    return [(factor[i], factor[i] * a[i] - 1.0, g[i]) for i in each], wbar


def pack(matrix, wbar, eye, upper):
    factor, diagonal, g = matrix
    q = quarters(g)
    left = factor * q[0] + diagonal * eye
    right = factor * q[1]
    corner = factor * q[3] + diagonal * eye
    merged = jnp.where(upper, left, corner)
    high = wbar.astype(BF16).astype(F32)
    low = wbar - high
    rows = [
        jnp.sum(corner * eye, axis=0, keepdims=True),
        high[:, :128],
        high[:, 128:],
        low[:, :128],
        low[:, 128:],
    ]
    down = lax.broadcasted_iota(jnp.int32, (16, 128), 0)
    extra = jnp.zeros((16, 128), F32)
    for k, r in enumerate(rows):
        extra = jnp.where(down == k, r, extra)
    return right.astype(BF16), merged.astype(BF16), extra.astype(BF16)


def mix_regions(first, count, gram, proj, packed):
    n = 256
    extras = n * proj.shape[0]
    down = lax.broadcasted_iota(jnp.int32, (128, 128), 0)
    across = lax.broadcasted_iota(jnp.int32, (128, 128), 1)
    eye = jnp.where(down == across, 1.0, 0.0)
    some = range(first, first + count)
    matrices, weights = roots(
        [gram[r - first] for r in some], [proj[r : r + 1, :] for r in some], eye, n
    )
    for k, r in enumerate(some):
        right, merged, extra = pack(matrices[k], weights[k], eye, down <= across)
        packed[n * r : n * r + 128, :] = right
        packed[n * r + 128 : n * (r + 1), :] = merged
        packed[extras + 16 * r : extras + 16 * (r + 1), :] = extra


def grams_of(first, count, gram_own, weights, parts):
    out = []
    for r in range(first, first + count):
        total_r = gram_own[256 * r : 256 * (r + 1), :]
        for y, y_t, lane in parts:
            w16 = weights[r : r + 1, lane : lane + y.shape[0]].astype(BF16)
            total_r = total_r + dot(y_t * w16, y)
        out.append(total_r)
    return out


def mix_kernel(together, lanes, *refs):
    pools, refs = refs[: len(lanes)], refs[len(lanes) :]
    weights, gram_own, scaled, proj_own, packed, proj = refs
    regions = proj.shape[0]
    part = sum(
        dot(scaled[:, lane : lane + y.shape[0]], y[...]) for y, lane in zip(pools, lanes)
    )
    proj[...] = proj_own[...] + part[:regions] + part[regions:]
    parts = [(y[...], transposed(y[...]), lane) for y, lane in zip(pools, lanes)]
    for first in range(0, regions, together):
        grams = grams_of(first, together, gram_own, weights, parts)
        mix_regions(first, together, grams, proj, packed)


def unpack(count, packed, full):
    n = 256
    down = lax.broadcasted_iota(jnp.int32, (128, 128), 0)
    across = lax.broadcasted_iota(jnp.int32, (128, 128), 1)
    upper = down <= across
    lower = down > across
    extra = packed[n * count : (n + 16) * count, :].astype(F32)
    columns = extra.T.astype(BF16)

    def spread(k):
        return dot(columns, jnp.where((down == k) | (down == k + 2), 1.0, 0.0).astype(BF16))

    for k in range(count):
        right = packed[n * k : n * k + 128, :].astype(F32)
        merged = packed[n * k + 128 : n * (k + 1), :].astype(F32)
        turned = merged.T
        top = spread(16 * k + 1)
        low = spread(16 * k + 2)
        diagonal = extra[16 * k : 16 * k + 1]
        corner = jnp.where(lower, merged, jnp.where(down == across, diagonal, turned))
        full[n * k : n * k + 128, :128] = (jnp.where(upper, merged, turned) + top).astype(BF16)
        full[n * k : n * k + 128, 128:] = (right + top).astype(BF16)
        full[n * k + 128 : n * (k + 1), :128] = (right.T + low).astype(BF16)
        full[n * k + 128 : n * (k + 1), 128:] = (corner + low).astype(BF16)


def add_increment(members, table, first_slot, packed, count, acc, left, full, state_rows):
    n = members.shape[1]
    unpack(count, packed, full)
    places = [
        pl.multiple_of(table[BLOCK_ROW, first_slot + i].astype(jnp.int32) * state_rows, state_rows)
        for i in range(CAP)
    ]
    for i in range(CAP):
        x = members[pl.ds(places[i], state_rows), :]
        for k in range(count):
            t = jnp.full((16, 128), table[k, first_slot + i], F32).astype(BF16)
            for u in range(state_rows // 16):
                for v in range(n // 128):
                    left[
                        state_rows * i + 16 * u : state_rows * i + 16 * (u + 1),
                        n * k + 128 * v : n * k + 128 * (v + 1),
                    ] = x[16 * u : 16 * (u + 1), 128 * v : 128 * (v + 1)] * t
    product = dot(left[...], full[...])
    for i in range(CAP):
        acc[pl.ds(places[i], state_rows), :] += product[state_rows * i : state_rows * (i + 1), :]


def increment_kernel(slots, halves, start, finish, state_rows, count, *refs):
    refs = list(refs)
    members = refs.pop(0)
    before = None if start else refs.pop(0)
    items = len(slots)
    tables, packed, refs = refs[:items], refs[items : 2 * items], refs[2 * items :]
    rows = count * (members.shape[1] + 16)
    if finish:
        out, acc = refs[:2]
        scratch = refs[2:]
    else:
        acc = refs[0]
        scratch = refs[1:]
    acc[...] = members[...].astype(F32) if start else before[...]
    for k, slot in enumerate(slots):
        left, full = scratch[2 * (k % 2) : 2 * (k % 2) + 2]
        mixes = packed[k].at[rows * halves[k] : rows * (halves[k] + 1), :]
        add_increment(members, tables[k], slot, mixes, count, acc, left, full, state_rows)
    if finish:
        out[...] = acc[...].astype(BF16)


def from_band(x, place):
    count = lax.axis_size("band")
    step = 1 if place == FIRST else -1
    pairs = [(i + step * (1 - 2 * (i % 2)), i) for i in range(count)]
    return lax.ppermute(x, "band", [(j, i) for j, i in pairs if 0 <= j < count])


def from_lon(x, place):
    count = lax.axis_size("lon")
    step = -1 if place == FIRST else 1
    return lax.ppermute(
        x, "lon", [((i + step * (1 - 2 * (i % 2))) % count, i) for i in range(count)]
    )


def local(members, obs_perts, innovations, lists, placement, obs_taper, state_taper):
    lon_count = lax.axis_size("lon")
    blocks, state_rows, n = members.shape
    obs_rows = obs_perts.shape[1]
    regions, list_len = lists.shape
    entries = regions * list_len

    obs = obs_perts.reshape(blocks * obs_rows, n)
    obs_1 = from_band(obs, FIRST)
    obs_2 = from_band(obs, SECOND)

    meta, entry_slot, obs = call(
        functools.partial(table_kernel, (lon_count, blocks)),
        (
            jax.ShapeDtypeStruct((META_ROWS, META_LANES), F32),
            jax.ShapeDtypeStruct((entries, 128), F32),
            jax.ShapeDtypeStruct(obs.shape, BF16),
        ),
        [VMEM_SPEC] * 5,
        "tables",
        10**9,
        10**6,
    )(lists, placement.reshape(-1, 128), state_taper, innovations, obs)
    meta_1 = from_lon(meta, FIRST)
    meta_2 = from_lon(meta, SECOND)

    weights = call(
        functools.partial(weight_kernel, regions, list_len),
        jax.ShapeDtypeStruct((regions, CLASSES * CAP * obs_rows), F32),
        [VMEM_SPEC] * 2,
        "weights",
        10**9,
        10**6,
    )(entry_slot, jnp.swapaxes(obs_taper, 1, 2))
    obs_1, obs_2, weights = lax.optimization_barrier((obs_1, obs_2, weights))
    size = BAND_SLOTS * obs_rows
    pool_shape = jax.ShapeDtypeStruct((size, n), BF16)
    to_1, to_2 = call(
        functools.partial(select_kernel, obs_rows),
        (pool_shape, pool_shape),
        [VMEM_SPEC] * 3 + [SMEM_SPEC] * 2,
        "select",
        10**8,
        4 * 10**6,
    )(obs, obs_1, obs_2, meta_1, meta_2)
    pool_1 = from_lon(to_1, FIRST)
    pool_2 = from_lon(to_2, SECOND)
    metas = jnp.concatenate([meta, meta_1, meta_2], axis=0)
    metas_1 = from_band(metas, FIRST)
    metas_2 = from_band(metas, SECOND)

    region_flops = 2 * n**3
    gram_own, pool = call(
        functools.partial(own_gram_kernel, obs_rows, regions),
        (
            jax.ShapeDtypeStruct((regions * n, n), F32),
            pool_shape,
        ),
        [VMEM_SPEC] * 3 + [SMEM_SPEC] + [VMEM_SPEC],
        "own_gram",
        regions * 6 * region_flops,
        5 * 10**6,
    )(obs, obs_1, obs_2, meta, weights)
    proj_shape = jax.ShapeDtypeStruct((regions, n), F32)
    scaled, proj_own = call(
        functools.partial(innov_kernel, obs_rows, regions, blocks),
        (jax.ShapeDtypeStruct((2 * regions, 3 * size), BF16), proj_shape),
        [VMEM_SPEC] * 5,
        "innov",
        10**8,
        2 * 10**6,
    )(metas, metas_1, metas_2, weights, pool)
    mix = call(
        functools.partial(mix_kernel, 4, [FIRST * size, SECOND * size]),
        jax.ShapeDtypeStruct((regions * (n + 16), 128), BF16),
        [VMEM_SPEC] * 6,
        "mixing",
        regions * 24 * region_flops,
        4 * 10**6,
        [pltpu.VMEM(proj_shape.shape, F32)],
    )(pool_1, pool_2, weights, gram_own, scaled, proj_own)

    stacked = (metas, metas_1, metas_2)

    def table(lon, band):
        return stacked[band][META_ROWS * lon : META_ROWS * (lon + 1)]

    def slots(lon, band):
        return CAP * (lon * 3 + band)

    flat = members.reshape(blocks * state_rows, n)
    acc_shape = jax.ShapeDtypeStruct((blocks * state_rows, n), F32)
    scratch = [
        pltpu.VMEM((CAP * state_rows, regions * n), BF16),
        pltpu.VMEM((regions * n, n), BF16),
    ] * 2

    def increments(acc, groups, finish, name):
        start = acc is None
        kernel = functools.partial(
            increment_kernel,
            [slots(*g) for g in groups],
            [arrived[g][1] for g in groups],
            start,
            finish,
            state_rows,
            regions,
        )
        return call(
            kernel,
            jax.ShapeDtypeStruct(acc_shape.shape, BF16) if finish else acc_shape,
            [VMEM_SPEC] * (1 if start else 2)
            + [SMEM_SPEC] * len(groups)
            + [VMEM_SPEC] * len(groups),
            name,
            len(groups) * 3 * regions * region_flops,
            6 * 10**6,
            ([pltpu.VMEM(acc_shape.shape, F32)] if finish else []) + scratch,
        )(
            *([flat] if start else [flat, acc]),
            *[table(*g) for g in groups],
            *[arrived[g][0] for g in groups],
        )

    arrived = {(SELF, SELF): (mix, 0)}
    for lon in (FIRST, SECOND):
        arrived[lon, SELF] = (from_lon(mix, lon), 0)
    mix_1, mix_2 = from_band(mix, FIRST), from_band(mix, SECOND)
    acc = increments(None, [(SELF, SELF), (SECOND, SELF)], False, "own")
    acc, mix_1, mix_2, near = lax.optimization_barrier(
        (acc, mix_1, mix_2, arrived[FIRST, SELF][0])
    )
    arrived[FIRST, SELF] = (near, 0)
    both = jnp.concatenate([mix_1, mix_2], axis=0)
    arrived[SELF, FIRST], arrived[SELF, SECOND] = (mix_1, 0), (mix_2, 0)
    for lon in (FIRST, SECOND):
        there = from_lon(both, lon)
        arrived[lon, FIRST], arrived[lon, SECOND] = (there, 0), (there, 1)
    acc = increments(acc, [(SELF, FIRST), (SELF, SECOND), (FIRST, SELF)], False, "inner")
    acc = increments(acc, [(SECOND, FIRST), (SECOND, SECOND)], False, "outer")
    acc = increments(acc, [(FIRST, FIRST), (FIRST, SECOND)], True, "finish")
    return acc.reshape(members.shape)


def solution(mesh):
    in_specs = (
        P(("band", "lon"), None, None),
        P(("band", "lon"), None, None),
        P(("band", "lon"), None),
        P(("band", "lon"), None),
        P(),
        P(("band", "lon"), None, None),
        P(("band", "lon"), None),
    )
    out_specs = P(("band", "lon"), None, None)
    return jax.shard_map(local, mesh=mesh, in_specs=in_specs, out_specs=out_specs, check_vma=False)
```

time: 96 us -> 88.3 us (0.920); the launches traced: 94.5 us -> 88 us
  starting transfers between devices: 43.7 us -> 29.7 us
  waiting for transfers between devices: 8.85 us -> 16.9 us
    ppermute x16 -> x14, starting transfers between devices: 43.7 us -> 29.7 us  [the longest x8 21.5 us: from_lon(): lax.ppermute(x, 'lon', [((i + step * (1 - 2 * (i % 2))) % count, i) for i...]
    ppermute x16 -> x14, waiting for transfers between devices: 8.85 us -> 16.9 us  [the longest x6 10.6 us: from_band(): return lax.ppermute(x, 'band', [(j, i) for j, i in pairs if 0 <= j < count])]
    pallas_call x3 -> x4, Pallas kernels: 17.1 us -> 19.5 us  [increments(): call(kernel, jax.ShapeDtypeStruct(acc_shape.shape, BF16) if finish else a...]
    pallas_call x1, Pallas kernels: 2.89 us -> 1.27 us  [local(): call(functools.partial(select_kernel, obs_rows), (pool_shape, pool_shape)...]
    unnamed x15 -> x16, local copies, waits for them, and re-layouts: 4.05 us -> 4.08 us
  transfers between devices with their start and end apart: 16 -> 14, of which waited for: 3 -> 7; matrix products, arithmetic and copies ran while one was open for 1% -> 1% of each run, Pallas kernels for 21% -> 25%
where the time goes in v3:
time: 88.3 us; the launch traced here: 88 us
  Pallas kernels  37 us (42%)
  starting transfers between devices  29.7 us (34%)
  waiting for transfers between devices  16.9 us (19%)
  local copies, waits for them, and re-layouts  4.16 us (5%)
    ppermute x8, starting transfers between devices, from_lon(): lax.ppermute(x, 'lon', [((i + step * (1 - 2 * (i % 2))) % count, i) for i...  21.5 us
    pallas_call x4, Pallas kernels, increments(): call(kernel, jax.ShapeDtypeStruct(acc_shape.shape, BF16) if finish else a...  19.5 us
    ppermute x6, waiting for transfers between devices, from_band(): return lax.ppermute(x, 'band', [(j, i) for j, i in pairs if 0 <= j < count])  10.6 us
    pallas_call x1, Pallas kernels, local(): call(functools.partial(mix_kernel, 4, [FIRST * size, SECOND * size]), jax...  8.97 us
    ppermute x6, starting transfers between devices, from_band(): return lax.ppermute(x, 'band', [(j, i) for j, i in pairs if 0 <= j < count])  8.18 us
    ppermute x8, waiting for transfers between devices, from_lon(): lax.ppermute(x, 'lon', [((i + step * (1 - 2 * (i % 2))) % count, i) for i...  6.27 us
    unnamed x16, local copies, waits for them, and re-layouts  4.08 us
    pallas_call x1, Pallas kernels, local(): call(functools.partial(own_gram_kernel, obs_rows, regions), (jax.ShapeDty...  2.65 us
  transfers between devices with their start and end apart: 14, of which 7 were waited for; matrix products, arithmetic and copies ran while one was open for 1% of the time, Pallas kernels for 25%

profile of v3, /device:TPU:4, one launch (start us, length us, event | category | flops | bytes accessed | tf_op | source)
XLA Modules:
  0.0 88.0 jit_solution(6259190029117525087)
XLA Ops:
  0.0 1.2 %collective-permute-start.1 = (bf16[1536,256]{1,0:T(8,128)(2,1)}, bf16[1536,256]{1,0:T(8,128)(2,1)S(1)}, u32[]{:S(2)}, u32[]{:S(2)}) collective-permute-start(bf16[1536,256]{1,0:T(8,128)(2,1)} %bitcast.9), channel_id=1, source_target_pairs={{32,0},{0,32},{96,64},{64,96},{33,1},{1,33},{97,65},{65,97},{34,2}... | collective-permute-start | bytes 2359304 | tf_op jit(solution)/shard_map/ppermute | solution.py:429
  1.2 1.9 %collective-permute-start.2 = (bf16[1536,256]{1,0:T(8,128)(2,1)}, bf16[1536,256]{1,0:T(8,128)(2,1)S(1)}, u32[]{:S(2)}, u32[]{:S(2)}) collective-permute-start(bf16[1536,256]{1,0:T(8,128)(2,1)} %bitcast.10), channel_id=1, source_target_pairs={{64,32},{32,64},{65,33},{33,65},{66,34},{34,66},{67,35},{35,67},{6... | collective-permute-start | bytes 2359304 | tf_op jit(solution)/shard_map/ppermute | solution.py:429
  3.1 0.8 copy.8.innov
  3.9 0.0 copy-start.1
  3.9 1.1 %copy-done.1 = bf16[48,32,256]{2,1,0:T(8,128)(2,1)S(1)} copy-done((bf16[48,32,256]{2,1,0:T(8,128)(2,1)S(1)}, bf16[48,32,256]{2,1,0:T(8,128)(2,1)}, u32[]{:S(2)}) %copy-start.1) | copy-done | bytes 786456
  5.0 0.0 copy-start.3
  5.0 0.7 copy-done.3
  5.8 0.7 copy-done.4
  6.5 0.7 copy-done.5
  7.2 2.2 %tables.1 = (f32[16,256]{1,0:T(8,128)S(1)}, f32[512,128]{1,0:T(8,128)S(1)}, bf16[1536,256]{1,0:T(8,128)(2,1)S(1)}) custom-call(s32[8,64]{1,0:T(8,128)S(1)} %copy-done.4, s32[48,128]{1,0:T(8,128)S(1)} %bitcast.13, f32[8,64]{1,0:T(8,128)S(1)} %copy-done.5, bf16[48,32]{1,0:T(8,128)(2,1)S(1)} %copy.8.innov, bf16[1536,256]{1,0:T(8,128)(2,1)S(1)} %bitcast.11), custom_call_target="tpu_custom_call" | custom-call | flops 1000000000 | bytes 1000000 | tf_op jit(solution)/shard_map/tables/pallas_call | solution.py:451
  9.3 0.1 collective-permute-start
  9.4 6.6 %collective-permute-start.3 = (f32[16,256]{1,0:T(8,128)S(1)}, f32[16,256]{1,0:T(8,128)S(1)}, u32[]{:S(2)}, u32[]{:S(2)}) collective-permute-start(f32[16,256]{1,0:T(8,128)S(1)} %get-tuple-element.21.table.refs_1_), channel_id=1, source_target_pairs={{31,0},{2,1},{1,2},{4,3},{3,4},{6,5},{5,6},{8,7},{7,8},{10,9},{9,1... | collective-permute-start | bytes 49160 | tf_op jit(solution)/shard_map/ppermute | solution.py:435
  16.0 0.0 copy-done.2
  16.0 2.0 %weights.1.refs_2_ = f32[8,4608]{1,0:T(8,128)S(1)} custom-call(f32[512,128]{1,0:T(8,128)S(1)} %get-tuple-element.23.entry_slot, f32[8,32,64]{2,1,0:T(8,128)S(1)} %bitcast.12), custom_call_target="tpu_custom_call" | custom-call | flops 1000000000 | bytes 1000000 | tf_op jit(solution)/shard_map/weights/pallas_call | solution.py:466
  18.0 1.5 %collective-permute-done.1.obs_1 = bf16[1536,256]{1,0:T(8,128)(2,1)S(1)} collective-permute-done((bf16[1536,256]{1,0:T(8,128)(2,1)}, bf16[1536,256]{1,0:T(8,128)(2,1)S(1)}, u32[]{:S(2)}, u32[]{:S(2)}) %collective-permute-start.1) | collective-permute-done | bytes 786464 | tf_op jit(solution)/shard_map/ppermute | solution.py:429
  19.5 2.8 %collective-permute-done.2.obs_2 = bf16[1536,256]{1,0:T(8,128)(2,1)S(1)} collective-permute-done((bf16[1536,256]{1,0:T(8,128)(2,1)}, bf16[1536,256]{1,0:T(8,128)(2,1)S(1)}, u32[]{:S(2)}, u32[]{:S(2)}) %collective-permute-start.2) | collective-permute-done | bytes 786464 | tf_op jit(solution)/shard_map/ppermute | solution.py:429
  22.3 0.0 collective-permute-done.table_2.refs_2_
  22.3 0.0 collective-permute-done.3.table_1.refs_4_
  22.3 1.3 %select.1 = (bf16[1536,256]{1,0:T(8,128)(2,1)S(1)}, bf16[1536,256]{1,0:T(8,128)(2,1)S(1)}) custom-call(bf16[1536,256]{1,0:T(8,128)(2,1)S(1)} %get-tuple-element.22.obs, bf16[1536,256]{1,0:T(8,128)(2,1)S(1)} %collective-permute-done.1.obs_1, bf16[1536,256]{1,0:T(8,128)(2,1)S(1)} %collective-permute-done.2.obs_2, ...), custom_call_target="tpu_custom_call" | custom-call | flops 100000000 | bytes 4000000 | tf_op jit(solution)/shard_map/select/pallas_call | solution.py:477
  23.6 4.8 %collective-permute-start.4 = (bf16[1536,256]{1,0:T(8,128)(2,1)S(1)}, bf16[1536,256]{1,0:T(8,128)(2,1)S(1)}, u32[]{:S(2)}, u32[]{:S(2)}) collective-permute-start(bf16[1536,256]{1,0:T(8,128)(2,1)S(1)} %get-tuple-element.26), channel_id=1, source_target_pairs={{31,0},{2,1},{1,2},{4,3},{3,4},{6,5},{5,6},{8,7},{7,8},{10,9},{9,1... | collective-permute-start | bytes 2359304 | tf_op jit(solution)/shard_map/ppermute | solution.py:435
  28.4 0.0 collective-permute-start.5
  28.4 0.1 collective-permute-start.6
  28.5 2.7 %collective-permute-start.7 = (f32[48,256]{1,0:T(8,128)S(1)}, f32[48,256]{1,0:T(8,128)S(1)}, u32[]{:S(2)}, u32[]{:S(2)}) collective-permute-start(f32[48,256]{1,0:T(8,128)S(1)} %constant_dynamic-update-slice_fusion.metas), channel_id=1, source_target_pairs={{64,32},{32,64},{65,33},{33,65},{66,34},{34,66},{67,35},{35,67},{6... | collective-permute-start | bytes 147464 | tf_op jit(solution)/shard_map/ppermute | solution.py:429
  31.2 2.6 %own_gram.1 = (f32[2048,256]{1,0:T(8,128)S(1)}, bf16[1536,256]{1,0:T(8,128)(2,1)S(1)}) custom-call(bf16[1536,256]{1,0:T(8,128)(2,1)S(1)} %get-tuple-element.22.obs, bf16[1536,256]{1,0:T(8,128)(2,1)S(1)} %collective-permute-done.1.obs_1, bf16[1536,256]{1,0:T(8,128)(2,1)S(1)} %collective-permute-done.2.obs_2, f32[16,256]{1,0:T(8,128)S(1)} %get-tuple-element.21.table.refs_1_, ...), custom_call_target="tpu_custom_call" | custom-call | flops 1610612736 | bytes 5000000 | tf_op jit(solution)/shard_map/own_gram/pallas_call | solution.py:492
  33.9 0.0 collective-permute-done.6.metas_1
  33.9 0.7 collective-permute-done.7.metas_2
  34.5 0.5 innov.2
  35.1 3.3 %collective-permute-done.4.refs_0_ = bf16[1536,256]{1,0:T(8,128)(2,1)S(1)} collective-permute-done((bf16[1536,256]{1,0:T(8,128)(2,1)S(1)}, bf16[1536,256]{1,0:T(8,128)(2,1)S(1)}, u32[]{:S(2)}, u32[]{:S(2)}) %collective-permute-start.4) | collective-permute-done | bytes 786464 | tf_op jit(solution)/shard_map/ppermute | solution.py:435
  38.4 0.0 collective-permute-done.5.refs_1_
  38.4 9.0 %mixing.1.refs_3_ = bf16[2176,128]{1,0:T(8,128)(2,1)S(1)} custom-call(bf16[1536,256]{1,0:T(8,128)(2,1)S(1)} %collective-permute-done.4.refs_0_, bf16[1536,256]{1,0:T(8,128)(2,1)S(1)} %collective-permute-done.5.refs_1_, f32[8,4608]{1,0:T(8,128)S(1)} %weights.1.refs_2_, f32[2048,256]{1,0:T(8,128)S(1)} %get-tuple-element.29.refs_3_, ...), custom_call_target="tpu_custom_call" | custom-call | flops 6442450944 | bytes 4000000 | tf_op jit(solution)/shard_map/mixing/pallas_call | solution.py:512
  47.4 0.1 collective-permute-start.8
  47.5 0.1 collective-permute-start.9
  47.6 2.2 %collective-permute-start.10 = (bf16[2176,128]{1,0:T(8,128)(2,1)S(1)}, bf16[2176,128]{1,0:T(8,128)(2,1)S(1)}, u32[]{:S(2)}, u32[]{:S(2)}) collective-permute-start(bf16[2176,128]{1,0:T(8,128)(2,1)S(1)} %mixing.1.refs_3_), channel_id=1, source_target_pairs={{64,32},{32,64},{65,33},{33,65},{66,34},{34,66},{67,35},{35,67},{6... | collective-permute-start | bytes 1671176 | tf_op jit(solution)/shard_map/ppermute | solution.py:429
  49.8 5.1 %collective-permute-start.11 = (bf16[2176,128]{1,0:T(8,128)(2,1)S(1)}, bf16[2176,128]{1,0:T(8,128)(2,1)S(1)}, u32[]{:S(2)}, u32[]{:S(2)}) collective-permute-start(bf16[2176,128]{1,0:T(8,128)(2,1)S(1)} %mixing.1.refs_3_), channel_id=1, source_target_pairs={{31,0},{2,1},{1,2},{4,3},{3,4},{6,5},{5,6},{8,7},{7,8},{10,9},{9,1... | collective-permute-start | bytes 1671176 | tf_op jit(solution)/shard_map/ppermute | solution.py:435
  54.8 0.0 collective-permute-done.8.refs_4_
  54.8 0.0 copy-done
  54.9 3.9 %own.1.refs_1_ = f32[2304,256]{1,0:T(8,128)S(1)} custom-call(bf16[2304,256]{1,0:T(8,128)(2,1)S(1)} %bitcast.5, f32[16,256]{1,0:T(8,128)S(1)} %get-tuple-element.21.table.refs_1_, f32[16,256]{1,0:T(8,128)S(1)} %collective-permute-done.table_2.refs_2_, bf16[2176,128]{1,0:T(8,128)(2,1)S(1)} %mixing.1.refs_3_, bf16[2176,128]{1,0:T(8,128)(2,1)S(1)} %collective-permute-done.8.refs_4_), custom_call_target="tpu_custom_call" | custom-call | flops 1610612736 | bytes 6000000 | tf_op jit(solution)/shard_map/own/pallas_call | solution.py:548
  58.7 3.8 %collective-permute-done.9.refs_5_ = bf16[2176,128]{1,0:T(8,128)(2,1)S(1)} collective-permute-done((bf16[2176,128]{1,0:T(8,128)(2,1)S(1)}, bf16[2176,128]{1,0:T(8,128)(2,1)S(1)}, u32[]{:S(2)}, u32[]{:S(2)}) %collective-permute-start.9) | collective-permute-done | bytes 557088 | tf_op jit(solution)/shard_map/ppermute | solution.py:429
  62.5 1.9 %collective-permute-done.10.refs_6_ = bf16[2176,128]{1,0:T(8,128)(2,1)S(1)} collective-permute-done((bf16[2176,128]{1,0:T(8,128)(2,1)S(1)}, bf16[2176,128]{1,0:T(8,128)(2,1)S(1)}, u32[]{:S(2)}, u32[]{:S(2)}) %collective-permute-start.10) | collective-permute-done | bytes 557088 | tf_op jit(solution)/shard_map/ppermute | solution.py:429
  64.4 0.0 collective-permute-done.11.refs_7_
  64.5 0.1 constant_dynamic-update-slice_fusion.3
  64.5 0.1 collective-permute-start.12
  64.6 4.8 %collective-permute-start.13 = (bf16[4352,128]{1,0:T(8,128)(2,1)S(1)}, bf16[4352,128]{1,0:T(8,128)(2,1)S(1)}, u32[]{:S(2)}, u32[]{:S(2)}) collective-permute-start(bf16[4352,128]{1,0:T(8,128)(2,1)S(1)} %constant_dynamic-update-slice_fusion.3), channel_id=1, source_target_pairs={{31,0},{2,1},{1,2},{4,3},{3,4},{6,5},{5,6},{8,7},{7,8},{10,9},{9,1... | collective-permute-start | bytes 3342344 | tf_op jit(solution)/shard_map/ppermute | solution.py:435
  69.5 6.7 %inner.1.refs_1_ = f32[2304,256]{1,0:T(8,128)S(1)} custom-call(bf16[2304,256]{1,0:T(8,128)(2,1)S(1)} %bitcast.6, f32[2304,256]{1,0:T(8,128)S(1)} %own.1.refs_1_, f32[16,256]{1,0:T(8,128)S(1)} %get-tuple-element.42.refs_2_, f32[16,256]{1,0:T(8,128)S(1)} %get-tuple-element.39.refs_3_, f32[16,256]{1,0:T(8,128)S(1)} %collective-permute-done.3.table_1.refs_4_, ...), custom_call_target="tpu_custom_call" | custom-call | flops 2415919104 | bytes 6000000 | tf_op jit(solution)/shard_map/inner/pallas_call | solution.py:548
  76.2 0.0 collective-permute-done.12.refs_4_.refs_5_
  76.2 3.9 %outer.1.refs_1_ = f32[2304,256]{1,0:T(8,128)S(1)} custom-call(bf16[2304,256]{1,0:T(8,128)(2,1)S(1)} %bitcast.7, f32[2304,256]{1,0:T(8,128)S(1)} %inner.1.refs_1_, f32[16,256]{1,0:T(8,128)S(1)} %get-tuple-element.41.refs_2_, f32[16,256]{1,0:T(8,128)S(1)} %get-tuple-element.38.refs_3_, bf16[4352,128]{1,0:T(8,128)(2,1)S(1)} %collective-permute-done.12.refs_4_.refs_5_, ...), custom_call_target="tpu_custom_call" | custom-call | flops 1610612736 | bytes 6000000 | tf_op jit(solution)/shard_map/outer/pallas_call | solution.py:548
  80.0 2.9 %collective-permute-done.13.refs_4_.refs_5_ = bf16[4352,128]{1,0:T(8,128)(2,1)S(1)} collective-permute-done((bf16[4352,128]{1,0:T(8,128)(2,1)S(1)}, bf16[4352,128]{1,0:T(8,128)(2,1)S(1)}, u32[]{:S(2)}, u32[]{:S(2)}) %collective-permute-start.13) | collective-permute-done | bytes 1114144 | tf_op jit(solution)/shard_map/ppermute | solution.py:435
  83.0 5.0 %finish.1 = bf16[2304,256]{1,0:T(8,128)(2,1)} custom-call(bf16[2304,256]{1,0:T(8,128)(2,1)S(1)} %bitcast.8, f32[2304,256]{1,0:T(8,128)S(1)} %outer.1.refs_1_, f32[16,256]{1,0:T(8,128)S(1)} %get-tuple-element.40.refs_2_, f32[16,256]{1,0:T(8,128)S(1)} %get-tuple-element.37.refs_3_, bf16[4352,128]{1,0:T(8,128)(2,1)S(1)} %collective-permute-done.13.refs_4_.refs_5_, ...), custom_call_target="tpu_custom_call" | custom-call | flops 1610612736 | bytes 6000000 | tf_op jit(solution)/shard_map/finish/pallas_call | solution.py:548
  (10 shorter events, 0.1 us)
Async XLA Ops:
  0.0 19.5 %collective-permute-start.1 = (bf16[1536,256]{1,0:T(8,128)(2,1)}, bf16[1536,256]{1,0:T(8,128)(2,1)S(1)}, u32[]{:S(2)}, u32[]{:S(2)}) collective-permute-start(bf16[1536,256]{1,0:T(8,128)(2,1)} %bitcast.9), channel_id=1, source_target_pairs={{32,0},{0,32},{96,64},{64,96},{33,1},{1,33},{97,65},{65,97},{34,2}... | collective-permute-start | bytes 2359304 | tf_op jit(solution)/shard_map/ppermute | solution.py:429
  1.2 21.1 %collective-permute-start.2 = (bf16[1536,256]{1,0:T(8,128)(2,1)}, bf16[1536,256]{1,0:T(8,128)(2,1)S(1)}, u32[]{:S(2)}, u32[]{:S(2)}) collective-permute-start(bf16[1536,256]{1,0:T(8,128)(2,1)} %bitcast.10), channel_id=1, source_target_pairs={{64,32},{32,64},{65,33},{33,65},{66,34},{34,66},{67,35},{35,67},{6... | collective-permute-start | bytes 2359304 | tf_op jit(solution)/shard_map/ppermute | solution.py:429
  3.9 1.1 %copy-start.1 = (bf16[48,32,256]{2,1,0:T(8,128)(2,1)S(1)}, bf16[48,32,256]{2,1,0:T(8,128)(2,1)}, u32[]{:S(2)}) copy-start(bf16[48,32,256]{2,1,0:T(8,128)(2,1)} %param.8) | copy-start | bytes 2359300
  5.0 0.7 copy-start.3
  5.8 0.7 copy-start.4
  6.5 0.7 copy-start.5
  7.2 8.9 %copy-start.2 = (f32[8,64,32]{1,2,0:T(8,128)S(1)}, f32[8,64,32]{1,2,0:T(8,128)}, u32[]{:S(2)}) copy-start(f32[8,64,32]{1,2,0:T(8,128)} %param.12) | copy-start | bytes 196612
  9.3 13.0 %collective-permute-start = (f32[16,256]{1,0:T(8,128)S(1)}, f32[16,256]{1,0:T(8,128)S(1)}, u32[]{:S(2)}, u32[]{:S(2)}) collective-permute-start(f32[16,256]{1,0:T(8,128)S(1)} %get-tuple-element.21.table.refs_1_), channel_id=1, source_target_pairs={{1,0},{0,1},{3,2},{2,3},{5,4},{4,5},{7,6},{6,7},{9,8},{8,9},{11,10... | collective-permute-start | bytes 49160 | tf_op jit(solution)/shard_map/ppermute | solution.py:435
  9.4 12.9 %collective-permute-start.3 = (f32[16,256]{1,0:T(8,128)S(1)}, f32[16,256]{1,0:T(8,128)S(1)}, u32[]{:S(2)}, u32[]{:S(2)}) collective-permute-start(f32[16,256]{1,0:T(8,128)S(1)} %get-tuple-element.21.table.refs_1_), channel_id=1, source_target_pairs={{31,0},{2,1},{1,2},{4,3},{3,4},{6,5},{5,6},{8,7},{7,8},{10,9},{9,1... | collective-permute-start | bytes 49160 | tf_op jit(solution)/shard_map/ppermute | solution.py:435
  23.6 14.8 %collective-permute-start.4 = (bf16[1536,256]{1,0:T(8,128)(2,1)S(1)}, bf16[1536,256]{1,0:T(8,128)(2,1)S(1)}, u32[]{:S(2)}, u32[]{:S(2)}) collective-permute-start(bf16[1536,256]{1,0:T(8,128)(2,1)S(1)} %get-tuple-element.26), channel_id=1, source_target_pairs={{31,0},{2,1},{1,2},{4,3},{3,4},{6,5},{5,6},{8,7},{7,8},{10,9},{9,1... | collective-permute-start | bytes 2359304 | tf_op jit(solution)/shard_map/ppermute | solution.py:435
  28.4 10.0 %collective-permute-start.5 = (bf16[1536,256]{1,0:T(8,128)(2,1)S(1)}, bf16[1536,256]{1,0:T(8,128)(2,1)S(1)}, u32[]{:S(2)}, u32[]{:S(2)}) collective-permute-start(bf16[1536,256]{1,0:T(8,128)(2,1)S(1)} %get-tuple-element.27), channel_id=1, source_target_pairs={{1,0},{0,1},{3,2},{2,3},{5,4},{4,5},{7,6},{6,7},{9,8},{8,9},{11,10... | collective-permute-start | bytes 2359304 | tf_op jit(solution)/shard_map/ppermute | solution.py:435
  28.4 5.5 %collective-permute-start.6 = (f32[48,256]{1,0:T(8,128)S(1)}, f32[48,256]{1,0:T(8,128)S(1)}, u32[]{:S(2)}, u32[]{:S(2)}) collective-permute-start(f32[48,256]{1,0:T(8,128)S(1)} %constant_dynamic-update-slice_fusion.metas), channel_id=1, source_target_pairs={{32,0},{0,32},{96,64},{64,96},{33,1},{1,33},{97,65},{65,97},{34,2}... | collective-permute-start | bytes 147464 | tf_op jit(solution)/shard_map/ppermute | solution.py:429
  28.5 6.0 %collective-permute-start.7 = (f32[48,256]{1,0:T(8,128)S(1)}, f32[48,256]{1,0:T(8,128)S(1)}, u32[]{:S(2)}, u32[]{:S(2)}) collective-permute-start(f32[48,256]{1,0:T(8,128)S(1)} %constant_dynamic-update-slice_fusion.metas), channel_id=1, source_target_pairs={{64,32},{32,64},{65,33},{33,65},{66,34},{34,66},{67,35},{35,67},{6... | collective-permute-start | bytes 147464 | tf_op jit(solution)/shard_map/ppermute | solution.py:429
  38.4 16.5 %copy-start = (bf16[48,48,256]{2,1,0:T(8,128)(2,1)S(1)}, bf16[48,48,256]{2,1,0:T(8,128)(2,1)}, u32[]{:S(2)}) copy-start(bf16[48,48,256]{2,1,0:T(8,128)(2,1)} %param.7) | copy-start | bytes 3538948
  47.4 7.5 %collective-permute-start.8 = (bf16[2176,128]{1,0:T(8,128)(2,1)S(1)}, bf16[2176,128]{1,0:T(8,128)(2,1)S(1)}, u32[]{:S(2)}, u32[]{:S(2)}) collective-permute-start(bf16[2176,128]{1,0:T(8,128)(2,1)S(1)} %mixing.1.refs_3_), channel_id=1, source_target_pairs={{1,0},{0,1},{3,2},{2,3},{5,4},{4,5},{7,6},{6,7},{9,8},{8,9},{11,10... | collective-permute-start | bytes 1671176 | tf_op jit(solution)/shard_map/ppermute | solution.py:435
  47.5 15.0 %collective-permute-start.9 = (bf16[2176,128]{1,0:T(8,128)(2,1)S(1)}, bf16[2176,128]{1,0:T(8,128)(2,1)S(1)}, u32[]{:S(2)}, u32[]{:S(2)}) collective-permute-start(bf16[2176,128]{1,0:T(8,128)(2,1)S(1)} %mixing.1.refs_3_), channel_id=1, source_target_pairs={{32,0},{0,32},{96,64},{64,96},{33,1},{1,33},{97,65},{65,97},{34,2}... | collective-permute-start | bytes 1671176 | tf_op jit(solution)/shard_map/ppermute | solution.py:429
  47.6 16.9 %collective-permute-start.10 = (bf16[2176,128]{1,0:T(8,128)(2,1)S(1)}, bf16[2176,128]{1,0:T(8,128)(2,1)S(1)}, u32[]{:S(2)}, u32[]{:S(2)}) collective-permute-start(bf16[2176,128]{1,0:T(8,128)(2,1)S(1)} %mixing.1.refs_3_), channel_id=1, source_target_pairs={{64,32},{32,64},{65,33},{33,65},{66,34},{34,66},{67,35},{35,67},{6... | collective-permute-start | bytes 1671176 | tf_op jit(solution)/shard_map/ppermute | solution.py:429
  49.8 14.6 %collective-permute-start.11 = (bf16[2176,128]{1,0:T(8,128)(2,1)S(1)}, bf16[2176,128]{1,0:T(8,128)(2,1)S(1)}, u32[]{:S(2)}, u32[]{:S(2)}) collective-permute-start(bf16[2176,128]{1,0:T(8,128)(2,1)S(1)} %mixing.1.refs_3_), channel_id=1, source_target_pairs={{31,0},{2,1},{1,2},{4,3},{3,4},{6,5},{5,6},{8,7},{7,8},{10,9},{9,1... | collective-permute-start | bytes 1671176 | tf_op jit(solution)/shard_map/ppermute | solution.py:435
  64.5 11.6 %collective-permute-start.12 = (bf16[4352,128]{1,0:T(8,128)(2,1)S(1)}, bf16[4352,128]{1,0:T(8,128)(2,1)S(1)}, u32[]{:S(2)}, u32[]{:S(2)}) collective-permute-start(bf16[4352,128]{1,0:T(8,128)(2,1)S(1)} %constant_dynamic-update-slice_fusion.3), channel_id=1, source_target_pairs={{1,0},{0,1},{3,2},{2,3},{5,4},{4,5},{7,6},{6,7},{9,8},{8,9},{11,10... | collective-permute-start | bytes 3342344 | tf_op jit(solution)/shard_map/ppermute | solution.py:435
  64.6 18.3 %collective-permute-start.13 = (bf16[4352,128]{1,0:T(8,128)(2,1)S(1)}, bf16[4352,128]{1,0:T(8,128)(2,1)S(1)}, u32[]{:S(2)}, u32[]{:S(2)}) collective-permute-start(bf16[4352,128]{1,0:T(8,128)(2,1)S(1)} %constant_dynamic-update-slice_fusion.3), channel_id=1, source_target_pairs={{31,0},{2,1},{1,2},{4,3},{3,4},{6,5},{5,6},{8,7},{7,8},{10,9},{9,1... | collective-permute-start | bytes 3342344 | tf_op jit(solution)/shard_map/ppermute | solution.py:435

commit v4 on v3

--- a/solution.py
+++ b/solution.py
@@ -23,6 +23,7 @@
 BF16 = jnp.bfloat16
 VMEM_SPEC = pl.BlockSpec(memory_space=pltpu.VMEM)
 SMEM_SPEC = pl.BlockSpec(memory_space=pltpu.SMEM)
+HBM_SPEC = pl.BlockSpec(memory_space=pltpu.HBM)
 
 
 def dot(a, b):
@@ -58,12 +59,21 @@
     )
 
 
-def table_kernel(shape, lists, placement, state, innov, obs, meta, entry_slot, obs_copy):
+def table_kernel(shape, *refs):
     lon_count, blocks = shape
+    sources, (meta, entry_slot, obs), copies, sems = refs[:5], refs[5:8], refs[8:12], refs[12]
+    transfers = [
+        pltpu.make_async_copy(source, to, sems.at[k])
+        for k, (source, to) in enumerate(zip(sources, copies + (obs,)))
+    ]
+    for transfer in transfers:
+        transfer.start()
+    for transfer in transfers[:-1]:
+        transfer.wait()
+    lists, placement, state, innov = copies
     regions, list_len = lists.shape
     entries = regions * list_len
     obs_rows = innov.shape[1]
-    obs_copy[...] = obs[...]
     p = lax.broadcasted_iota(jnp.int32, (obs_rows, META_LANES), 0)
     q = lax.broadcasted_iota(jnp.int32, (obs_rows, META_LANES), 1) % obs_rows
     repeated = dot(innov[...], jnp.where(p == q, 1.0, 0.0).astype(BF16))
@@ -137,6 +147,7 @@
             meta[r : r + 1, 128 * c : 128 * (c + 1)] = jnp.sum(
                 hit[r * list_len : (r + 1) * list_len], axis=0, keepdims=True
             )
+    transfers[-1].wait()
 
 
 def weight_kernel(regions, list_len, entry_slot, taper, weights):
@@ -185,17 +196,23 @@
     )
 
 
-def own_gram_kernel(obs_rows, regions, obs, obs_1, obs_2, table, weights, gram, pool):
+def near_gram_kernel(obs_rows, regions, obs, obs_1, obs_2, pool_2, table, weights, gram, pool):
     gather_blocks((obs, obs_1, obs_2), table, SELF * BAND_SLOTS, obs_rows, pool)
-    y = pool[...]
-    y_t = transposed(y)
-    first = SELF * BAND_SLOTS * obs_rows
-    w16 = weights[:, first : first + y.shape[0]].astype(BF16)
+    size = pool.shape[0]
+    parts = [(y[...], transposed(y[...]), at * size) for y, at in ((pool, SELF), (pool_2, SECOND))]
     for r in range(regions):
-        gram[256 * r : 256 * (r + 1), :] = dot(y_t * w16[r : r + 1, :], y)
-
-
-def innov_kernel(obs_rows, regions, blocks, metas, metas_1, metas_2, weights, pool, scaled, proj):
+        gram[256 * r : 256 * (r + 1), :] = gram_of(r, weights, parts)
+
+
+def gram_of(r, weights, parts):
+    products = [
+        dot(y_t * weights[r : r + 1, lane : lane + y.shape[0]].astype(BF16), y)
+        for y, y_t, lane in parts
+    ]
+    return sum(products[1:], products[0])
+
+
+def innov_kernel(obs_rows, regions, blocks, metas, metas_1, metas_2, weights, pool, pool_2, scaled, proj):
     down = lax.broadcasted_iota(jnp.int32, (blocks, META_LANES), 0).astype(F32)
     mine = metas[META_ROWS * SELF + BLOCK_ROW : META_ROWS * SELF + BLOCK_ROW + 1, :]
     hot = jnp.where(down == mine, 1.0, 0.0).T.astype(BF16)
@@ -221,8 +238,9 @@
     high = wd.astype(BF16)
     both = jnp.concatenate([high.astype(F32), wd - high.astype(F32)], axis=0).astype(BF16)
     scaled[...] = both
-    first = SELF * BAND_SLOTS * obs_rows
-    part = dot(both[:, first : first + pool.shape[0]], pool[...])
+    size = pool.shape[0]
+    part = dot(both[:, SELF * size : (SELF + 1) * size], pool[...])
+    part = part + dot(both[:, SECOND * size : (SECOND + 1) * size], pool_2[...])
     proj[...] = part[:regions] + part[regions:]
 
 
@@ -243,7 +261,7 @@
     return jnp.sum(jnp.sum(both, axis=0, keepdims=True), axis=1, keepdims=True)
 
 
-def roots(grams, proj_rows, eye, ensemble):
+def roots(grams, proj_rows, eye, ensemble, between):
     each = range(len(grams))
     base = ensemble - 1.0
     scale = [
@@ -266,6 +284,7 @@
         u2 = [dot(ub[i], ub[i]) for i in each]
         w = [((1.5 + 1.5 * c[i]) * u[i] + u2[i]).astype(BF16) for i in each]
         u3 = [dot(ub[i], w[i]) for i in each]
+        between()
         u = [(1.5 * c[i] + 0.75 * c[i] * c[i]) * u[i] + u3[i] for i in each]
         c = [(0.75 + 0.25 * c[i]) * c[i] * c[i] for i in each]
         ub = [u[i].astype(BF16) for i in each]
@@ -285,6 +304,13 @@
     wbar = [times(i, half[i]) * inverse[i] for i in each]
     factor = [lax.sqrt(base * inverse[i]) for i in each]
     return [(factor[i], factor[i] * a[i] - 1.0, g[i]) for i in each], wbar
+
+
+EXTRAS = 5
+
+
+def packed_rows(regions):
+    return regions * 256 + -(-EXTRAS * regions // 16) * 16
 
 
 def pack(matrix, wbar, eye, upper):
@@ -296,60 +322,60 @@
     merged = jnp.where(upper, left, corner)
     high = wbar.astype(BF16).astype(F32)
     low = wbar - high
-    rows = [
+    extra = [
         jnp.sum(corner * eye, axis=0, keepdims=True),
         high[:, :128],
         high[:, 128:],
         low[:, :128],
         low[:, 128:],
     ]
-    down = lax.broadcasted_iota(jnp.int32, (16, 128), 0)
-    extra = jnp.zeros((16, 128), F32)
-    for k, r in enumerate(rows):
-        extra = jnp.where(down == k, r, extra)
-    return right.astype(BF16), merged.astype(BF16), extra.astype(BF16)
-
-
-def mix_regions(first, count, gram, proj, packed):
+    return right.astype(BF16), merged.astype(BF16), extra
+
+
+def mix_regions(first, count, gram, proj, packed, between):
     n = 256
-    extras = n * proj.shape[0]
     down = lax.broadcasted_iota(jnp.int32, (128, 128), 0)
     across = lax.broadcasted_iota(jnp.int32, (128, 128), 1)
     eye = jnp.where(down == across, 1.0, 0.0)
     some = range(first, first + count)
     matrices, weights = roots(
-        [gram[r - first] for r in some], [proj[r : r + 1, :] for r in some], eye, n
-    )
+        [gram[r - first] for r in some], [proj[r : r + 1, :] for r in some], eye, n, between
+    )
+    extras = []
     for k, r in enumerate(some):
         right, merged, extra = pack(matrices[k], weights[k], eye, down <= across)
         packed[n * r : n * r + 128, :] = right
         packed[n * r + 128 : n * (r + 1), :] = merged
-        packed[extras + 16 * r : extras + 16 * (r + 1), :] = extra
-
-
-def grams_of(first, count, gram_own, weights, parts):
-    out = []
-    for r in range(first, first + count):
-        total_r = gram_own[256 * r : 256 * (r + 1), :]
-        for y, y_t, lane in parts:
-            w16 = weights[r : r + 1, lane : lane + y.shape[0]].astype(BF16)
-            total_r = total_r + dot(y_t * w16, y)
-        out.append(total_r)
-    return out
-
-
-def mix_kernel(together, lanes, *refs):
-    pools, refs = refs[: len(lanes)], refs[len(lanes) :]
-    weights, gram_own, scaled, proj_own, packed, proj = refs
+        extras.append(extra)
+    return extras
+
+
+def mix_kernel(together, pool, weights, gram_near, scaled, proj_near, packed, proj):
     regions = proj.shape[0]
-    part = sum(
-        dot(scaled[:, lane : lane + y.shape[0]], y[...]) for y, lane in zip(pools, lanes)
-    )
-    proj[...] = proj_own[...] + part[:regions] + part[regions:]
-    parts = [(y[...], transposed(y[...]), lane) for y, lane in zip(pools, lanes)]
+    size = pool.shape[0]
+    part = dot(scaled[:, FIRST * size : (FIRST + 1) * size], pool[...])
+    proj[...] = proj_near[...] + part[:regions] + part[regions:]
+    parts = [(pool[...], transposed(pool[...]), FIRST * size)]
+
+    def gram(r):
+        return gram_near[256 * r : 256 * (r + 1), :] + gram_of(r, weights, parts)
+
+    extras = []
+    ready = [gram(r) for r in range(together)]
     for first in range(0, regions, together):
-        grams = grams_of(first, together, gram_own, weights, parts)
-        mix_regions(first, together, grams, proj, packed)
+        later = []
+        rest = list(range(first + together, min(first + 2 * together, regions)))
+
+        def between(rest=rest, later=later):
+            if rest:
+                later.append(gram(rest.pop(0)))
+
+        extras += mix_regions(first, together, ready, proj, packed, between)
+        ready = later + [gram(r) for r in rest]
+    rows = packed.shape[0] - 256 * regions
+    below = jnp.zeros((rows - EXTRAS * regions, 128), F32)
+    stacked = [extras[r][k] for k in range(EXTRAS) for r in range(regions)] + [below]
+    packed[256 * regions :, :] = jnp.concatenate(stacked, axis=0).astype(BF16)
 
 
 def unpack(count, packed, full):
@@ -358,19 +384,21 @@
     across = lax.broadcasted_iota(jnp.int32, (128, 128), 1)
     upper = down <= across
     lower = down > across
-    extra = packed[n * count : (n + 16) * count, :].astype(F32)
-    columns = extra.T.astype(BF16)
+    extra = packed[n * count :, :].astype(F32)
+    below = jnp.zeros((128 - extra.shape[0], 128), F32)
+    columns = jnp.concatenate([extra, below], axis=0).T.astype(BF16)
 
     def spread(k):
-        return dot(columns, jnp.where((down == k) | (down == k + 2), 1.0, 0.0).astype(BF16))
+        both = (down == k) | (down == k + 2 * count)
+        return dot(columns, jnp.where(both, 1.0, 0.0).astype(BF16))
 
     for k in range(count):
         right = packed[n * k : n * k + 128, :].astype(F32)
         merged = packed[n * k + 128 : n * (k + 1), :].astype(F32)
         turned = merged.T
-        top = spread(16 * k + 1)
-        low = spread(16 * k + 2)
-        diagonal = extra[16 * k : 16 * k + 1]
+        top = spread(count + k)
+        low = spread(2 * count + k)
+        diagonal = extra[k : k + 1]
         corner = jnp.where(lower, merged, jnp.where(down == across, diagonal, turned))
         full[n * k : n * k + 128, :128] = (jnp.where(upper, merged, turned) + top).astype(BF16)
         full[n * k : n * k + 128, 128:] = (right + top).astype(BF16)
@@ -378,13 +406,15 @@
         full[n * k + 128 : n * (k + 1), 128:] = (corner + low).astype(BF16)
 
 
-def add_increment(members, table, first_slot, packed, count, acc, left, full, state_rows):
-    n = members.shape[1]
-    unpack(count, packed, full)
-    places = [
+def block_places(table, first_slot, state_rows):
+    return [
         pl.multiple_of(table[BLOCK_ROW, first_slot + i].astype(jnp.int32) * state_rows, state_rows)
         for i in range(CAP)
     ]
+
+
+def scale_members(members, table, first_slot, places, count, left, state_rows):
+    n = members.shape[1]
     for i in range(CAP):
         x = members[pl.ds(places[i], state_rows), :]
         for k in range(count):
@@ -395,31 +425,47 @@
                         state_rows * i + 16 * u : state_rows * i + 16 * (u + 1),
                         n * k + 128 * v : n * k + 128 * (v + 1),
                     ] = x[16 * u : 16 * (u + 1), 128 * v : 128 * (v + 1)] * t
+
+
+def add_products(left, full, places, acc, state_rows):
     product = dot(left[...], full[...])
     for i in range(CAP):
         acc[pl.ds(places[i], state_rows), :] += product[state_rows * i : state_rows * (i + 1), :]
 
 
-def increment_kernel(slots, halves, start, finish, state_rows, count, *refs):
+def increment_kernel(slots, halves, next_slots, start, state_rows, count, *refs):
     refs = list(refs)
     members = refs.pop(0)
     before = None if start else refs.pop(0)
-    items = len(slots)
-    tables, packed, refs = refs[:items], refs[items : 2 * items], refs[2 * items :]
-    rows = count * (members.shape[1] + 16)
-    if finish:
-        out, acc = refs[:2]
-        scratch = refs[2:]
-    else:
-        acc = refs[0]
-        scratch = refs[1:]
+    items, ahead = len(slots), len(next_slots)
+    tables, refs = refs[: items + ahead], refs[items + ahead :]
+    packed, refs = refs[:items], refs[items:]
+    acc, lefts, scratch = refs[0], refs[1 : 1 + ahead], refs[1 + ahead :]
+    rows = packed_rows(count)
     acc[...] = members[...].astype(F32) if start else before[...]
     for k, slot in enumerate(slots):
         left, full = scratch[2 * (k % 2) : 2 * (k % 2) + 2]
-        mixes = packed[k].at[rows * halves[k] : rows * (halves[k] + 1), :]
-        add_increment(members, tables[k], slot, mixes, count, acc, left, full, state_rows)
-    if finish:
-        out[...] = acc[...].astype(BF16)
+        places = block_places(tables[k], slot, state_rows)
+        unpack(count, packed[k].at[rows * halves[k] : rows * (halves[k] + 1), :], full)
+        scale_members(members, tables[k], slot, places, count, left, state_rows)
+        add_products(left, full, places, acc, state_rows)
+    for k, slot in enumerate(next_slots):
+        table = tables[items + k]
+        places = block_places(table, slot, state_rows)
+        scale_members(members, table, slot, places, count, lefts[k], state_rows)
+
+
+def finish_kernel(slots, halves, state_rows, count, before, *refs):
+    items = len(slots)
+    tables, packed, lefts = refs[:items], refs[items : 2 * items], refs[2 * items : 3 * items]
+    out, acc, *fulls = refs[3 * items :]
+    rows = packed_rows(count)
+    acc[...] = before[...]
+    for k in range(items):
+        unpack(count, packed[k].at[rows * halves[k] : rows * (halves[k] + 1), :], fulls[k])
+        places = block_places(tables[k], slots[k], state_rows)
+        add_products(lefts[k], fulls[k], places, acc, state_rows)
+    out[...] = acc[...].astype(BF16)
 
 
 def from_band(x, place):
@@ -455,10 +501,17 @@
             jax.ShapeDtypeStruct((entries, 128), F32),
             jax.ShapeDtypeStruct(obs.shape, BF16),
         ),
-        [VMEM_SPEC] * 5,
+        [HBM_SPEC] * 5,
         "tables",
         10**9,
         10**6,
+        [
+            pltpu.VMEM(lists.shape, jnp.int32),
+            pltpu.VMEM((placement.shape[0] // 128, 128), jnp.int32),
+            pltpu.VMEM(state_taper.shape, F32),
+            pltpu.VMEM(innovations.shape, BF16),
+            pltpu.SemaphoreType.DMA((5,)),
+        ],
     )(lists, placement.reshape(-1, 128), state_taper, innovations, obs)
     meta_1 = from_lon(meta, FIRST)
     meta_2 = from_lon(meta, SECOND)
@@ -471,7 +524,7 @@
         10**9,
         10**6,
     )(entry_slot, jnp.swapaxes(obs_taper, 1, 2))
-    obs_1, obs_2, weights = lax.optimization_barrier((obs_1, obs_2, weights))
+    obs_2, obs_1, weights = lax.optimization_barrier((obs_2, obs_1, weights))
     size = BAND_SLOTS * obs_rows
     pool_shape = jax.ShapeDtypeStruct((size, n), BF16)
     to_1, to_2 = call(
@@ -489,35 +542,33 @@
     metas_2 = from_band(metas, SECOND)
 
     region_flops = 2 * n**3
-    gram_own, pool = call(
-        functools.partial(own_gram_kernel, obs_rows, regions),
-        (
-            jax.ShapeDtypeStruct((regions * n, n), F32),
-            pool_shape,
-        ),
-        [VMEM_SPEC] * 3 + [SMEM_SPEC] + [VMEM_SPEC],
-        "own_gram",
-        regions * 6 * region_flops,
+    gram_near, pool = call(
+        functools.partial(near_gram_kernel, obs_rows, regions),
+        (jax.ShapeDtypeStruct((regions * n, n), F32), pool_shape),
+        [VMEM_SPEC] * 4 + [SMEM_SPEC] + [VMEM_SPEC],
+        "near_gram",
+        regions * 12 * region_flops,
         5 * 10**6,
-    )(obs, obs_1, obs_2, meta, weights)
+    )(obs, obs_1, obs_2, pool_2, meta, weights)
+    metas_2, metas_1, pool = lax.optimization_barrier((metas_2, metas_1, pool))
     proj_shape = jax.ShapeDtypeStruct((regions, n), F32)
-    scaled, proj_own = call(
+    scaled, proj_near = call(
         functools.partial(innov_kernel, obs_rows, regions, blocks),
         (jax.ShapeDtypeStruct((2 * regions, 3 * size), BF16), proj_shape),
-        [VMEM_SPEC] * 5,
+        [VMEM_SPEC] * 6,
         "innov",
         10**8,
         2 * 10**6,
-    )(metas, metas_1, metas_2, weights, pool)
+    )(metas, metas_1, metas_2, weights, pool, pool_2)
     mix = call(
-        functools.partial(mix_kernel, 4, [FIRST * size, SECOND * size]),
-        jax.ShapeDtypeStruct((regions * (n + 16), 128), BF16),
-        [VMEM_SPEC] * 6,
+        functools.partial(mix_kernel, 4),
+        jax.ShapeDtypeStruct((packed_rows(regions), 128), BF16),
+        [VMEM_SPEC] * 5,
         "mixing",
-        regions * 24 * region_flops,
+        regions * 18 * region_flops,
         4 * 10**6,
         [pltpu.VMEM(proj_shape.shape, F32)],
-    )(pool_1, pool_2, weights, gram_own, scaled, proj_own)
+    )(pool_1, weights, gram_near, scaled, proj_near)
 
     stacked = (metas, metas_1, metas_2)
 
@@ -534,40 +585,43 @@
         pltpu.VMEM((regions * n, n), BF16),
     ] * 2
 
-    def increments(acc, groups, finish, name):
+    left_shape = jax.ShapeDtypeStruct((CAP * state_rows, regions * n), BF16)
+
+    def increments(acc, groups, ahead, name):
         start = acc is None
         kernel = functools.partial(
             increment_kernel,
             [slots(*g) for g in groups],
             [arrived[g][1] for g in groups],
+            [slots(*g) for g in ahead],
             start,
-            finish,
             state_rows,
             regions,
         )
         return call(
             kernel,
-            jax.ShapeDtypeStruct(acc_shape.shape, BF16) if finish else acc_shape,
+            (acc_shape,) + (left_shape,) * len(ahead),
             [VMEM_SPEC] * (1 if start else 2)
-            + [SMEM_SPEC] * len(groups)
+            + [SMEM_SPEC] * (len(groups) + len(ahead))
             + [VMEM_SPEC] * len(groups),
             name,
             len(groups) * 3 * regions * region_flops,
             6 * 10**6,
-            ([pltpu.VMEM(acc_shape.shape, F32)] if finish else []) + scratch,
+            scratch,
         )(
             *([flat] if start else [flat, acc]),
-            *[table(*g) for g in groups],
+            *[table(*g) for g in groups + ahead],
             *[arrived[g][0] for g in groups],
         )
 
     arrived = {(SELF, SELF): (mix, 0)}
-    for lon in (FIRST, SECOND):
+    for lon in (SECOND, FIRST):
         arrived[lon, SELF] = (from_lon(mix, lon), 0)
-    mix_1, mix_2 = from_band(mix, FIRST), from_band(mix, SECOND)
-    acc = increments(None, [(SELF, SELF), (SECOND, SELF)], False, "own")
-    acc, mix_1, mix_2, near = lax.optimization_barrier(
-        (acc, mix_1, mix_2, arrived[FIRST, SELF][0])
+    mix_2 = from_band(mix, SECOND)
+    mix_1 = from_band(mix, FIRST)
+    (acc,) = increments(None, [(SELF, SELF), (SECOND, SELF)], [], "own")
+    near, mix_2, mix_1, acc = lax.optimization_barrier(
+        (arrived[FIRST, SELF][0], mix_2, mix_1, acc)
     )
     arrived[FIRST, SELF] = (near, 0)
     both = jnp.concatenate([mix_1, mix_2], axis=0)
@@ -575,10 +629,25 @@
     for lon in (FIRST, SECOND):
         there = from_lon(both, lon)
         arrived[lon, FIRST], arrived[lon, SECOND] = (there, 0), (there, 1)
-    acc = increments(acc, [(SELF, FIRST), (SELF, SECOND), (FIRST, SELF)], False, "inner")
-    acc = increments(acc, [(SECOND, FIRST), (SECOND, SECOND)], False, "outer")
-    acc = increments(acc, [(FIRST, FIRST), (FIRST, SECOND)], True, "finish")
-    return acc.reshape(members.shape)
+    last = [(FIRST, FIRST), (FIRST, SECOND)]
+    (acc,) = increments(acc, [(SELF, FIRST), (SELF, SECOND), (FIRST, SELF)], [], "inner")
+    acc, *lefts = increments(acc, [(SECOND, FIRST), (SECOND, SECOND)], last, "outer")
+    out = call(
+        functools.partial(
+            finish_kernel,
+            [slots(*g) for g in last],
+            [arrived[g][1] for g in last],
+            state_rows,
+            regions,
+        ),
+        jax.ShapeDtypeStruct(acc_shape.shape, BF16),
+        [VMEM_SPEC] + [SMEM_SPEC] * 2 + [VMEM_SPEC] * 4,
+        "finish",
+        6 * regions * region_flops,
+        9 * 10**6,
+        [pltpu.VMEM(acc_shape.shape, F32)] + [pltpu.VMEM((regions * n, n), BF16)] * 2,
+    )(acc, *[table(*g) for g in last], *[arrived[g][0] for g in last], *lefts)
+    return out.reshape(members.shape)
 
 
 def solution(mesh):

time: 88.3 us -> 86.7 us (0.982)
  waiting for transfers between devices: 16.9 us -> 12.5 us
  starting transfers between devices: 29.7 us -> 31.6 us
  Pallas kernels: 37 us -> 37.9 us
    ppermute x8, waiting for transfers between devices: 6.27 us -> 3.1 us  [from_lon(): lax.ppermute(x, 'lon', [((i + step * (1 - 2 * (i % 2))) % count, i) for i...]
    ppermute x8, starting transfers between devices: 21.5 us -> 23.7 us  [from_lon(): lax.ppermute(x, 'lon', [((i + step * (1 - 2 * (i % 2))) % count, i) for i...]
    ppermute x6, waiting for transfers between devices: 10.6 us -> 9.39 us  [from_band(): return lax.ppermute(x, 'band', [(j, i) for j, i in pairs if 0 <= j < count])]
  transfers between devices with their start and end apart: 14 -> 14, of which waited for: 7 -> 6; matrix products, arithmetic and copies ran while one was open for 1% -> 1% of each run, Pallas kernels for 25% -> 29%
where the time goes in v4:
time: 86.7 us; the launch traced here: 86.4 us
  Pallas kernels  37.9 us (44%)
  starting transfers between devices  31.6 us (36%)
  waiting for transfers between devices  12.5 us (14%)
  local copies, waits for them, and re-layouts  4.16 us (5%)
    ppermute x8, starting transfers between devices, from_lon(): lax.ppermute(x, 'lon', [((i + step * (1 - 2 * (i % 2))) % count, i) for i...  23.7 us
    pallas_call x3, Pallas kernels, increments(): call(kernel, (acc_shape,) + (left_shape,) * len(ahead), [VMEM_SPEC] * (1...  15.7 us
    ppermute x6, waiting for transfers between devices, from_band(): return lax.ppermute(x, 'band', [(j, i) for j, i in pairs if 0 <= j < count])  9.39 us
    ppermute x6, starting transfers between devices, from_band(): return lax.ppermute(x, 'band', [(j, i) for j, i in pairs if 0 <= j < count])  7.86 us
    pallas_call x1, Pallas kernels, local(): call(functools.partial(mix_kernel, 4), jax.ShapeDtypeStruct((packed_rows(...  6.92 us
    pallas_call x1, Pallas kernels, local(): call(functools.partial(finish_kernel, [slots(*g) for g in last], [arrived...  4.78 us
    pallas_call x1, Pallas kernels, local(): call(functools.partial(near_gram_kernel, obs_rows, regions), (jax.ShapeDt...  4.26 us
    unnamed x16, local copies, waits for them, and re-layouts  4.08 us
  transfers between devices with their start and end apart: 14, of which 6 were waited for; matrix products, arithmetic and copies ran while one was open for 1% of the time, Pallas kernels for 29%

profile of v4, /device:TPU:4, one launch (start us, length us, event | category | flops | bytes accessed | tf_op | source)
XLA Modules:
  0.0 86.4 jit_solution(13636178259371313280)
XLA Ops:
  0.0 1.2 %collective-permute-start.1 = (bf16[1536,256]{1,0:T(8,128)(2,1)}, bf16[1536,256]{1,0:T(8,128)(2,1)S(1)}, u32[]{:S(2)}, u32[]{:S(2)}) collective-permute-start(bf16[1536,256]{1,0:T(8,128)(2,1)} %bitcast.8), channel_id=1, source_target_pairs={{32,0},{0,32},{96,64},{64,96},{33,1},{1,33},{97,65},{65,97},{34,2}... | collective-permute-start | bytes 2359304 | tf_op jit(solution)/shard_map/ppermute | solution.py:475
  1.2 1.9 %collective-permute-start = (bf16[1536,256]{1,0:T(8,128)(2,1)}, bf16[1536,256]{1,0:T(8,128)(2,1)S(1)}, u32[]{:S(2)}, u32[]{:S(2)}) collective-permute-start(bf16[1536,256]{1,0:T(8,128)(2,1)} %bitcast.9), channel_id=1, source_target_pairs={{64,32},{32,64},{65,33},{33,65},{66,34},{34,66},{67,35},{35,67},{6... | collective-permute-start | bytes 2359304 | tf_op jit(solution)/shard_map/ppermute | solution.py:475
  3.1 0.8 copy.8.refs_3_
  3.9 0.0 copy-start.1
  3.9 1.1 %copy-done.1 = bf16[48,32,256]{2,1,0:T(8,128)(2,1)S(1)} copy-done((bf16[48,32,256]{2,1,0:T(8,128)(2,1)S(1)}, bf16[48,32,256]{2,1,0:T(8,128)(2,1)}, u32[]{:S(2)}) %copy-start.1) | copy-done | bytes 786456
  5.0 0.0 copy-start.3
  5.0 0.7 copy-done.3
  5.8 0.7 copy-done.4
  6.5 0.7 copy-done.5
  7.2 2.3 %tables.1 = (f32[16,256]{1,0:T(8,128)S(1)}, f32[512,128]{1,0:T(8,128)S(1)}, bf16[1536,256]{1,0:T(8,128)(2,1)S(1)}) custom-call(s32[8,64]{1,0:T(8,128)S(1)} %copy-done.4, s32[48,128]{1,0:T(8,128)S(1)} %bitcast.12, f32[8,64]{1,0:T(8,128)S(1)} %copy-done.5, bf16[48,32]{1,0:T(8,128)(2,1)S(1)} %copy.8.refs_3_, bf16[1536,256]{1,0:T(8,128)(2,1)S(1)} %bitcast.10), custom_call_target="tpu_custom_call" | custom-call | flops 1000000000 | bytes 1000000 | tf_op jit(solution)/shard_map/tables/pallas_call | solution.py:497
  9.5 0.1 collective-permute-start.3
  9.6 6.6 %collective-permute-start.2 = (f32[16,256]{1,0:T(8,128)S(1)}, f32[16,256]{1,0:T(8,128)S(1)}, u32[]{:S(2)}, u32[]{:S(2)}) collective-permute-start(f32[16,256]{1,0:T(8,128)S(1)} %get-tuple-element.31.table.refs_1_), channel_id=1, source_target_pairs={{31,0},{2,1},{1,2},{4,3},{3,4},{6,5},{5,6},{8,7},{7,8},{10,9},{9,1... | collective-permute-start | bytes 49160 | tf_op jit(solution)/shard_map/ppermute | solution.py:481
  16.2 0.0 copy-done.2
  16.2 2.0 %weights.1 = f32[8,4608]{1,0:T(8,128)S(1)} custom-call(f32[512,128]{1,0:T(8,128)S(1)} %get-tuple-element.28.entry_slot, f32[8,32,64]{2,1,0:T(8,128)S(1)} %bitcast.11), custom_call_target="tpu_custom_call" | custom-call | flops 1000000000 | bytes 1000000 | tf_op jit(solution)/shard_map/weights/pallas_call | solution.py:519
  18.1 1.4 %collective-permute-done.1.obs_1 = bf16[1536,256]{1,0:T(8,128)(2,1)S(1)} collective-permute-done((bf16[1536,256]{1,0:T(8,128)(2,1)}, bf16[1536,256]{1,0:T(8,128)(2,1)S(1)}, u32[]{:S(2)}, u32[]{:S(2)}) %collective-permute-start.1) | collective-permute-done | bytes 786464 | tf_op jit(solution)/shard_map/ppermute | solution.py:475
  19.5 2.8 %collective-permute-done.obs_2 = bf16[1536,256]{1,0:T(8,128)(2,1)S(1)} collective-permute-done((bf16[1536,256]{1,0:T(8,128)(2,1)}, bf16[1536,256]{1,0:T(8,128)(2,1)S(1)}, u32[]{:S(2)}, u32[]{:S(2)}) %collective-permute-start) | collective-permute-done | bytes 786464 | tf_op jit(solution)/shard_map/ppermute | solution.py:475
  22.3 0.0 collective-permute-done.3.table_2.refs_2_
  22.3 0.0 collective-permute-done.2.table_1.refs_4_
  22.3 1.3 %select.1 = (bf16[1536,256]{1,0:T(8,128)(2,1)S(1)}, bf16[1536,256]{1,0:T(8,128)(2,1)S(1)}) custom-call(bf16[1536,256]{1,0:T(8,128)(2,1)S(1)} %get-tuple-element.27.obs, bf16[1536,256]{1,0:T(8,128)(2,1)S(1)} %collective-permute-done.1.obs_1, bf16[1536,256]{1,0:T(8,128)(2,1)S(1)} %collective-permute-done.obs_2, ...), custom_call_target="tpu_custom_call" | custom-call | flops 100000000 | bytes 4000000 | tf_op jit(solution)/shard_map/select/pallas_call | solution.py:530
  23.6 0.1 collective-permute-start.5
  23.7 6.6 %collective-permute-start.4 = (bf16[1536,256]{1,0:T(8,128)(2,1)S(1)}, bf16[1536,256]{1,0:T(8,128)(2,1)S(1)}, u32[]{:S(2)}, u32[]{:S(2)}) collective-permute-start(bf16[1536,256]{1,0:T(8,128)(2,1)S(1)} %get-tuple-element.32), channel_id=1, source_target_pairs={{31,0},{2,1},{1,2},{4,3},{3,4},{6,5},{5,6},{8,7},{7,8},{10,9},{9,1... | collective-permute-start | bytes 2359304 | tf_op jit(solution)/shard_map/ppermute | solution.py:481
  30.3 0.1 collective-permute-start.7
  30.4 2.4 %collective-permute-start.6 = (f32[48,256]{1,0:T(8,128)S(1)}, f32[48,256]{1,0:T(8,128)S(1)}, u32[]{:S(2)}, u32[]{:S(2)}) collective-permute-start(f32[48,256]{1,0:T(8,128)S(1)} %constant_dynamic-update-slice_fusion.metas), channel_id=1, source_target_pairs={{64,32},{32,64},{65,33},{33,65},{66,34},{34,66},{67,35},{35,67},{6... | collective-permute-start | bytes 147464 | tf_op jit(solution)/shard_map/ppermute | solution.py:475
  32.7 0.0 collective-permute-done.5.pool_2
  32.8 4.3 %near_gram.1 = (f32[2048,256]{1,0:T(8,128)S(1)}, bf16[1536,256]{1,0:T(8,128)(2,1)S(1)}) custom-call(bf16[1536,256]{1,0:T(8,128)(2,1)S(1)} %get-tuple-element.27.obs, bf16[1536,256]{1,0:T(8,128)(2,1)S(1)} %collective-permute-done.1.obs_1, bf16[1536,256]{1,0:T(8,128)(2,1)S(1)} %collective-permute-done.obs_2, ...), custom_call_target="tpu_custom_call" | custom-call | flops 3221225472 | bytes 5000000 | tf_op jit(solution)/shard_map/near_gram/pallas_call | solution.py:545
  37.0 0.0 collective-permute-done.7.metas_1
  37.0 0.0 collective-permute-done.6.metas_2
  37.0 0.6 innov.1
  37.7 2.2 %collective-permute-done.4.pool = bf16[1536,256]{1,0:T(8,128)(2,1)S(1)} collective-permute-done((bf16[1536,256]{1,0:T(8,128)(2,1)S(1)}, bf16[1536,256]{1,0:T(8,128)(2,1)S(1)}, u32[]{:S(2)}, u32[]{:S(2)}) %collective-permute-start.4) | collective-permute-done | bytes 786464 | tf_op jit(solution)/shard_map/ppermute | solution.py:481
  39.9 6.9 %mixing.1.refs_3_ = bf16[2096,128]{1,0:T(8,128)(2,1)S(1)} custom-call(bf16[1536,256]{1,0:T(8,128)(2,1)S(1)} %collective-permute-done.4.pool, f32[8,4608]{1,0:T(8,128)S(1)} %weights.1, f32[2048,256]{1,0:T(8,128)S(1)} %get-tuple-element.35.gram_near, bf16[16,4608]{1,0:T(8,128)(2,1)S(1)} %get-tuple-element.40.scaled, f32[8,256]{1,0:T(8,128)S(1)} %get-tuple-element.41.proj_near), custom_call_target="tpu_custom_call" | custom-call | flops 4831838208 | bytes 4000000 | tf_op jit(solution)/shard_map/mixing/pallas_call | solution.py:563
  46.9 0.1 collective-permute-start.11
  47.0 0.1 collective-permute-start.10
  47.1 2.2 %collective-permute-start.9 = (bf16[2096,128]{1,0:T(8,128)(2,1)S(1)}, bf16[2096,128]{1,0:T(8,128)(2,1)S(1)}, u32[]{:S(2)}, u32[]{:S(2)}) collective-permute-start(bf16[2096,128]{1,0:T(8,128)(2,1)S(1)} %mixing.1.refs_3_), channel_id=1, source_target_pairs={{64,32},{32,64},{65,33},{33,65},{66,34},{34,66},{67,35},{35,67},{6... | collective-permute-start | bytes 1609736 | tf_op jit(solution)/shard_map/ppermute | solution.py:475
  49.3 5.1 %collective-permute-start.8 = (bf16[2096,128]{1,0:T(8,128)(2,1)S(1)}, bf16[2096,128]{1,0:T(8,128)(2,1)S(1)}, u32[]{:S(2)}, u32[]{:S(2)}) collective-permute-start(bf16[2096,128]{1,0:T(8,128)(2,1)S(1)} %mixing.1.refs_3_), channel_id=1, source_target_pairs={{31,0},{2,1},{1,2},{4,3},{3,4},{6,5},{5,6},{8,7},{7,8},{10,9},{9,1... | collective-permute-start | bytes 1609736 | tf_op jit(solution)/shard_map/ppermute | solution.py:481
  54.4 0.0 collective-permute-done.11.refs_4_
  54.4 0.0 copy-done
  54.4 3.9 %own.1.refs_1_ = f32[2304,256]{1,0:T(8,128)S(1)} custom-call(bf16[2304,256]{1,0:T(8,128)(2,1)S(1)} %bitcast.5, f32[16,256]{1,0:T(8,128)S(1)} %get-tuple-element.31.table.refs_1_, f32[16,256]{1,0:T(8,128)S(1)} %collective-permute-done.3.table_2.refs_2_, bf16[2096,128]{1,0:T(8,128)(2,1)S(1)} %mixing.1.refs_3_, ...), custom_call_target="tpu_custom_call" | custom-call | flops 1610612736 | bytes 6000000 | tf_op jit(solution)/shard_map/own/pallas_call | solution.py:601
  58.2 3.3 %collective-permute-done.10.refs_5_ = bf16[2096,128]{1,0:T(8,128)(2,1)S(1)} collective-permute-done((bf16[2096,128]{1,0:T(8,128)(2,1)S(1)}, bf16[2096,128]{1,0:T(8,128)(2,1)S(1)}, u32[]{:S(2)}, u32[]{:S(2)}) %collective-permute-start.10) | collective-permute-done | bytes 536608 | tf_op jit(solution)/shard_map/ppermute | solution.py:475
  61.6 1.9 %collective-permute-done.9.refs_6_ = bf16[2096,128]{1,0:T(8,128)(2,1)S(1)} collective-permute-done((bf16[2096,128]{1,0:T(8,128)(2,1)S(1)}, bf16[2096,128]{1,0:T(8,128)(2,1)S(1)}, u32[]{:S(2)}, u32[]{:S(2)}) %collective-permute-start.9) | collective-permute-done | bytes 536608 | tf_op jit(solution)/shard_map/ppermute | solution.py:475
  63.5 0.0 collective-permute-done.8.refs_7_
  63.5 0.1 constant_dynamic-update-slice_fusion.3
  63.6 0.1 collective-permute-start.12
  63.7 5.1 %collective-permute-start.13 = (bf16[4192,128]{1,0:T(8,128)(2,1)S(1)}, bf16[4192,128]{1,0:T(8,128)(2,1)S(1)}, u32[]{:S(2)}, u32[]{:S(2)}) collective-permute-start(bf16[4192,128]{1,0:T(8,128)(2,1)S(1)} %constant_dynamic-update-slice_fusion.3), channel_id=1, source_target_pairs={{31,0},{2,1},{1,2},{4,3},{3,4},{6,5},{5,6},{8,7},{7,8},{10,9},{9,1... | collective-permute-start | bytes 3219464 | tf_op jit(solution)/shard_map/ppermute | solution.py:481
  68.8 6.7 %inner.1.refs_1_ = f32[2304,256]{1,0:T(8,128)S(1)} custom-call(bf16[2304,256]{1,0:T(8,128)(2,1)S(1)} %bitcast.6, f32[2304,256]{1,0:T(8,128)S(1)} %own.1.refs_1_, f32[16,256]{1,0:T(8,128)S(1)} %get-tuple-element.55.refs_2_, f32[16,256]{1,0:T(8,128)S(1)} %get-tuple-element.51.refs_3_, f32[16,256]{1,0:T(8,128)S(1)} %collective-permute-done.2.table_1.refs_4_, ...), custom_call_target="tpu_custom_call" | custom-call | flops 2415919104 | bytes 6000000 | tf_op jit(solution)/shard_map/inner/pallas_call | solution.py:601
  75.6 0.0 collective-permute-done.12.refs_6_.refs_7_
  75.6 5.1 %outer.1 = (f32[2304,256]{1,0:T(8,128)S(1)}, bf16[768,2048]{1,0:T(8,128)(2,1)S(1)}, bf16[768,2048]{1,0:T(8,128)(2,1)S(1)}) custom-call(bf16[2304,256]{1,0:T(8,128)(2,1)S(1)} %bitcast.7, f32[2304,256]{1,0:T(8,128)S(1)} %inner.1.refs_1_, f32[16,256]{1,0:T(8,128)S(1)} %get-tuple-element.56.refs_2_, f32[16,256]{1,0:T(8,128)S(1)} %get-tuple-element.50.refs_3_, ...), custom_call_target="tpu_custom_call" | custom-call | flops 1610612736 | bytes 6000000 | tf_op jit(solution)/shard_map/outer/pallas_call | solution.py:601
  80.7 0.8 collective-permute-done.13.refs_2_.refs_3_
  81.6 4.8 %finish.1 = bf16[2304,256]{1,0:T(8,128)(2,1)} custom-call(f32[2304,256]{1,0:T(8,128)S(1)} %get-tuple-element.46.before, f32[16,256]{1,0:T(8,128)S(1)} %get-tuple-element.57.refs_4_.refs_0_, f32[16,256]{1,0:T(8,128)S(1)} %get-tuple-element.49.refs_5_.refs_1_, bf16[4192,128]{1,0:T(8,128)(2,1)S(1)} %collective-permute-done.13.refs_2_.refs_3_, ...), custom_call_target="tpu_custom_call" | custom-call | flops 1610612736 | bytes 9000000 | tf_op jit(solution)/shard_map/finish/pallas_call | solution.py:635
  (9 shorter events, 0.1 us)
Async XLA Ops:
  0.0 19.5 %collective-permute-start.1 = (bf16[1536,256]{1,0:T(8,128)(2,1)}, bf16[1536,256]{1,0:T(8,128)(2,1)S(1)}, u32[]{:S(2)}, u32[]{:S(2)}) collective-permute-start(bf16[1536,256]{1,0:T(8,128)(2,1)} %bitcast.8), channel_id=1, source_target_pairs={{32,0},{0,32},{96,64},{64,96},{33,1},{1,33},{97,65},{65,97},{34,2}... | collective-permute-start | bytes 2359304 | tf_op jit(solution)/shard_map/ppermute | solution.py:475
  1.2 21.1 %collective-permute-start = (bf16[1536,256]{1,0:T(8,128)(2,1)}, bf16[1536,256]{1,0:T(8,128)(2,1)S(1)}, u32[]{:S(2)}, u32[]{:S(2)}) collective-permute-start(bf16[1536,256]{1,0:T(8,128)(2,1)} %bitcast.9), channel_id=1, source_target_pairs={{64,32},{32,64},{65,33},{33,65},{66,34},{34,66},{67,35},{35,67},{6... | collective-permute-start | bytes 2359304 | tf_op jit(solution)/shard_map/ppermute | solution.py:475
  3.9 1.1 %copy-start.1 = (bf16[48,32,256]{2,1,0:T(8,128)(2,1)S(1)}, bf16[48,32,256]{2,1,0:T(8,128)(2,1)}, u32[]{:S(2)}) copy-start(bf16[48,32,256]{2,1,0:T(8,128)(2,1)} %param.8) | copy-start | bytes 2359300
  5.0 0.7 copy-start.3
  5.8 0.7 copy-start.4
  6.5 0.7 copy-start.5
  7.2 9.0 %copy-start.2 = (f32[8,64,32]{1,2,0:T(8,128)S(1)}, f32[8,64,32]{1,2,0:T(8,128)}, u32[]{:S(2)}) copy-start(f32[8,64,32]{1,2,0:T(8,128)} %param.12) | copy-start | bytes 196612
  9.5 12.8 %collective-permute-start.3 = (f32[16,256]{1,0:T(8,128)S(1)}, f32[16,256]{1,0:T(8,128)S(1)}, u32[]{:S(2)}, u32[]{:S(2)}) collective-permute-start(f32[16,256]{1,0:T(8,128)S(1)} %get-tuple-element.31.table.refs_1_), channel_id=1, source_target_pairs={{1,0},{0,1},{3,2},{2,3},{5,4},{4,5},{7,6},{6,7},{9,8},{8,9},{11,10... | collective-permute-start | bytes 49160 | tf_op jit(solution)/shard_map/ppermute | solution.py:481
  9.6 12.7 %collective-permute-start.2 = (f32[16,256]{1,0:T(8,128)S(1)}, f32[16,256]{1,0:T(8,128)S(1)}, u32[]{:S(2)}, u32[]{:S(2)}) collective-permute-start(f32[16,256]{1,0:T(8,128)S(1)} %get-tuple-element.31.table.refs_1_), channel_id=1, source_target_pairs={{31,0},{2,1},{1,2},{4,3},{3,4},{6,5},{5,6},{8,7},{7,8},{10,9},{9,1... | collective-permute-start | bytes 49160 | tf_op jit(solution)/shard_map/ppermute | solution.py:481
  23.6 9.2 %collective-permute-start.5 = (bf16[1536,256]{1,0:T(8,128)(2,1)S(1)}, bf16[1536,256]{1,0:T(8,128)(2,1)S(1)}, u32[]{:S(2)}, u32[]{:S(2)}) collective-permute-start(bf16[1536,256]{1,0:T(8,128)(2,1)S(1)} %get-tuple-element.34), channel_id=1, source_target_pairs={{1,0},{0,1},{3,2},{2,3},{5,4},{4,5},{7,6},{6,7},{9,8},{8,9},{11,10... | collective-permute-start | bytes 2359304 | tf_op jit(solution)/shard_map/ppermute | solution.py:481
  23.7 16.3 %collective-permute-start.4 = (bf16[1536,256]{1,0:T(8,128)(2,1)S(1)}, bf16[1536,256]{1,0:T(8,128)(2,1)S(1)}, u32[]{:S(2)}, u32[]{:S(2)}) collective-permute-start(bf16[1536,256]{1,0:T(8,128)(2,1)S(1)} %get-tuple-element.32), channel_id=1, source_target_pairs={{31,0},{2,1},{1,2},{4,3},{3,4},{6,5},{5,6},{8,7},{7,8},{10,9},{9,1... | collective-permute-start | bytes 2359304 | tf_op jit(solution)/shard_map/ppermute | solution.py:481
  30.3 6.8 %collective-permute-start.7 = (f32[48,256]{1,0:T(8,128)S(1)}, f32[48,256]{1,0:T(8,128)S(1)}, u32[]{:S(2)}, u32[]{:S(2)}) collective-permute-start(f32[48,256]{1,0:T(8,128)S(1)} %constant_dynamic-update-slice_fusion.metas), channel_id=1, source_target_pairs={{32,0},{0,32},{96,64},{64,96},{33,1},{1,33},{97,65},{65,97},{34,2}... | collective-permute-start | bytes 147464 | tf_op jit(solution)/shard_map/ppermute | solution.py:475
  30.4 6.7 %collective-permute-start.6 = (f32[48,256]{1,0:T(8,128)S(1)}, f32[48,256]{1,0:T(8,128)S(1)}, u32[]{:S(2)}, u32[]{:S(2)}) collective-permute-start(f32[48,256]{1,0:T(8,128)S(1)} %constant_dynamic-update-slice_fusion.metas), channel_id=1, source_target_pairs={{64,32},{32,64},{65,33},{33,65},{66,34},{34,66},{67,35},{35,67},{6... | collective-permute-start | bytes 147464 | tf_op jit(solution)/shard_map/ppermute | solution.py:475
  39.9 14.4 %copy-start = (bf16[48,48,256]{2,1,0:T(8,128)(2,1)S(1)}, bf16[48,48,256]{2,1,0:T(8,128)(2,1)}, u32[]{:S(2)}) copy-start(bf16[48,48,256]{2,1,0:T(8,128)(2,1)} %param.7) | copy-start | bytes 3538948
  46.9 7.5 %collective-permute-start.11 = (bf16[2096,128]{1,0:T(8,128)(2,1)S(1)}, bf16[2096,128]{1,0:T(8,128)(2,1)S(1)}, u32[]{:S(2)}, u32[]{:S(2)}) collective-permute-start(bf16[2096,128]{1,0:T(8,128)(2,1)S(1)} %mixing.1.refs_3_), channel_id=1, source_target_pairs={{1,0},{0,1},{3,2},{2,3},{5,4},{4,5},{7,6},{6,7},{9,8},{8,9},{11,10... | collective-permute-start | bytes 1609736 | tf_op jit(solution)/shard_map/ppermute | solution.py:481
  47.0 14.6 %collective-permute-start.10 = (bf16[2096,128]{1,0:T(8,128)(2,1)S(1)}, bf16[2096,128]{1,0:T(8,128)(2,1)S(1)}, u32[]{:S(2)}, u32[]{:S(2)}) collective-permute-start(bf16[2096,128]{1,0:T(8,128)(2,1)S(1)} %mixing.1.refs_3_), channel_id=1, source_target_pairs={{32,0},{0,32},{96,64},{64,96},{33,1},{1,33},{97,65},{65,97},{34,2}... | collective-permute-start | bytes 1609736 | tf_op jit(solution)/shard_map/ppermute | solution.py:475
  47.1 16.4 %collective-permute-start.9 = (bf16[2096,128]{1,0:T(8,128)(2,1)S(1)}, bf16[2096,128]{1,0:T(8,128)(2,1)S(1)}, u32[]{:S(2)}, u32[]{:S(2)}) collective-permute-start(bf16[2096,128]{1,0:T(8,128)(2,1)S(1)} %mixing.1.refs_3_), channel_id=1, source_target_pairs={{64,32},{32,64},{65,33},{33,65},{66,34},{34,66},{67,35},{35,67},{6... | collective-permute-start | bytes 1609736 | tf_op jit(solution)/shard_map/ppermute | solution.py:475
  49.3 14.2 %collective-permute-start.8 = (bf16[2096,128]{1,0:T(8,128)(2,1)S(1)}, bf16[2096,128]{1,0:T(8,128)(2,1)S(1)}, u32[]{:S(2)}, u32[]{:S(2)}) collective-permute-start(bf16[2096,128]{1,0:T(8,128)(2,1)S(1)} %mixing.1.refs_3_), channel_id=1, source_target_pairs={{31,0},{2,1},{1,2},{4,3},{3,4},{6,5},{5,6},{8,7},{7,8},{10,9},{9,1... | collective-permute-start | bytes 1609736 | tf_op jit(solution)/shard_map/ppermute | solution.py:481
  63.6 12.0 %collective-permute-start.12 = (bf16[4192,128]{1,0:T(8,128)(2,1)S(1)}, bf16[4192,128]{1,0:T(8,128)(2,1)S(1)}, u32[]{:S(2)}, u32[]{:S(2)}) collective-permute-start(bf16[4192,128]{1,0:T(8,128)(2,1)S(1)} %constant_dynamic-update-slice_fusion.3), channel_id=1, source_target_pairs={{1,0},{0,1},{3,2},{2,3},{5,4},{4,5},{7,6},{6,7},{9,8},{8,9},{11,10... | collective-permute-start | bytes 3219464 | tf_op jit(solution)/shard_map/ppermute | solution.py:481
  63.7 17.9 %collective-permute-start.13 = (bf16[4192,128]{1,0:T(8,128)(2,1)S(1)}, bf16[4192,128]{1,0:T(8,128)(2,1)S(1)}, u32[]{:S(2)}, u32[]{:S(2)}) collective-permute-start(bf16[4192,128]{1,0:T(8,128)(2,1)S(1)} %constant_dynamic-update-slice_fusion.3), channel_id=1, source_target_pairs={{31,0},{2,1},{1,2},{4,3},{3,4},{6,5},{5,6},{8,7},{7,8},{10,9},{9,1... | collective-permute-start | bytes 3219464 | tf_op jit(solution)/shard_map/ppermute | solution.py:481

commit v5 on v4

--- a/solution.py
+++ b/solution.py
@@ -624,11 +624,11 @@
         (arrived[FIRST, SELF][0], mix_2, mix_1, acc)
     )
     arrived[FIRST, SELF] = (near, 0)
-    both = jnp.concatenate([mix_1, mix_2], axis=0)
+    arrived[FIRST, FIRST] = (from_band(near, FIRST), 0)
+    arrived[FIRST, SECOND] = (from_band(near, SECOND), 0)
     arrived[SELF, FIRST], arrived[SELF, SECOND] = (mix_1, 0), (mix_2, 0)
-    for lon in (FIRST, SECOND):
-        there = from_lon(both, lon)
-        arrived[lon, FIRST], arrived[lon, SECOND] = (there, 0), (there, 1)
+    both = from_lon(jnp.concatenate([mix_1, mix_2], axis=0), SECOND)
+    arrived[SECOND, FIRST], arrived[SECOND, SECOND] = (both, 0), (both, 1)
     last = [(FIRST, FIRST), (FIRST, SECOND)]
     (acc,) = increments(acc, [(SELF, FIRST), (SELF, SECOND), (FIRST, SELF)], [], "inner")
     acc, *lefts = increments(acc, [(SECOND, FIRST), (SECOND, SECOND)], last, "outer")

time: 86.7 us -> 85.7 us (0.988)
  starting transfers between devices: 31.6 us -> 30.3 us
    ppermute x8 -> x7, starting transfers between devices: 23.7 us -> 16.7 us  [from_lon(): lax.ppermute(x, 'lon', [((i + step * (1 - 2 * (i % 2))) % count, i) for i...]
    ppermute x6 -> x8, starting transfers between devices: 7.86 us -> 13.6 us  [from_band(): return lax.ppermute(x, 'band', [(j, i) for j, i in pairs if 0 <= j < count])]
    ppermute x8 -> x7, waiting for transfers between devices: 3.1 us -> 1.06 us  [from_lon(): lax.ppermute(x, 'lon', [((i + step * (1 - 2 * (i % 2))) % count, i) for i...]
    ppermute x6 -> x8, waiting for transfers between devices: 9.39 us -> 11.4 us  [from_band(): return lax.ppermute(x, 'band', [(j, i) for j, i in pairs if 0 <= j < count])]
    unnamed x16 -> x15, local copies, waits for them, and re-layouts: 4.08 us -> 4.04 us
  transfers between devices with their start and end apart: 14 -> 15, of which waited for: 6 -> 6; matrix products, arithmetic and copies ran while one was open for 1% -> 1% of each run, Pallas kernels for 29% -> 29%
where the time goes in v5:
time: 85.7 us; the launch traced here: 85.1 us
  Pallas kernels  37.9 us (44%)
  starting transfers between devices  30.3 us (35%)
  waiting for transfers between devices  12.5 us (15%)
  local copies, waits for them, and re-layouts  4.05 us (5%)
    ppermute x7, starting transfers between devices, from_lon(): lax.ppermute(x, 'lon', [((i + step * (1 - 2 * (i % 2))) % count, i) for i...  16.7 us
    pallas_call x3, Pallas kernels, increments(): call(kernel, (acc_shape,) + (left_shape,) * len(ahead), [VMEM_SPEC] * (1...  15.8 us
    ppermute x8, starting transfers between devices, from_band(): return lax.ppermute(x, 'band', [(j, i) for j, i in pairs if 0 <= j < count])  13.6 us
    ppermute x8, waiting for transfers between devices, from_band(): return lax.ppermute(x, 'band', [(j, i) for j, i in pairs if 0 <= j < count])  11.4 us
    pallas_call x1, Pallas kernels, local(): call(functools.partial(mix_kernel, 4), jax.ShapeDtypeStruct((packed_rows(...  6.89 us
    pallas_call x1, Pallas kernels, local(): call(functools.partial(finish_kernel, [slots(*g) for g in last], [arrived...  4.79 us
    pallas_call x1, Pallas kernels, local(): call(functools.partial(near_gram_kernel, obs_rows, regions), (jax.ShapeDt...  4.26 us
    unnamed x15, local copies, waits for them, and re-layouts  4.04 us
  transfers between devices with their start and end apart: 15, of which 6 were waited for; matrix products, arithmetic and copies ran while one was open for 1% of the time, Pallas kernels for 29%

profile of v5, /device:TPU:4, one launch (start us, length us, event | category | flops | bytes accessed | tf_op | source)
XLA Modules:
  0.0 85.1 jit_solution(10787411597369290287)
XLA Ops:
  0.0 2.4 %collective-permute-start = (bf16[1536,256]{1,0:T(8,128)(2,1)}, bf16[1536,256]{1,0:T(8,128)(2,1)S(1)}, u32[]{:S(2)}, u32[]{:S(2)}) collective-permute-start(bf16[1536,256]{1,0:T(8,128)(2,1)} %bitcast.8), channel_id=1, source_target_pairs={{64,32},{32,64},{65,33},{33,65},{66,34},{34,66},{67,35},{35,67},{6... | collective-permute-start | bytes 2359304 | tf_op jit(solution)/shard_map/ppermute | solution.py:475
  2.4 0.1 collective-permute-start.1
  2.5 0.8 copy.8.refs_3_
  3.3 1.1 %copy-done.1 = bf16[48,32,256]{2,1,0:T(8,128)(2,1)S(1)} copy-done((bf16[48,32,256]{2,1,0:T(8,128)(2,1)S(1)}, bf16[48,32,256]{2,1,0:T(8,128)(2,1)}, u32[]{:S(2)}) %copy-start.1) | copy-done | bytes 786456
  4.5 0.7 copy-done.3
  5.2 0.7 copy-done.4
  5.9 0.7 copy-done.5
  6.6 2.3 %tables.1 = (f32[16,256]{1,0:T(8,128)S(1)}, f32[512,128]{1,0:T(8,128)S(1)}, bf16[1536,256]{1,0:T(8,128)(2,1)S(1)}) custom-call(s32[8,64]{1,0:T(8,128)S(1)} %copy-done.4, s32[48,128]{1,0:T(8,128)S(1)} %bitcast.12, f32[8,64]{1,0:T(8,128)S(1)} %copy-done.5, bf16[48,32]{1,0:T(8,128)(2,1)S(1)} %copy.8.refs_3_, bf16[1536,256]{1,0:T(8,128)(2,1)S(1)} %bitcast.10), custom_call_target="tpu_custom_call" | custom-call | flops 1000000000 | bytes 1000000 | tf_op jit(solution)/shard_map/tables/pallas_call | solution.py:497
  8.9 5.7 %collective-permute-start.2 = (f32[16,256]{1,0:T(8,128)S(1)}, f32[16,256]{1,0:T(8,128)S(1)}, u32[]{:S(2)}, u32[]{:S(2)}) collective-permute-start(f32[16,256]{1,0:T(8,128)S(1)} %get-tuple-element.31.table.refs_1_), channel_id=1, source_target_pairs={{31,0},{2,1},{1,2},{4,3},{3,4},{6,5},{5,6},{8,7},{7,8},{10,9},{9,1... | collective-permute-start | bytes 49160 | tf_op jit(solution)/shard_map/ppermute | solution.py:481
  14.6 0.0 collective-permute-start.3
  14.6 0.0 copy-done.2
  14.6 2.0 %weights.1 = f32[8,4608]{1,0:T(8,128)S(1)} custom-call(f32[512,128]{1,0:T(8,128)S(1)} %get-tuple-element.28.entry_slot, f32[8,32,64]{2,1,0:T(8,128)S(1)} %bitcast.11), custom_call_target="tpu_custom_call" | custom-call | flops 1000000000 | bytes 1000000 | tf_op jit(solution)/shard_map/weights/pallas_call | solution.py:519
  16.6 4.8 %collective-permute-done.obs_2 = bf16[1536,256]{1,0:T(8,128)(2,1)S(1)} collective-permute-done((bf16[1536,256]{1,0:T(8,128)(2,1)}, bf16[1536,256]{1,0:T(8,128)(2,1)S(1)}, u32[]{:S(2)}, u32[]{:S(2)}) %collective-permute-start) | collective-permute-done | bytes 786464 | tf_op jit(solution)/shard_map/ppermute | solution.py:475
  21.4 0.4 collective-permute-done.1.obs_1
  21.7 0.0 collective-permute-done.2.table_1.refs_4_
  21.7 0.0 collective-permute-done.3.table_2.refs_2_
  21.7 1.3 %select.1 = (bf16[1536,256]{1,0:T(8,128)(2,1)S(1)}, bf16[1536,256]{1,0:T(8,128)(2,1)S(1)}) custom-call(bf16[1536,256]{1,0:T(8,128)(2,1)S(1)} %get-tuple-element.27.obs, bf16[1536,256]{1,0:T(8,128)(2,1)S(1)} %collective-permute-done.1.obs_1, bf16[1536,256]{1,0:T(8,128)(2,1)S(1)} %collective-permute-done.obs_2, ...), custom_call_target="tpu_custom_call" | custom-call | flops 100000000 | bytes 4000000 | tf_op jit(solution)/shard_map/select/pallas_call | solution.py:530
  23.0 0.1 collective-permute-start.5
  23.1 6.6 %collective-permute-start.4 = (bf16[1536,256]{1,0:T(8,128)(2,1)S(1)}, bf16[1536,256]{1,0:T(8,128)(2,1)S(1)}, u32[]{:S(2)}, u32[]{:S(2)}) collective-permute-start(bf16[1536,256]{1,0:T(8,128)(2,1)S(1)} %get-tuple-element.32), channel_id=1, source_target_pairs={{31,0},{2,1},{1,2},{4,3},{3,4},{6,5},{5,6},{8,7},{7,8},{10,9},{9,1... | collective-permute-start | bytes 2359304 | tf_op jit(solution)/shard_map/ppermute | solution.py:481
  29.7 3.4 %collective-permute-start.6 = (f32[48,256]{1,0:T(8,128)S(1)}, f32[48,256]{1,0:T(8,128)S(1)}, u32[]{:S(2)}, u32[]{:S(2)}) collective-permute-start(f32[48,256]{1,0:T(8,128)S(1)} %constant_dynamic-update-slice_fusion.metas), channel_id=1, source_target_pairs={{64,32},{32,64},{65,33},{33,65},{66,34},{34,66},{67,35},{35,67},{6... | collective-permute-start | bytes 147464 | tf_op jit(solution)/shard_map/ppermute | solution.py:475
  33.1 0.3 collective-permute-start.7
  33.4 0.0 collective-permute-done.5.pool_2
  33.4 4.3 %near_gram.1 = (f32[2048,256]{1,0:T(8,128)S(1)}, bf16[1536,256]{1,0:T(8,128)(2,1)S(1)}) custom-call(bf16[1536,256]{1,0:T(8,128)(2,1)S(1)} %get-tuple-element.27.obs, bf16[1536,256]{1,0:T(8,128)(2,1)S(1)} %collective-permute-done.1.obs_1, bf16[1536,256]{1,0:T(8,128)(2,1)S(1)} %collective-permute-done.obs_2, ...), custom_call_target="tpu_custom_call" | custom-call | flops 3221225472 | bytes 5000000 | tf_op jit(solution)/shard_map/near_gram/pallas_call | solution.py:545
  37.7 0.0 collective-permute-done.6.metas_2
  37.7 0.0 collective-permute-done.7.metas_1
  37.7 0.6 innov.1
  38.3 1.0 %collective-permute-done.4.pool = bf16[1536,256]{1,0:T(8,128)(2,1)S(1)} collective-permute-done((bf16[1536,256]{1,0:T(8,128)(2,1)S(1)}, bf16[1536,256]{1,0:T(8,128)(2,1)S(1)}, u32[]{:S(2)}, u32[]{:S(2)}) %collective-permute-start.4) | collective-permute-done | bytes 786464 | tf_op jit(solution)/shard_map/ppermute | solution.py:481
  39.4 6.9 %mixing.1.refs_3_ = bf16[2096,128]{1,0:T(8,128)(2,1)S(1)} custom-call(bf16[1536,256]{1,0:T(8,128)(2,1)S(1)} %collective-permute-done.4.pool, f32[8,4608]{1,0:T(8,128)S(1)} %weights.1, f32[2048,256]{1,0:T(8,128)S(1)} %get-tuple-element.35.gram_near, bf16[16,4608]{1,0:T(8,128)(2,1)S(1)} %get-tuple-element.40.scaled, f32[8,256]{1,0:T(8,128)S(1)} %get-tuple-element.41.proj_near), custom_call_target="tpu_custom_call" | custom-call | flops 4831838208 | bytes 4000000 | tf_op jit(solution)/shard_map/mixing/pallas_call | solution.py:563
  46.3 0.1 collective-permute-start.11
  46.4 1.1 %collective-permute-start.10 = (bf16[2096,128]{1,0:T(8,128)(2,1)S(1)}, bf16[2096,128]{1,0:T(8,128)(2,1)S(1)}, u32[]{:S(2)}, u32[]{:S(2)}) collective-permute-start(bf16[2096,128]{1,0:T(8,128)(2,1)S(1)} %mixing.1.refs_3_), channel_id=1, source_target_pairs={{32,0},{0,32},{96,64},{64,96},{33,1},{1,33},{97,65},{65,97},{34,2}... | collective-permute-start | bytes 1609736 | tf_op jit(solution)/shard_map/ppermute | solution.py:475
  47.5 4.1 %collective-permute-start.8 = (bf16[2096,128]{1,0:T(8,128)(2,1)S(1)}, bf16[2096,128]{1,0:T(8,128)(2,1)S(1)}, u32[]{:S(2)}, u32[]{:S(2)}) collective-permute-start(bf16[2096,128]{1,0:T(8,128)(2,1)S(1)} %mixing.1.refs_3_), channel_id=1, source_target_pairs={{31,0},{2,1},{1,2},{4,3},{3,4},{6,5},{5,6},{8,7},{7,8},{10,9},{9,1... | collective-permute-start | bytes 1609736 | tf_op jit(solution)/shard_map/ppermute | solution.py:481
  51.6 3.6 %collective-permute-start.9 = (bf16[2096,128]{1,0:T(8,128)(2,1)S(1)}, bf16[2096,128]{1,0:T(8,128)(2,1)S(1)}, u32[]{:S(2)}, u32[]{:S(2)}) collective-permute-start(bf16[2096,128]{1,0:T(8,128)(2,1)S(1)} %mixing.1.refs_3_), channel_id=1, source_target_pairs={{64,32},{32,64},{65,33},{33,65},{66,34},{34,66},{67,35},{35,67},{6... | collective-permute-start | bytes 1609736 | tf_op jit(solution)/shard_map/ppermute | solution.py:475
  55.2 0.0 collective-permute-done.11.refs_4_
  55.2 0.0 copy-done
  55.2 3.8 %own.1.refs_1_ = f32[2304,256]{1,0:T(8,128)S(1)} custom-call(bf16[2304,256]{1,0:T(8,128)(2,1)S(1)} %bitcast.5, f32[16,256]{1,0:T(8,128)S(1)} %get-tuple-element.31.table.refs_1_, f32[16,256]{1,0:T(8,128)S(1)} %collective-permute-done.3.table_2.refs_2_, bf16[2096,128]{1,0:T(8,128)(2,1)S(1)} %mixing.1.refs_3_, ...), custom_call_target="tpu_custom_call" | custom-call | flops 1610612736 | bytes 6000000 | tf_op jit(solution)/shard_map/own/pallas_call | solution.py:601
  59.1 1.9 %collective-permute-done.10.refs_5_ = bf16[2096,128]{1,0:T(8,128)(2,1)S(1)} collective-permute-done((bf16[2096,128]{1,0:T(8,128)(2,1)S(1)}, bf16[2096,128]{1,0:T(8,128)(2,1)S(1)}, u32[]{:S(2)}, u32[]{:S(2)}) %collective-permute-start.10) | collective-permute-done | bytes 536608 | tf_op jit(solution)/shard_map/ppermute | solution.py:475
  61.0 0.0 collective-permute-done.8.refs_7_
  61.0 2.6 %collective-permute-done.9.refs_6_ = bf16[2096,128]{1,0:T(8,128)(2,1)S(1)} collective-permute-done((bf16[2096,128]{1,0:T(8,128)(2,1)S(1)}, bf16[2096,128]{1,0:T(8,128)(2,1)S(1)}, u32[]{:S(2)}, u32[]{:S(2)}) %collective-permute-start.9) | collective-permute-done | bytes 536608 | tf_op jit(solution)/shard_map/ppermute | solution.py:475
  63.6 0.1 pad_maximum_fusion
  63.7 0.1 collective-permute-start.12
  63.8 0.1 collective-permute-start.13
  63.8 2.7 %collective-permute-start.14 = (bf16[2096,128]{1,0:T(8,128)(2,1)S(1)}, bf16[2096,128]{1,0:T(8,128)(2,1)S(1)}, u32[]{:S(2)}, u32[]{:S(2)}) collective-permute-start(bf16[2096,128]{1,0:T(8,128)(2,1)S(1)} %collective-permute-done.8.refs_7_), channel_id=1, source_target_pairs={{64,32},{32,64},{65,33},{33,65},{66,34},{34,66},{67,35},{35,67},{6... | collective-permute-start | bytes 1609736 | tf_op jit(solution)/shard_map/ppermute | solution.py:475
  66.5 6.8 %inner.1.refs_1_ = f32[2304,256]{1,0:T(8,128)S(1)} custom-call(bf16[2304,256]{1,0:T(8,128)(2,1)S(1)} %bitcast.6, f32[2304,256]{1,0:T(8,128)S(1)} %own.1.refs_1_, f32[16,256]{1,0:T(8,128)S(1)} %get-tuple-element.55.refs_2_, f32[16,256]{1,0:T(8,128)S(1)} %get-tuple-element.51.refs_3_, f32[16,256]{1,0:T(8,128)S(1)} %collective-permute-done.2.table_1.refs_4_, ...), custom_call_target="tpu_custom_call" | custom-call | flops 2415919104 | bytes 6000000 | tf_op jit(solution)/shard_map/inner/pallas_call | solution.py:601
  73.3 0.0 collective-permute-done.12.refs_6_.refs_7_
  73.3 5.1 %outer.1 = (f32[2304,256]{1,0:T(8,128)S(1)}, bf16[768,2048]{1,0:T(8,128)(2,1)S(1)}, bf16[768,2048]{1,0:T(8,128)(2,1)S(1)}) custom-call(bf16[2304,256]{1,0:T(8,128)(2,1)S(1)} %bitcast.7, f32[2304,256]{1,0:T(8,128)S(1)} %inner.1.refs_1_, f32[16,256]{1,0:T(8,128)S(1)} %get-tuple-element.56.refs_2_, f32[16,256]{1,0:T(8,128)S(1)} %get-tuple-element.50.refs_3_, ...), custom_call_target="tpu_custom_call" | custom-call | flops 1610612736 | bytes 6000000 | tf_op jit(solution)/shard_map/outer/pallas_call | solution.py:601
  78.5 0.0 collective-permute-done.13.refs_2_
  78.5 1.8 %collective-permute-done.14.refs_3_ = bf16[2096,128]{1,0:T(8,128)(2,1)S(1)} collective-permute-done((bf16[2096,128]{1,0:T(8,128)(2,1)S(1)}, bf16[2096,128]{1,0:T(8,128)(2,1)S(1)}, u32[]{:S(2)}, u32[]{:S(2)}) %collective-permute-start.14) | collective-permute-done | bytes 536608 | tf_op jit(solution)/shard_map/ppermute | solution.py:475
  80.3 4.8 %finish.1 = bf16[2304,256]{1,0:T(8,128)(2,1)} custom-call(f32[2304,256]{1,0:T(8,128)S(1)} %get-tuple-element.46.before, f32[16,256]{1,0:T(8,128)S(1)} %get-tuple-element.57.refs_4_.refs_0_, f32[16,256]{1,0:T(8,128)S(1)} %get-tuple-element.49.refs_5_.refs_1_, bf16[2096,128]{1,0:T(8,128)(2,1)S(1)} %collective-permute-done.13.refs_2_, ...), custom_call_target="tpu_custom_call" | custom-call | flops 1610612736 | bytes 9000000 | tf_op jit(solution)/shard_map/finish/pallas_call | solution.py:635
  (10 shorter events, 0.0 us)
Async XLA Ops:
  0.0 21.4 %collective-permute-start = (bf16[1536,256]{1,0:T(8,128)(2,1)}, bf16[1536,256]{1,0:T(8,128)(2,1)S(1)}, u32[]{:S(2)}, u32[]{:S(2)}) collective-permute-start(bf16[1536,256]{1,0:T(8,128)(2,1)} %bitcast.8), channel_id=1, source_target_pairs={{64,32},{32,64},{65,33},{33,65},{66,34},{34,66},{67,35},{35,67},{6... | collective-permute-start | bytes 2359304 | tf_op jit(solution)/shard_map/ppermute | solution.py:475
  2.4 19.3 %collective-permute-start.1 = (bf16[1536,256]{1,0:T(8,128)(2,1)}, bf16[1536,256]{1,0:T(8,128)(2,1)S(1)}, u32[]{:S(2)}, u32[]{:S(2)}) collective-permute-start(bf16[1536,256]{1,0:T(8,128)(2,1)} %bitcast.9), channel_id=1, source_target_pairs={{32,0},{0,32},{96,64},{64,96},{33,1},{1,33},{97,65},{65,97},{34,2}... | collective-permute-start | bytes 2359304 | tf_op jit(solution)/shard_map/ppermute | solution.py:475
  3.3 1.1 %copy-start.1 = (bf16[48,32,256]{2,1,0:T(8,128)(2,1)S(1)}, bf16[48,32,256]{2,1,0:T(8,128)(2,1)}, u32[]{:S(2)}) copy-start(bf16[48,32,256]{2,1,0:T(8,128)(2,1)} %param.8) | copy-start | bytes 2359300
  4.5 0.7 copy-start.3
  5.2 0.7 copy-start.4
  5.9 0.7 copy-start.5
  6.6 8.1 %copy-start.2 = (f32[8,64,32]{1,2,0:T(8,128)S(1)}, f32[8,64,32]{1,2,0:T(8,128)}, u32[]{:S(2)}) copy-start(f32[8,64,32]{1,2,0:T(8,128)} %param.12) | copy-start | bytes 196612
  8.9 12.8 %collective-permute-start.2 = (f32[16,256]{1,0:T(8,128)S(1)}, f32[16,256]{1,0:T(8,128)S(1)}, u32[]{:S(2)}, u32[]{:S(2)}) collective-permute-start(f32[16,256]{1,0:T(8,128)S(1)} %get-tuple-element.31.table.refs_1_), channel_id=1, source_target_pairs={{31,0},{2,1},{1,2},{4,3},{3,4},{6,5},{5,6},{8,7},{7,8},{10,9},{9,1... | collective-permute-start | bytes 49160 | tf_op jit(solution)/shard_map/ppermute | solution.py:481
  14.6 7.1 %collective-permute-start.3 = (f32[16,256]{1,0:T(8,128)S(1)}, f32[16,256]{1,0:T(8,128)S(1)}, u32[]{:S(2)}, u32[]{:S(2)}) collective-permute-start(f32[16,256]{1,0:T(8,128)S(1)} %get-tuple-element.31.table.refs_1_), channel_id=1, source_target_pairs={{1,0},{0,1},{3,2},{2,3},{5,4},{4,5},{7,6},{6,7},{9,8},{8,9},{11,10... | collective-permute-start | bytes 49160 | tf_op jit(solution)/shard_map/ppermute | solution.py:481
  23.0 10.4 %collective-permute-start.5 = (bf16[1536,256]{1,0:T(8,128)(2,1)S(1)}, bf16[1536,256]{1,0:T(8,128)(2,1)S(1)}, u32[]{:S(2)}, u32[]{:S(2)}) collective-permute-start(bf16[1536,256]{1,0:T(8,128)(2,1)S(1)} %get-tuple-element.34), channel_id=1, source_target_pairs={{1,0},{0,1},{3,2},{2,3},{5,4},{4,5},{7,6},{6,7},{9,8},{8,9},{11,10... | collective-permute-start | bytes 2359304 | tf_op jit(solution)/shard_map/ppermute | solution.py:481
  23.1 16.3 %collective-permute-start.4 = (bf16[1536,256]{1,0:T(8,128)(2,1)S(1)}, bf16[1536,256]{1,0:T(8,128)(2,1)S(1)}, u32[]{:S(2)}, u32[]{:S(2)}) collective-permute-start(bf16[1536,256]{1,0:T(8,128)(2,1)S(1)} %get-tuple-element.32), channel_id=1, source_target_pairs={{31,0},{2,1},{1,2},{4,3},{3,4},{6,5},{5,6},{8,7},{7,8},{10,9},{9,1... | collective-permute-start | bytes 2359304 | tf_op jit(solution)/shard_map/ppermute | solution.py:481
  29.7 8.0 %collective-permute-start.6 = (f32[48,256]{1,0:T(8,128)S(1)}, f32[48,256]{1,0:T(8,128)S(1)}, u32[]{:S(2)}, u32[]{:S(2)}) collective-permute-start(f32[48,256]{1,0:T(8,128)S(1)} %constant_dynamic-update-slice_fusion.metas), channel_id=1, source_target_pairs={{64,32},{32,64},{65,33},{33,65},{66,34},{34,66},{67,35},{35,67},{6... | collective-permute-start | bytes 147464 | tf_op jit(solution)/shard_map/ppermute | solution.py:475
  33.1 4.6 %collective-permute-start.7 = (f32[48,256]{1,0:T(8,128)S(1)}, f32[48,256]{1,0:T(8,128)S(1)}, u32[]{:S(2)}, u32[]{:S(2)}) collective-permute-start(f32[48,256]{1,0:T(8,128)S(1)} %constant_dynamic-update-slice_fusion.metas), channel_id=1, source_target_pairs={{32,0},{0,32},{96,64},{64,96},{33,1},{1,33},{97,65},{65,97},{34,2}... | collective-permute-start | bytes 147464 | tf_op jit(solution)/shard_map/ppermute | solution.py:475
  39.4 15.8 %copy-start = (bf16[48,48,256]{2,1,0:T(8,128)(2,1)S(1)}, bf16[48,48,256]{2,1,0:T(8,128)(2,1)}, u32[]{:S(2)}) copy-start(bf16[48,48,256]{2,1,0:T(8,128)(2,1)} %param.7) | copy-start | bytes 3538948
  46.3 8.9 %collective-permute-start.11 = (bf16[2096,128]{1,0:T(8,128)(2,1)S(1)}, bf16[2096,128]{1,0:T(8,128)(2,1)S(1)}, u32[]{:S(2)}, u32[]{:S(2)}) collective-permute-start(bf16[2096,128]{1,0:T(8,128)(2,1)S(1)} %mixing.1.refs_3_), channel_id=1, source_target_pairs={{1,0},{0,1},{3,2},{2,3},{5,4},{4,5},{7,6},{6,7},{9,8},{8,9},{11,10... | collective-permute-start | bytes 1609736 | tf_op jit(solution)/shard_map/ppermute | solution.py:481
  46.4 14.6 %collective-permute-start.10 = (bf16[2096,128]{1,0:T(8,128)(2,1)S(1)}, bf16[2096,128]{1,0:T(8,128)(2,1)S(1)}, u32[]{:S(2)}, u32[]{:S(2)}) collective-permute-start(bf16[2096,128]{1,0:T(8,128)(2,1)S(1)} %mixing.1.refs_3_), channel_id=1, source_target_pairs={{32,0},{0,32},{96,64},{64,96},{33,1},{1,33},{97,65},{65,97},{34,2}... | collective-permute-start | bytes 1609736 | tf_op jit(solution)/shard_map/ppermute | solution.py:475
  47.5 13.5 %collective-permute-start.8 = (bf16[2096,128]{1,0:T(8,128)(2,1)S(1)}, bf16[2096,128]{1,0:T(8,128)(2,1)S(1)}, u32[]{:S(2)}, u32[]{:S(2)}) collective-permute-start(bf16[2096,128]{1,0:T(8,128)(2,1)S(1)} %mixing.1.refs_3_), channel_id=1, source_target_pairs={{31,0},{2,1},{1,2},{4,3},{3,4},{6,5},{5,6},{8,7},{7,8},{10,9},{9,1... | collective-permute-start | bytes 1609736 | tf_op jit(solution)/shard_map/ppermute | solution.py:481
  51.6 12.0 %collective-permute-start.9 = (bf16[2096,128]{1,0:T(8,128)(2,1)S(1)}, bf16[2096,128]{1,0:T(8,128)(2,1)S(1)}, u32[]{:S(2)}, u32[]{:S(2)}) collective-permute-start(bf16[2096,128]{1,0:T(8,128)(2,1)S(1)} %mixing.1.refs_3_), channel_id=1, source_target_pairs={{64,32},{32,64},{65,33},{33,65},{66,34},{34,66},{67,35},{35,67},{6... | collective-permute-start | bytes 1609736 | tf_op jit(solution)/shard_map/ppermute | solution.py:475
  63.7 9.7 %collective-permute-start.12 = (bf16[4192,128]{1,0:T(8,128)(2,1)S(1)}, bf16[4192,128]{1,0:T(8,128)(2,1)S(1)}, u32[]{:S(2)}, u32[]{:S(2)}) collective-permute-start(bf16[4192,128]{1,0:T(8,128)(2,1)S(1)} %pad_maximum_fusion), channel_id=1, source_target_pairs={{1,0},{0,1},{3,2},{2,3},{5,4},{4,5},{7,6},{6,7},{9,8},{8,9},{11,10... | collective-permute-start | bytes 3219464 | tf_op jit(solution)/shard_map/ppermute | solution.py:481
  63.8 14.7 %collective-permute-start.13 = (bf16[2096,128]{1,0:T(8,128)(2,1)S(1)}, bf16[2096,128]{1,0:T(8,128)(2,1)S(1)}, u32[]{:S(2)}, u32[]{:S(2)}) collective-permute-start(bf16[2096,128]{1,0:T(8,128)(2,1)S(1)} %collective-permute-done.8.refs_7_), channel_id=1, source_target_pairs={{32,0},{0,32},{96,64},{64,96},{33,1},{1,33},{97,65},{65,97},{34,2}... | collective-permute-start | bytes 1609736 | tf_op jit(solution)/shard_map/ppermute | solution.py:475
  63.8 16.4 %collective-permute-start.14 = (bf16[2096,128]{1,0:T(8,128)(2,1)S(1)}, bf16[2096,128]{1,0:T(8,128)(2,1)S(1)}, u32[]{:S(2)}, u32[]{:S(2)}) collective-permute-start(bf16[2096,128]{1,0:T(8,128)(2,1)S(1)} %collective-permute-done.8.refs_7_), channel_id=1, source_target_pairs={{64,32},{32,64},{65,33},{33,65},{66,34},{34,66},{67,35},{35,67},{6... | collective-permute-start | bytes 1609736 | tf_op jit(solution)/shard_map/ppermute | solution.py:475

commit v6 on v5

--- a/solution.py
+++ b/solution.py
@@ -619,9 +619,10 @@
         arrived[lon, SELF] = (from_lon(mix, lon), 0)
     mix_2 = from_band(mix, SECOND)
     mix_1 = from_band(mix, FIRST)
-    (acc,) = increments(None, [(SELF, SELF), (SECOND, SELF)], [], "own")
-    near, mix_2, mix_1, acc = lax.optimization_barrier(
-        (arrived[FIRST, SELF][0], mix_2, mix_1, acc)
+    last = [(FIRST, FIRST), (FIRST, SECOND)]
+    acc, *lefts = increments(None, [(SELF, SELF), (SECOND, SELF)], last, "own")
+    mix_1, mix_2, near, acc = lax.optimization_barrier(
+        (mix_1, mix_2, arrived[FIRST, SELF][0], acc)
     )
     arrived[FIRST, SELF] = (near, 0)
     arrived[FIRST, FIRST] = (from_band(near, FIRST), 0)
@@ -629,9 +630,8 @@
     arrived[SELF, FIRST], arrived[SELF, SECOND] = (mix_1, 0), (mix_2, 0)
     both = from_lon(jnp.concatenate([mix_1, mix_2], axis=0), SECOND)
     arrived[SECOND, FIRST], arrived[SECOND, SECOND] = (both, 0), (both, 1)
-    last = [(FIRST, FIRST), (FIRST, SECOND)]
     (acc,) = increments(acc, [(SELF, FIRST), (SELF, SECOND), (FIRST, SELF)], [], "inner")
-    acc, *lefts = increments(acc, [(SECOND, FIRST), (SECOND, SECOND)], last, "outer")
+    (acc,) = increments(acc, [(SECOND, FIRST), (SECOND, SECOND)], [], "outer")
     out = call(
         functools.partial(
             finish_kernel,

time: 85.7 us -> 85.7 us (level)
    ppermute x8, starting transfers between devices: 13.6 us -> 12.7 us  [from_band(): return lax.ppermute(x, 'band', [(j, i) for j, i in pairs if 0 <= j < count])]
  transfers between devices with their start and end apart: 15 -> 15, of which waited for: 6 -> 7; matrix products, arithmetic and copies ran while one was open for 1% -> 1% of each run, Pallas kernels for 29% -> 29%
where the time goes in v6:
time: 85.7 us; the launch traced here: 85.1 us
  Pallas kernels  38 us (44%)
  starting transfers between devices  30.1 us (35%)
  waiting for transfers between devices  12.7 us (15%)
  local copies, waits for them, and re-layouts  4.05 us (5%)
    ppermute x7, starting transfers between devices, from_lon(): lax.ppermute(x, 'lon', [((i + step * (1 - 2 * (i % 2))) % count, i) for i...  17.4 us
    pallas_call x3, Pallas kernels, increments(): call(kernel, (acc_shape,) + (left_shape,) * len(ahead), [VMEM_SPEC] * (1...  15.8 us
    ppermute x8, starting transfers between devices, from_band(): return lax.ppermute(x, 'band', [(j, i) for j, i in pairs if 0 <= j < count])  12.7 us
    ppermute x8, waiting for transfers between devices, from_band(): return lax.ppermute(x, 'band', [(j, i) for j, i in pairs if 0 <= j < count])  11.6 us
    pallas_call x1, Pallas kernels, local(): call(functools.partial(mix_kernel, 4), jax.ShapeDtypeStruct((packed_rows(...  6.92 us
    pallas_call x1, Pallas kernels, local(): call(functools.partial(finish_kernel, [slots(*g) for g in last], [arrived...  4.8 us
    pallas_call x1, Pallas kernels, local(): call(functools.partial(near_gram_kernel, obs_rows, regions), (jax.ShapeDt...  4.26 us
    unnamed x15, local copies, waits for them, and re-layouts  4.04 us
  transfers between devices with their start and end apart: 15, of which 7 were waited for; matrix products, arithmetic and copies ran while one was open for 1% of the time, Pallas kernels for 29%

profile of v6, /device:TPU:4, one launch (start us, length us, event | category | flops | bytes accessed | tf_op | source)
XLA Modules:
  0.0 85.1 jit_solution(17221548904536276674)
XLA Ops:
  0.0 2.4 %collective-permute-start = (bf16[1536,256]{1,0:T(8,128)(2,1)}, bf16[1536,256]{1,0:T(8,128)(2,1)S(1)}, u32[]{:S(2)}, u32[]{:S(2)}) collective-permute-start(bf16[1536,256]{1,0:T(8,128)(2,1)} %bitcast.8), channel_id=1, source_target_pairs={{64,32},{32,64},{65,33},{33,65},{66,34},{34,66},{67,35},{35,67},{6... | collective-permute-start | bytes 2359304 | tf_op jit(solution)/shard_map/ppermute | solution.py:475
  2.4 0.1 collective-permute-start.1
  2.5 0.8 copy.8.refs_3_
  3.3 1.1 %copy-done.1 = bf16[48,32,256]{2,1,0:T(8,128)(2,1)S(1)} copy-done((bf16[48,32,256]{2,1,0:T(8,128)(2,1)S(1)}, bf16[48,32,256]{2,1,0:T(8,128)(2,1)}, u32[]{:S(2)}) %copy-start.1) | copy-done | bytes 786456
  4.5 0.7 copy-done.3
  5.2 0.7 copy-done.4
  5.9 0.7 copy-done.5
  6.6 2.3 %tables.1 = (f32[16,256]{1,0:T(8,128)S(1)}, f32[512,128]{1,0:T(8,128)S(1)}, bf16[1536,256]{1,0:T(8,128)(2,1)S(1)}) custom-call(s32[8,64]{1,0:T(8,128)S(1)} %copy-done.4, s32[48,128]{1,0:T(8,128)S(1)} %bitcast.12, f32[8,64]{1,0:T(8,128)S(1)} %copy-done.5, bf16[48,32]{1,0:T(8,128)(2,1)S(1)} %copy.8.refs_3_, bf16[1536,256]{1,0:T(8,128)(2,1)S(1)} %bitcast.10), custom_call_target="tpu_custom_call" | custom-call | flops 1000000000 | bytes 1000000 | tf_op jit(solution)/shard_map/tables/pallas_call | solution.py:497
  8.9 5.7 %collective-permute-start.2 = (f32[16,256]{1,0:T(8,128)S(1)}, f32[16,256]{1,0:T(8,128)S(1)}, u32[]{:S(2)}, u32[]{:S(2)}) collective-permute-start(f32[16,256]{1,0:T(8,128)S(1)} %get-tuple-element.31.table.refs_1_), channel_id=1, source_target_pairs={{31,0},{2,1},{1,2},{4,3},{3,4},{6,5},{5,6},{8,7},{7,8},{10,9},{9,1... | collective-permute-start | bytes 49160 | tf_op jit(solution)/shard_map/ppermute | solution.py:481
  14.6 0.0 collective-permute-start.3
  14.6 0.0 copy-done.2
  14.6 2.0 %weights.1 = f32[8,4608]{1,0:T(8,128)S(1)} custom-call(f32[512,128]{1,0:T(8,128)S(1)} %get-tuple-element.28.entry_slot, f32[8,32,64]{2,1,0:T(8,128)S(1)} %bitcast.11), custom_call_target="tpu_custom_call" | custom-call | flops 1000000000 | bytes 1000000 | tf_op jit(solution)/shard_map/weights/pallas_call | solution.py:519
  16.6 4.8 %collective-permute-done.obs_2 = bf16[1536,256]{1,0:T(8,128)(2,1)S(1)} collective-permute-done((bf16[1536,256]{1,0:T(8,128)(2,1)}, bf16[1536,256]{1,0:T(8,128)(2,1)S(1)}, u32[]{:S(2)}, u32[]{:S(2)}) %collective-permute-start) | collective-permute-done | bytes 786464 | tf_op jit(solution)/shard_map/ppermute | solution.py:475
  21.4 0.4 collective-permute-done.1.obs_1
  21.7 0.0 collective-permute-done.2.table_1.refs_4_
  21.7 0.0 collective-permute-done.3.table_2.refs_2_
  21.7 1.3 %select.1 = (bf16[1536,256]{1,0:T(8,128)(2,1)S(1)}, bf16[1536,256]{1,0:T(8,128)(2,1)S(1)}) custom-call(bf16[1536,256]{1,0:T(8,128)(2,1)S(1)} %get-tuple-element.27.obs, bf16[1536,256]{1,0:T(8,128)(2,1)S(1)} %collective-permute-done.1.obs_1, bf16[1536,256]{1,0:T(8,128)(2,1)S(1)} %collective-permute-done.obs_2, ...), custom_call_target="tpu_custom_call" | custom-call | flops 100000000 | bytes 4000000 | tf_op jit(solution)/shard_map/select/pallas_call | solution.py:530
  23.0 0.1 collective-permute-start.5
  23.1 6.6 %collective-permute-start.4 = (bf16[1536,256]{1,0:T(8,128)(2,1)S(1)}, bf16[1536,256]{1,0:T(8,128)(2,1)S(1)}, u32[]{:S(2)}, u32[]{:S(2)}) collective-permute-start(bf16[1536,256]{1,0:T(8,128)(2,1)S(1)} %get-tuple-element.32), channel_id=1, source_target_pairs={{31,0},{2,1},{1,2},{4,3},{3,4},{6,5},{5,6},{8,7},{7,8},{10,9},{9,1... | collective-permute-start | bytes 2359304 | tf_op jit(solution)/shard_map/ppermute | solution.py:481
  29.7 3.4 %collective-permute-start.6 = (f32[48,256]{1,0:T(8,128)S(1)}, f32[48,256]{1,0:T(8,128)S(1)}, u32[]{:S(2)}, u32[]{:S(2)}) collective-permute-start(f32[48,256]{1,0:T(8,128)S(1)} %constant_dynamic-update-slice_fusion.metas), channel_id=1, source_target_pairs={{64,32},{32,64},{65,33},{33,65},{66,34},{34,66},{67,35},{35,67},{6... | collective-permute-start | bytes 147464 | tf_op jit(solution)/shard_map/ppermute | solution.py:475
  33.1 0.3 collective-permute-start.7
  33.4 0.0 collective-permute-done.5.pool_2
  33.4 4.3 %near_gram.1 = (f32[2048,256]{1,0:T(8,128)S(1)}, bf16[1536,256]{1,0:T(8,128)(2,1)S(1)}) custom-call(bf16[1536,256]{1,0:T(8,128)(2,1)S(1)} %get-tuple-element.27.obs, bf16[1536,256]{1,0:T(8,128)(2,1)S(1)} %collective-permute-done.1.obs_1, bf16[1536,256]{1,0:T(8,128)(2,1)S(1)} %collective-permute-done.obs_2, ...), custom_call_target="tpu_custom_call" | custom-call | flops 3221225472 | bytes 5000000 | tf_op jit(solution)/shard_map/near_gram/pallas_call | solution.py:545
  37.7 0.0 collective-permute-done.6.metas_2
  37.7 0.0 collective-permute-done.7.metas_1
  37.7 0.6 innov.1
  38.3 1.0 %collective-permute-done.4.pool = bf16[1536,256]{1,0:T(8,128)(2,1)S(1)} collective-permute-done((bf16[1536,256]{1,0:T(8,128)(2,1)S(1)}, bf16[1536,256]{1,0:T(8,128)(2,1)S(1)}, u32[]{:S(2)}, u32[]{:S(2)}) %collective-permute-start.4) | collective-permute-done | bytes 786464 | tf_op jit(solution)/shard_map/ppermute | solution.py:481
  39.4 6.9 %mixing.1.refs_5_ = bf16[2096,128]{1,0:T(8,128)(2,1)S(1)} custom-call(bf16[1536,256]{1,0:T(8,128)(2,1)S(1)} %collective-permute-done.4.pool, f32[8,4608]{1,0:T(8,128)S(1)} %weights.1, f32[2048,256]{1,0:T(8,128)S(1)} %get-tuple-element.35.gram_near, bf16[16,4608]{1,0:T(8,128)(2,1)S(1)} %get-tuple-element.40.scaled, f32[8,256]{1,0:T(8,128)S(1)} %get-tuple-element.41.proj_near), custom_call_target="tpu_custom_call" | custom-call | flops 4831838208 | bytes 4000000 | tf_op jit(solution)/shard_map/mixing/pallas_call | solution.py:563
  46.3 0.1 collective-permute-start.11
  46.4 1.1 %collective-permute-start.8 = (bf16[2096,128]{1,0:T(8,128)(2,1)S(1)}, bf16[2096,128]{1,0:T(8,128)(2,1)S(1)}, u32[]{:S(2)}, u32[]{:S(2)}) collective-permute-start(bf16[2096,128]{1,0:T(8,128)(2,1)S(1)} %mixing.1.refs_5_), channel_id=1, source_target_pairs={{32,0},{0,32},{96,64},{64,96},{33,1},{1,33},{97,65},{65,97},{34,2}... | collective-permute-start | bytes 1609736 | tf_op jit(solution)/shard_map/ppermute | solution.py:475
  47.5 2.7 %collective-permute-start.9 = (bf16[2096,128]{1,0:T(8,128)(2,1)S(1)}, bf16[2096,128]{1,0:T(8,128)(2,1)S(1)}, u32[]{:S(2)}, u32[]{:S(2)}) collective-permute-start(bf16[2096,128]{1,0:T(8,128)(2,1)S(1)} %mixing.1.refs_5_), channel_id=1, source_target_pairs={{64,32},{32,64},{65,33},{33,65},{66,34},{34,66},{67,35},{35,67},{6... | collective-permute-start | bytes 1609736 | tf_op jit(solution)/shard_map/ppermute | solution.py:475
  50.2 4.8 %collective-permute-start.10 = (bf16[2096,128]{1,0:T(8,128)(2,1)S(1)}, bf16[2096,128]{1,0:T(8,128)(2,1)S(1)}, u32[]{:S(2)}, u32[]{:S(2)}) collective-permute-start(bf16[2096,128]{1,0:T(8,128)(2,1)S(1)} %mixing.1.refs_5_), channel_id=1, source_target_pairs={{31,0},{2,1},{1,2},{4,3},{3,4},{6,5},{5,6},{8,7},{7,8},{10,9},{9,1... | collective-permute-start | bytes 1609736 | tf_op jit(solution)/shard_map/ppermute | solution.py:481
  55.0 0.0 collective-permute-done.11.refs_6_
  55.0 0.0 copy-done
  55.0 5.1 %own.1 = (f32[2304,256]{1,0:T(8,128)S(1)}, bf16[768,2048]{1,0:T(8,128)(2,1)S(1)}, bf16[768,2048]{1,0:T(8,128)(2,1)S(1)}) custom-call(bf16[2304,256]{1,0:T(8,128)(2,1)S(1)} %bitcast.5, f32[16,256]{1,0:T(8,128)S(1)} %get-tuple-element.31.table.refs_1_, f32[16,256]{1,0:T(8,128)S(1)} %collective-permute-done.3.table_2.refs_2_, ...), custom_call_target="tpu_custom_call" | custom-call | flops 1610612736 | bytes 6000000 | tf_op jit(solution)/shard_map/own/pallas_call | solution.py:601
  60.2 0.9 %collective-permute-done.8.refs_5_ = bf16[2096,128]{1,0:T(8,128)(2,1)S(1)} collective-permute-done((bf16[2096,128]{1,0:T(8,128)(2,1)S(1)}, bf16[2096,128]{1,0:T(8,128)(2,1)S(1)}, u32[]{:S(2)}, u32[]{:S(2)}) %collective-permute-start.8) | collective-permute-done | bytes 536608 | tf_op jit(solution)/shard_map/ppermute | solution.py:475
  61.0 2.6 %collective-permute-done.9.refs_6_ = bf16[2096,128]{1,0:T(8,128)(2,1)S(1)} collective-permute-done((bf16[2096,128]{1,0:T(8,128)(2,1)S(1)}, bf16[2096,128]{1,0:T(8,128)(2,1)S(1)}, u32[]{:S(2)}, u32[]{:S(2)}) %collective-permute-start.9) | collective-permute-done | bytes 536608 | tf_op jit(solution)/shard_map/ppermute | solution.py:475
  63.6 0.0 collective-permute-done.10.refs_7_
  63.6 0.1 pad_maximum_fusion
  63.7 0.1 collective-permute-start.12
  63.8 0.1 collective-permute-start.13
  63.9 2.7 %collective-permute-start.14 = (bf16[2096,128]{1,0:T(8,128)(2,1)S(1)}, bf16[2096,128]{1,0:T(8,128)(2,1)S(1)}, u32[]{:S(2)}, u32[]{:S(2)}) collective-permute-start(bf16[2096,128]{1,0:T(8,128)(2,1)S(1)} %collective-permute-done.10.refs_7_), channel_id=1, source_target_pairs={{64,32},{32,64},{65,33},{33,65},{66,34},{34,66},{67,35},{35,67},{6... | collective-permute-start | bytes 1609736 | tf_op jit(solution)/shard_map/ppermute | solution.py:475
  66.6 6.8 %inner.1.refs_1_ = f32[2304,256]{1,0:T(8,128)S(1)} custom-call(bf16[2304,256]{1,0:T(8,128)(2,1)S(1)} %bitcast.6, f32[2304,256]{1,0:T(8,128)S(1)} %get-tuple-element.43.refs_1_, f32[16,256]{1,0:T(8,128)S(1)} %get-tuple-element.56.refs_2_, f32[16,256]{1,0:T(8,128)S(1)} %get-tuple-element.50.refs_3_, f32[16,256]{1,0:T(8,128)S(1)} %collective-permute-done.2.table_1.refs_4_, ...), custom_call_target="tpu_custom_call" | custom-call | flops 2415919104 | bytes 6000000 | tf_op jit(solution)/shard_map/inner/pallas_call | solution.py:601
  73.4 0.0 collective-permute-done.12.refs_4_.refs_5_
  73.4 3.9 %outer.1.before = f32[2304,256]{1,0:T(8,128)S(1)} custom-call(bf16[2304,256]{1,0:T(8,128)(2,1)S(1)} %bitcast.7, f32[2304,256]{1,0:T(8,128)S(1)} %inner.1.refs_1_, f32[16,256]{1,0:T(8,128)S(1)} %get-tuple-element.57.refs_2_, f32[16,256]{1,0:T(8,128)S(1)} %get-tuple-element.49.refs_3_, bf16[4192,128]{1,0:T(8,128)(2,1)S(1)} %collective-permute-done.12.refs_4_.refs_5_, ...), custom_call_target="tpu_custom_call" | custom-call | flops 1610612736 | bytes 6000000 | tf_op jit(solution)/shard_map/outer/pallas_call | solution.py:601
  77.3 1.1 %collective-permute-done.13.refs_2_ = bf16[2096,128]{1,0:T(8,128)(2,1)S(1)} collective-permute-done((bf16[2096,128]{1,0:T(8,128)(2,1)S(1)}, bf16[2096,128]{1,0:T(8,128)(2,1)S(1)}, u32[]{:S(2)}, u32[]{:S(2)}) %collective-permute-start.13) | collective-permute-done | bytes 536608 | tf_op jit(solution)/shard_map/ppermute | solution.py:475
  78.4 1.9 %collective-permute-done.14.refs_3_ = bf16[2096,128]{1,0:T(8,128)(2,1)S(1)} collective-permute-done((bf16[2096,128]{1,0:T(8,128)(2,1)S(1)}, bf16[2096,128]{1,0:T(8,128)(2,1)S(1)}, u32[]{:S(2)}, u32[]{:S(2)}) %collective-permute-start.14) | collective-permute-done | bytes 536608 | tf_op jit(solution)/shard_map/ppermute | solution.py:475
  80.3 4.8 %finish.1 = bf16[2304,256]{1,0:T(8,128)(2,1)} custom-call(f32[2304,256]{1,0:T(8,128)S(1)} %outer.1.before, f32[16,256]{1,0:T(8,128)S(1)} %get-tuple-element.55.refs_3_.refs_0_, f32[16,256]{1,0:T(8,128)S(1)} %get-tuple-element.51.refs_4_.refs_1_, bf16[2096,128]{1,0:T(8,128)(2,1)S(1)} %collective-permute-done.13.refs_2_, ...), custom_call_target="tpu_custom_call" | custom-call | flops 1610612736 | bytes 9000000 | tf_op jit(solution)/shard_map/finish/pallas_call | solution.py:635
  (10 shorter events, 0.0 us)
Async XLA Ops:
  0.0 21.4 %collective-permute-start = (bf16[1536,256]{1,0:T(8,128)(2,1)}, bf16[1536,256]{1,0:T(8,128)(2,1)S(1)}, u32[]{:S(2)}, u32[]{:S(2)}) collective-permute-start(bf16[1536,256]{1,0:T(8,128)(2,1)} %bitcast.8), channel_id=1, source_target_pairs={{64,32},{32,64},{65,33},{33,65},{66,34},{34,66},{67,35},{35,67},{6... | collective-permute-start | bytes 2359304 | tf_op jit(solution)/shard_map/ppermute | solution.py:475
  2.4 19.3 %collective-permute-start.1 = (bf16[1536,256]{1,0:T(8,128)(2,1)}, bf16[1536,256]{1,0:T(8,128)(2,1)S(1)}, u32[]{:S(2)}, u32[]{:S(2)}) collective-permute-start(bf16[1536,256]{1,0:T(8,128)(2,1)} %bitcast.9), channel_id=1, source_target_pairs={{32,0},{0,32},{96,64},{64,96},{33,1},{1,33},{97,65},{65,97},{34,2}... | collective-permute-start | bytes 2359304 | tf_op jit(solution)/shard_map/ppermute | solution.py:475
  3.3 1.1 %copy-start.1 = (bf16[48,32,256]{2,1,0:T(8,128)(2,1)S(1)}, bf16[48,32,256]{2,1,0:T(8,128)(2,1)}, u32[]{:S(2)}) copy-start(bf16[48,32,256]{2,1,0:T(8,128)(2,1)} %param.8) | copy-start | bytes 2359300
  4.5 0.7 copy-start.3
  5.2 0.7 copy-start.4
  5.9 0.7 copy-start.5
  6.6 8.1 %copy-start.2 = (f32[8,64,32]{1,2,0:T(8,128)S(1)}, f32[8,64,32]{1,2,0:T(8,128)}, u32[]{:S(2)}) copy-start(f32[8,64,32]{1,2,0:T(8,128)} %param.12) | copy-start | bytes 196612
  8.9 12.8 %collective-permute-start.2 = (f32[16,256]{1,0:T(8,128)S(1)}, f32[16,256]{1,0:T(8,128)S(1)}, u32[]{:S(2)}, u32[]{:S(2)}) collective-permute-start(f32[16,256]{1,0:T(8,128)S(1)} %get-tuple-element.31.table.refs_1_), channel_id=1, source_target_pairs={{31,0},{2,1},{1,2},{4,3},{3,4},{6,5},{5,6},{8,7},{7,8},{10,9},{9,1... | collective-permute-start | bytes 49160 | tf_op jit(solution)/shard_map/ppermute | solution.py:481
  14.6 7.1 %collective-permute-start.3 = (f32[16,256]{1,0:T(8,128)S(1)}, f32[16,256]{1,0:T(8,128)S(1)}, u32[]{:S(2)}, u32[]{:S(2)}) collective-permute-start(f32[16,256]{1,0:T(8,128)S(1)} %get-tuple-element.31.table.refs_1_), channel_id=1, source_target_pairs={{1,0},{0,1},{3,2},{2,3},{5,4},{4,5},{7,6},{6,7},{9,8},{8,9},{11,10... | collective-permute-start | bytes 49160 | tf_op jit(solution)/shard_map/ppermute | solution.py:481
  23.0 10.4 %collective-permute-start.5 = (bf16[1536,256]{1,0:T(8,128)(2,1)S(1)}, bf16[1536,256]{1,0:T(8,128)(2,1)S(1)}, u32[]{:S(2)}, u32[]{:S(2)}) collective-permute-start(bf16[1536,256]{1,0:T(8,128)(2,1)S(1)} %get-tuple-element.34), channel_id=1, source_target_pairs={{1,0},{0,1},{3,2},{2,3},{5,4},{4,5},{7,6},{6,7},{9,8},{8,9},{11,10... | collective-permute-start | bytes 2359304 | tf_op jit(solution)/shard_map/ppermute | solution.py:481
  23.1 16.3 %collective-permute-start.4 = (bf16[1536,256]{1,0:T(8,128)(2,1)S(1)}, bf16[1536,256]{1,0:T(8,128)(2,1)S(1)}, u32[]{:S(2)}, u32[]{:S(2)}) collective-permute-start(bf16[1536,256]{1,0:T(8,128)(2,1)S(1)} %get-tuple-element.32), channel_id=1, source_target_pairs={{31,0},{2,1},{1,2},{4,3},{3,4},{6,5},{5,6},{8,7},{7,8},{10,9},{9,1... | collective-permute-start | bytes 2359304 | tf_op jit(solution)/shard_map/ppermute | solution.py:481
  29.7 8.0 %collective-permute-start.6 = (f32[48,256]{1,0:T(8,128)S(1)}, f32[48,256]{1,0:T(8,128)S(1)}, u32[]{:S(2)}, u32[]{:S(2)}) collective-permute-start(f32[48,256]{1,0:T(8,128)S(1)} %constant_dynamic-update-slice_fusion.metas), channel_id=1, source_target_pairs={{64,32},{32,64},{65,33},{33,65},{66,34},{34,66},{67,35},{35,67},{6... | collective-permute-start | bytes 147464 | tf_op jit(solution)/shard_map/ppermute | solution.py:475
  33.1 4.6 %collective-permute-start.7 = (f32[48,256]{1,0:T(8,128)S(1)}, f32[48,256]{1,0:T(8,128)S(1)}, u32[]{:S(2)}, u32[]{:S(2)}) collective-permute-start(f32[48,256]{1,0:T(8,128)S(1)} %constant_dynamic-update-slice_fusion.metas), channel_id=1, source_target_pairs={{32,0},{0,32},{96,64},{64,96},{33,1},{1,33},{97,65},{65,97},{34,2}... | collective-permute-start | bytes 147464 | tf_op jit(solution)/shard_map/ppermute | solution.py:475
  39.4 15.6 %copy-start = (bf16[48,48,256]{2,1,0:T(8,128)(2,1)S(1)}, bf16[48,48,256]{2,1,0:T(8,128)(2,1)}, u32[]{:S(2)}) copy-start(bf16[48,48,256]{2,1,0:T(8,128)(2,1)} %param.7) | copy-start | bytes 3538948
  46.3 8.7 %collective-permute-start.11 = (bf16[2096,128]{1,0:T(8,128)(2,1)S(1)}, bf16[2096,128]{1,0:T(8,128)(2,1)S(1)}, u32[]{:S(2)}, u32[]{:S(2)}) collective-permute-start(bf16[2096,128]{1,0:T(8,128)(2,1)S(1)} %mixing.1.refs_5_), channel_id=1, source_target_pairs={{1,0},{0,1},{3,2},{2,3},{5,4},{4,5},{7,6},{6,7},{9,8},{8,9},{11,10... | collective-permute-start | bytes 1609736 | tf_op jit(solution)/shard_map/ppermute | solution.py:481
  46.4 14.6 %collective-permute-start.8 = (bf16[2096,128]{1,0:T(8,128)(2,1)S(1)}, bf16[2096,128]{1,0:T(8,128)(2,1)S(1)}, u32[]{:S(2)}, u32[]{:S(2)}) collective-permute-start(bf16[2096,128]{1,0:T(8,128)(2,1)S(1)} %mixing.1.refs_5_), channel_id=1, source_target_pairs={{32,0},{0,32},{96,64},{64,96},{33,1},{1,33},{97,65},{65,97},{34,2}... | collective-permute-start | bytes 1609736 | tf_op jit(solution)/shard_map/ppermute | solution.py:475
  47.5 16.1 %collective-permute-start.9 = (bf16[2096,128]{1,0:T(8,128)(2,1)S(1)}, bf16[2096,128]{1,0:T(8,128)(2,1)S(1)}, u32[]{:S(2)}, u32[]{:S(2)}) collective-permute-start(bf16[2096,128]{1,0:T(8,128)(2,1)S(1)} %mixing.1.refs_5_), channel_id=1, source_target_pairs={{64,32},{32,64},{65,33},{33,65},{66,34},{34,66},{67,35},{35,67},{6... | collective-permute-start | bytes 1609736 | tf_op jit(solution)/shard_map/ppermute | solution.py:475
  50.2 13.5 %collective-permute-start.10 = (bf16[2096,128]{1,0:T(8,128)(2,1)S(1)}, bf16[2096,128]{1,0:T(8,128)(2,1)S(1)}, u32[]{:S(2)}, u32[]{:S(2)}) collective-permute-start(bf16[2096,128]{1,0:T(8,128)(2,1)S(1)} %mixing.1.refs_5_), channel_id=1, source_target_pairs={{31,0},{2,1},{1,2},{4,3},{3,4},{6,5},{5,6},{8,7},{7,8},{10,9},{9,1... | collective-permute-start | bytes 1609736 | tf_op jit(solution)/shard_map/ppermute | solution.py:481
  63.7 9.7 %collective-permute-start.12 = (bf16[4192,128]{1,0:T(8,128)(2,1)S(1)}, bf16[4192,128]{1,0:T(8,128)(2,1)S(1)}, u32[]{:S(2)}, u32[]{:S(2)}) collective-permute-start(bf16[4192,128]{1,0:T(8,128)(2,1)S(1)} %pad_maximum_fusion), channel_id=1, source_target_pairs={{1,0},{0,1},{3,2},{2,3},{5,4},{4,5},{7,6},{6,7},{9,8},{8,9},{11,10... | collective-permute-start | bytes 3219464 | tf_op jit(solution)/shard_map/ppermute | solution.py:481
  63.8 14.6 %collective-permute-start.13 = (bf16[2096,128]{1,0:T(8,128)(2,1)S(1)}, bf16[2096,128]{1,0:T(8,128)(2,1)S(1)}, u32[]{:S(2)}, u32[]{:S(2)}) collective-permute-start(bf16[2096,128]{1,0:T(8,128)(2,1)S(1)} %collective-permute-done.10.refs_7_), channel_id=1, source_target_pairs={{32,0},{0,32},{96,64},{64,96},{33,1},{1,33},{97,65},{65,97},{34,2}... | collective-permute-start | bytes 1609736 | tf_op jit(solution)/shard_map/ppermute | solution.py:475
  63.9 16.4 %collective-permute-start.14 = (bf16[2096,128]{1,0:T(8,128)(2,1)S(1)}, bf16[2096,128]{1,0:T(8,128)(2,1)S(1)}, u32[]{:S(2)}, u32[]{:S(2)}) collective-permute-start(bf16[2096,128]{1,0:T(8,128)(2,1)S(1)} %collective-permute-done.10.refs_7_), channel_id=1, source_target_pairs={{64,32},{32,64},{65,33},{33,65},{66,34},{34,66},{67,35},{35,67},{6... | collective-permute-start | bytes 1609736 | tf_op jit(solution)/shard_map/ppermute | solution.py:475
